TPU v7x, 512 devices: a whole 4x4x16 slice. The times are simulated.
512 devices in a mesh: sfc: 512 (over x, y, z, core).
Axes of the slice: x: 4, y: 4, z: 16, core: 2. Of those that a mesh axis runs over, the one named last changes fastest.
Arguments:
- fields: float32 [6, 64, 65536], P(None, None, 'sfc'), may hold values from -6 to 6
- material: float32 [2, 65536], P(None, 'sfc'), may hold values from 0.25 to 1
- refinement: int32 [65536], P('sfc'), may hold values from 0 to 2
- face_source: int32 [6, 65536], P(None, 'sfc'), may hold values from 0 to 2303, as said below
- face_code: int32 [6, 65536], P(None, 'sfc'), may hold values from 0 to 48, as said below
- send_face: int32 [8, 98304], P(None, 'sfc'), may hold values from 0 to 767, as said below
- mortar_source: int32 [4, 32768], P(None, 'sfc'), may hold values from 0 to 2303, as said below
- mortar_code: int32 [4, 32768], P(None, 'sfc'), may hold values from 0 to 7
- mortar_target: int32 [32768], P('sfc'), may hold values from -1 to 767, as said below
Outputs:
- new_fields: float32 [6, 64, 65536], P(None, None, 'sfc')
- register: float32 [6, 64, 65536], P(None, None, 'sfc')
Inputs may be any that keep to these rules, and one draw needn't show every extreme that they name: `face_source`: A value below 768 names a local face of the same block; a larger value 6 * 128 + k * 192 + s names slot s of list k of the block o_k places before, with o_k = k - 4 for k < 4, else k - 3, and that block exists. Boundary faces and coarse faces name themselves. face_code // 8 is the kind: 0 conforming, 1 boundary, 2 + q the fine face on quarter q of a coarse face, 6 a coarse face with four fine neighbours; face_code % 8 is the orientation code, 0 on boundary and coarse faces. A face has kind 6 exactly when a mortar row of its block targets it. `send_face`: local faces of the listing block. `mortar_source`: encoded as face_source, for the block that holds the row. `mortar_target`: A local face of the row's block, each one at most once; -1 marks a padding row, and padding rows follow the live rows of their block. Every block has 12 or more live rows, and some block has no padding row.
All inputs are finite; a program needn't handle non-finite values.
Results may differ from a plain program's by a relative error of at most 0.0003.
Values sent between devices are 32-bit elements; how exact they have to be, the bound alone decides.
No kernel may reach another device: no remote copies, remote signals or barrier semaphores. Data moves between devices by JAX's collectives and lax.ppermute only.
A program may use at most 64 MiB of HBM per device.

v0:
```python
import math

import jax
import jax.numpy as jnp
import numpy as np
from jax import lax
from jax.sharding import PartitionSpec as P

STEP_SIZE = 0.02
SECTION_A = (0.0, -567301805773.0 / 1357537059087.0)
SECTION_B = (1432997174477.0 / 9575080441755.0, 5161836677717.0 / 13612068292357.0)


def with_halo(cells, sides, width):
    for axis, dim in sides:
        count = lax.axis_size(axis)
        ends = count - 1
        head = lax.slice_in_dim(cells, 0, width, axis=dim)
        tail = lax.slice_in_dim(cells, cells.shape[dim] - width, cells.shape[dim], axis=dim)
        cells = jnp.concatenate(
            [
                lax.ppermute(tail, axis, [(i, (i + 1) % count) for i in range(ends)]),
                cells,
                lax.ppermute(head, axis, [((i + 1) % count, i) for i in range(ends)]),
            ],
            axis=dim,
        )
    return cells


def passed_along(value, axis, steps):
    count = lax.axis_size(axis)
    first, last = (max(0, -steps), min(count, count - steps))
    return lax.ppermute(value, axis, [(source, source + steps) for source in range(first, last)])


def gll_tables():
    points = np.array([-1.0, -1.0 / math.sqrt(5.0), 1.0 / math.sqrt(5.0), 1.0])
    weights = np.array([1.0, 5.0, 5.0, 1.0]) / 6.0

    def lagrange(where_at):
        values = np.ones((where_at.shape[0], 4))
        for column in range(4):
            for another in range(4):
                if another != column:
                    values[:, column] *= (where_at - points[another]) / (
                        points[column] - points[another]
                    )
        return values

    derivative = np.zeros((4, 4))
    for row_at in range(4):
        for column in range(4):
            summed = 0.0
            for another in range(4):
                if another == column:
                    continue
                factor = 1.0 / (points[column] - points[another])
                for further in range(4):
                    if further != column and further != another:
                        factor *= (points[row_at] - points[further]) / (
                            points[column] - points[further]
                        )
                summed += factor
            derivative[row_at, column] = summed
    halves = [lagrange((points - 1.0) / 2.0), lagrange((points + 1.0) / 2.0)]
    adjoint = [0.5 * halfway.T * weights[None, :] / weights[:, None] for halfway in halves]
    interpolate = [np.kron(halves[quarter % 2], halves[quarter // 2]) for quarter in range(4)] + [
        np.eye(16)
    ]
    projection = [np.kron(adjoint[quarter % 2], adjoint[quarter // 2]) for quarter in range(4)]
    normals = np.zeros((3, 6))
    for facing in range(6):
        normals[facing // 2, facing] = 1.0 if facing % 2 == 1 else -1.0
    return (
        jnp.asarray(derivative, jnp.float32),
        jnp.asarray(np.stack(interpolate), jnp.float32),
        jnp.asarray(np.stack(projection), jnp.float32),
        jnp.asarray(normals, jnp.float32),
    )


def face_traces(nodal_grid):
    elements = nodal_grid.shape[-1]
    sides = [
        nodal_grid[:, 0],
        nodal_grid[:, 3],
        nodal_grid[:, :, 0],
        nodal_grid[:, :, 3],
        nodal_grid[:, :, :, 0],
        nodal_grid[:, :, :, 3],
    ]
    return jnp.stack([facing.reshape(6, 16, elements) for facing in sides], axis=2)


def orient_order(code_value):
    order = []
    for corner in range(16):
        first_axis = corner // 4
        second = corner % 4
        along_a = 3 - first_axis if code_value % 2 == 1 else first_axis
        along_b = 3 - second if code_value // 2 % 2 == 1 else second
        order.append(4 * along_b + along_a if code_value >= 4 else 4 * along_a + along_b)
    return np.array(order, dtype=np.int32)


def oriented(trace_table, columns, orient_codes):
    whole_columns = jnp.take(trace_table, columns, axis=2)
    result = whole_columns
    for code_value in range(1, 8):
        permuted = whole_columns[:, orient_order(code_value)]
        result = jnp.where(orient_codes[None, None] == code_value, permuted, result)
    return result


def cross_product(normal, vector):
    return jnp.stack(
        [
            normal[1] * vector[2] - normal[2] * vector[1],
            normal[2] * vector[0] - normal[0] * vector[2],
            normal[0] * vector[1] - normal[1] * vector[0],
        ]
    )


def lifted(flux, metric):
    elements = flux.shape[-1]
    weight = 3.0 * metric
    volume = jnp.zeros((3, 4, 4, 4, elements), flux.dtype)
    volume = volume.at[:, 0].add(flux[:, :, 0].reshape(3, 4, 4, elements) * weight)
    volume = volume.at[:, 3].add(flux[:, :, 1].reshape(3, 4, 4, elements) * weight)
    volume = volume.at[:, :, 0].add(flux[:, :, 2].reshape(3, 4, 4, elements) * weight)
    volume = volume.at[:, :, 3].add(flux[:, :, 3].reshape(3, 4, 4, elements) * weight)
    volume = volume.at[:, :, :, 0].add(flux[:, :, 4].reshape(3, 4, 4, elements) * weight)
    volume = volume.at[:, :, :, 3].add(flux[:, :, 5].reshape(3, 4, 4, elements) * weight)
    return volume


def curl_of(vector, derivative, metric):
    highest = lax.Precision.HIGHEST
    along_x = jnp.einsum("ia,fajke->fijke", derivative, vector[1:3], precision=highest) * metric
    along_y = jnp.einsum("ja,fiake->fijke", derivative, vector[0::2], precision=highest) * metric
    along_z = jnp.einsum("ka,fijae->fijke", derivative, vector[0:2], precision=highest) * metric
    return jnp.stack([along_y[1] - along_z[1], along_z[0] - along_x[1], along_x[0] - along_y[0]])


def block_rates(
    solution,
    material,
    metric,
    inside,
    face_columns,
    face_code,
    mortar_columns,
    mortar_code,
    mortar_target,
    trace_table,
    tables,
):
    derivative, interpolate, projection, normals = tables
    highest = lax.Precision.HIGHEST
    elements = solution.shape[-1]
    nodal_grid = solution.reshape(6, 4, 4, 4, elements)
    face_kind = face_code // 8
    raw_trace = oriented(trace_table, face_columns, face_code % 8)
    exterior = raw_trace
    for quarter in range(4):
        refined = jnp.einsum("mn,fnge->fmge", interpolate[quarter], raw_trace, precision=highest)
        exterior = jnp.where(face_kind[None, None] == 2 + quarter, refined, exterior)
    field_ids = jnp.arange(6, dtype=jnp.int32)[:, None, None, None]
    exterior = jnp.where((face_kind[None, None] == 1) & (field_ids < 3), -exterior, exterior)
    pieces = oriented(trace_table, mortar_columns, mortar_code)
    mortar_value = jnp.einsum("qmn,fnqr->fmr", projection, pieces, precision=highest)
    target_column = jnp.where(mortar_target >= 0, mortar_target, 6 * elements)
    placed = (
        jnp.zeros((6, 16, 6 * elements + 1), jnp.float32).at[:, :, target_column].set(mortar_value)
    )
    placed = placed[:, :, : 6 * elements].reshape(6, 16, 6, elements)
    exterior = jnp.where(face_kind[None, None] == 6, placed, exterior)
    jump_e = exterior[0:3] - inside[0:3]
    jump_h = exterior[3:6] - inside[3:6]
    normal = normals[:, None, :, None]
    flux_e = cross_product(normal, jump_h) - (jump_e - jnp.sum(normal * jump_e, axis=0) * normal)
    flux_h = -cross_product(normal, jump_e) - (jump_h - jnp.sum(normal * jump_h, axis=0) * normal)
    curl_e = curl_of(nodal_grid[0:3], derivative, metric)
    curl_h = curl_of(nodal_grid[3:6], derivative, metric)
    rate_e = material[0] * (curl_h + lifted(flux_e, metric))
    rate_h = material[1] * (lifted(flux_h, metric) - curl_e)
    return jnp.concatenate([rate_e, rate_h], axis=0).reshape(6, 64, elements)


def deliver(outgoing, reach_max):
    received = [None] * (2 * reach_max)
    padded = with_halo(outgoing[:, :, reach_max - 1 : reach_max + 1], (("sfc", 2),), 1)
    received[reach_max] = padded[:, :, 0]
    received[reach_max - 1] = padded[:, :, 3]
    for direction in range(2 * reach_max):
        if direction == reach_max - 1 or direction == reach_max:
            continue
        offset = direction - reach_max if direction < reach_max else direction - reach_max + 1
        received[direction] = passed_along(outgoing[:, :, direction], "sfc", offset)
    return jnp.stack(received, axis=2)


def local(
    fields,
    material,
    refinement,
    face_source,
    face_code,
    send_face,
    mortar_source,
    mortar_code,
    mortar_target,
):
    tables = gll_tables()
    elements = fields.shape[-1]
    reach_max = send_face.shape[0] // 2
    metric = jnp.left_shift(jnp.ones_like(refinement), refinement).astype(jnp.float32)
    solution = fields
    register = jnp.zeros_like(fields)
    for section_index in range(2):
        inside = face_traces(solution.reshape(6, 4, 4, 4, elements))
        own_table = inside.reshape(6, 16, 6 * elements)
        outgoing = jnp.take(own_table, send_face, axis=2)
        incoming = deliver(outgoing, reach_max)
        trace_table = jnp.concatenate([own_table, incoming.reshape(6, 16, -1)], axis=2)
        section_rates = block_rates(
            solution,
            material,
            metric,
            inside,
            face_source,
            face_code,
            mortar_source,
            mortar_code,
            mortar_target,
            trace_table,
            tables,
        )
        register = SECTION_A[section_index] * register + STEP_SIZE * section_rates
        solution = solution + SECTION_B[section_index] * register
    return (solution, register)


def solution(mesh):
    return jax.shard_map(
        local,
        mesh=mesh,
        in_specs=(
            P(None, None, "sfc"),
            P(None, "sfc"),
            P("sfc"),
            P(None, "sfc"),
            P(None, "sfc"),
            P(None, "sfc"),
            P(None, "sfc"),
            P(None, "sfc"),
            P("sfc"),
        ),
        out_specs=(P(None, None, "sfc"), P(None, None, "sfc")),
        check_vma=False,
    )
```

profile of v0, /device:TPU:7, one launch (start us, length us, event | category | flops | bytes accessed | tf_op | source)
XLA Modules:
  0.0 225.7 jit_solution(8393792869795124310)
XLA Ops:
  2.3 1.1 fusion.89
  5.6 1.2 copy.280
  7.0 5.7 %gather_fusion.28 = f32[1536,6,16]{2,1,0:T(8,128)} fusion(f32[6,16,768]{1,0,2:T(8,128)S(1)} %copy.280, s32[2048]{0:T(1024)S(1)} %pad_clamp_fusion), kind=kCustom, calls=%fused_computation.clone | custom fusion | bytes 1185792 | tf_op jit(solution)/shard_map/jit(_take)/gather | solution.py:225
  12.7 4.5 %copy.281 = f32[8,192,6,16]{1,3,2,0:T(8,128)S(1)} copy(f32[8,192,6,16]{3,2,1,0:T(8,128)} %bitcast.394) | data formatting | bytes 1179648 | tf_op jit(solution)/shard_map/jit(_take)/gather | solution.py:225
  17.7 14.3 %collective-permute-start = (f32[6,16,192]{2,1,0:T(8,128)S(1)}, f32[6,16,192]{2,1,0:T(8,128)S(1)}, u32[]{:S(2)}, u32[]{:S(2)}) collective-permute-start(f32[6,16,192]{2,1,0:T(8,128)S(1)} %get-tuple-element.320), channel_id=1, source_target_pairs={{4,0},{5,1},{6,2},{7,3},{8,4},{9,5},{10,6},{11,7},{12,8},{13,9},{1... | collective-permute-start | bytes 221192 | tf_op jit(solution)/shard_map/ppermute | solution.py:34
  31.9 3.5 %collective-permute-start.1 = (f32[6,16,192]{2,1,0:T(8,128)S(1)}, f32[6,16,192]{2,1,0:T(8,128)S(1)}, u32[]{:S(2)}, u32[]{:S(2)}) collective-permute-start(f32[6,16,192]{2,1,0:T(8,128)S(1)} %get-tuple-element.319), channel_id=1, source_target_pairs={{3,0},{4,1},{5,2},{6,3},{7,4},{8,5},{9,6},{10,7},{11,8},{12,9},{13... | collective-permute-start | bytes 221192 | tf_op jit(solution)/shard_map/ppermute | solution.py:34
  35.4 2.6 %collective-permute-start.2 = (f32[6,16,192]{2,1,0:T(8,128)S(1)}, f32[6,16,192]{2,1,0:T(8,128)S(1)}, u32[]{:S(2)}, u32[]{:S(2)}) collective-permute-start(f32[6,16,192]{2,1,0:T(8,128)S(1)} %get-tuple-element.318), channel_id=1, source_target_pairs={{2,0},{3,1},{4,2},{5,3},{6,4},{7,5},{8,6},{9,7},{10,8},{11,9},{12,... | collective-permute-start | bytes 221192 | tf_op jit(solution)/shard_map/ppermute | solution.py:34
  38.1 3.4 %collective-permute-start.3 = (f32[6,16,1,192]{3,1,0,2:T(8,128)S(1)}, f32[6,16,1,192]{3,1,0,2:T(8,128)S(1)}, u32[]{:S(2)}, u32[]{:S(2)}) collective-permute-start(f32[6,16,1,192]{3,1,0,2:T(8,128)S(1)} %get-tuple-element.317), channel_id=1, source_target_pairs={{1,0},{2,1},{3,2},{4,3},{5,4},{6,5},{7,6},{8,7},{9,8},{10,9},{11,1... | collective-permute-start | bytes 221192 | tf_op jit(solution)/shard_map/ppermute | solution.py:24
  41.5 2.2 collective-permute-start.4
  55.3 2.6 %collective-permute-start.5 = (f32[6,16,192]{2,1,0:T(8,128)S(1)}, f32[6,16,192]{2,1,0:T(8,128)S(1)}, u32[]{:S(2)}, u32[]{:S(2)}) collective-permute-start(f32[6,16,192]{2,1,0:T(8,128)S(1)} %get-tuple-element.315), channel_id=1, source_target_pairs={{0,2},{1,3},{2,4},{3,5},{4,6},{5,7},{6,8},{7,9},{8,10},{9,11},{10,... | collective-permute-start | bytes 221192 | tf_op jit(solution)/shard_map/ppermute | solution.py:34
  57.9 2.6 %collective-permute-start.6 = (f32[6,16,192]{2,1,0:T(8,128)S(1)}, f32[6,16,192]{2,1,0:T(8,128)S(1)}, u32[]{:S(2)}, u32[]{:S(2)}) collective-permute-start(f32[6,16,192]{2,1,0:T(8,128)S(1)} %get-tuple-element.314), channel_id=1, source_target_pairs={{0,3},{1,4},{2,5},{3,6},{4,7},{5,8},{6,9},{7,10},{8,11},{9,12},{10... | collective-permute-start | bytes 221192 | tf_op jit(solution)/shard_map/ppermute | solution.py:34
  60.6 3.8 %collective-permute-start.7 = (f32[6,16,192]{2,1,0:T(8,128)S(1)}, f32[6,16,192]{2,1,0:T(8,128)S(1)}, u32[]{:S(2)}, u32[]{:S(2)}) collective-permute-start(f32[6,16,192]{2,1,0:T(8,128)S(1)} %get-tuple-element.313), channel_id=1, source_target_pairs={{0,4},{1,5},{2,6},{3,7},{4,8},{5,9},{6,10},{7,11},{8,12},{9,13},{1... | collective-permute-start | bytes 221192 | tf_op jit(solution)/shard_map/ppermute | solution.py:34
  66.3 3.6 %collective-permute-done.6 = f32[6,16,192]{2,1,0:T(8,128)S(1)} collective-permute-done((f32[6,16,192]{2,1,0:T(8,128)S(1)}, f32[6,16,192]{2,1,0:T(8,128)S(1)}, u32[]{:S(2)}, u32[]{:S(2)}) %collective-permute-start.6) | collective-permute-done | bytes 73760 | tf_op jit(solution)/shard_map/ppermute | solution.py:34
  70.2 3.2 %collective-permute-done.7 = f32[6,16,192]{2,1,0:T(8,128)S(1)} collective-permute-done((f32[6,16,192]{2,1,0:T(8,128)S(1)}, f32[6,16,192]{2,1,0:T(8,128)S(1)}, u32[]{:S(2)}, u32[]{:S(2)}) %collective-permute-start.7) | collective-permute-done | bytes 73760 | tf_op jit(solution)/shard_map/ppermute | solution.py:34
  73.5 1.2 stack.104
  75.0 5.2 %copy.289 = f32[6,16,2304]{1,0,2:T(8,128)} copy(f32[6,16,2304]{2,1,0:T(8,128)S(1)} %pad_maximum_fusion) | data formatting | bytes 1769472 | tf_op jit(solution)/shard_map/concatenate | solution.py:227
  80.2 4.9 %gather_fusion.30 = f32[768,6,16]{2,1,0:T(8,128)S(1)} fusion(f32[6,16,2304]{1,0,2:T(8,128)} %copy.289, s32[1024]{0:T(1024)S(1)} %get-tuple-element.446), kind=kCustom, calls=%fused_computation.2.clone | custom fusion | bytes 592896 | tf_op jit(solution)/shard_map/jit(_take)/gather | solution.py:108
  85.1 0.9 copy.304
  87.7 4.4 %gather_fusion.29 = f32[256,6,16]{2,1,0:T(8,128)S(1)} fusion(f32[6,16,2304]{1,0,2:T(8,128)} %copy.289, s32[1024]{0:T(1024)S(1)} %copy-done.57), kind=kCustom, calls=%fused_computation.1.clone | custom fusion | bytes 197632 | tf_op jit(solution)/shard_map/jit(_take)/gather | solution.py:108
  92.5 1.5 gather_fusion.6
  94.1 1.5 gather_fusion.4
  96.3 1.5 gather_fusion.5
  98.6 1.5 gather_fusion
  100.8 1.6 gather_fusion.1
  102.4 1.6 gather_fusion.9
  104.1 1.5 gather_fusion.2
  105.6 1.5 gather_fusion.10
  107.0 0.9 gather_fusion.3
  108.1 1.9 fusion.25
  110.0 1.1 convolution_bitcast_fusion.5
  111.1 1.1 convolution_bitcast_fusion.6
  112.2 1.5 fusion.38
  115.1 4.6 %scatter_fusion = f32[6,16,769]{1,0,2:T(8,128)S(1)} fusion(f32[6,16,769]{1,0,2:T(8,128)S(1)} %broadcast.649.clone, s32[64]{0:T(128)S(1)} %copy-done.106, f32[64,6,16]{2,1,0:T(8,128)} %copy.300), kind=kCustom, calls=%fused_computation.34 | custom fusion | bytes 73984 | tf_op jit(solution)/shard_map/scatter | solution.py:176
  119.7 1.9 slice.1448
  121.7 2.3 %copy.319 = f32[6,16,6,128]{3,1,2,0:T(8,128)S(1)} copy(f32[6,16,6,128]{1,0,3,2:T(8,128)} %bitcast.391) | data formatting | bytes 589824 | tf_op jit(solution)/shard_map/reshape | solution.py:178
  127.5 0.9 fusion.48
  128.4 0.9 fusion.50
  129.3 0.9 fusion.55
  130.2 0.9 fusion.98
  132.0 0.9 fusion.8
  133.7 1.2 copy.349
  134.9 5.9 %gather_fusion.31 = f32[1536,6,16]{2,1,0:T(8,128)} fusion(f32[6,16,768]{1,0,2:T(8,128)S(1)} %copy.349, s32[2048]{0:T(1024)} %copy-done.40), kind=kCustom, calls=%fused_computation.3.clone | custom fusion | bytes 1185792 | tf_op jit(solution)/shard_map/jit(_take)/gather | solution.py:225
  140.8 4.5 %copy.350 = f32[8,192,6,16]{1,3,2,0:T(8,128)S(1)} copy(f32[8,192,6,16]{3,2,1,0:T(8,128)} %bitcast.393) | data formatting | bytes 1179648 | tf_op jit(solution)/shard_map/jit(_take)/gather | solution.py:225
  145.6 1.9 collective-permute-start.8
  147.5 5.3 %collective-permute-start.9 = (f32[6,16,192]{2,1,0:T(8,128)S(1)}, f32[6,16,192]{2,1,0:T(8,128)S(1)}, u32[]{:S(2)}, u32[]{:S(2)}) collective-permute-start(f32[6,16,192]{2,1,0:T(8,128)S(1)} %get-tuple-element.311), channel_id=1, source_target_pairs={{3,0},{4,1},{5,2},{6,3},{7,4},{8,5},{9,6},{10,7},{11,8},{12,9},{13... | collective-permute-start | bytes 221192 | tf_op jit(solution)/shard_map/ppermute | solution.py:34
  152.8 1.9 collective-permute-start.10
  154.7 2.3 %collective-permute-start.11 = (f32[6,16,1,192]{3,1,0,2:T(8,128)S(1)}, f32[6,16,1,192]{3,1,0,2:T(8,128)S(1)}, u32[]{:S(2)}, u32[]{:S(2)}) collective-permute-start(f32[6,16,1,192]{3,1,0,2:T(8,128)S(1)} %get-tuple-element.309), channel_id=1, source_target_pairs={{1,0},{2,1},{3,2},{4,3},{5,4},{6,5},{7,6},{8,7},{9,8},{10,9},{11,1... | collective-permute-start | bytes 221192 | tf_op jit(solution)/shard_map/ppermute | solution.py:24
  157.0 3.3 %collective-permute-start.12 = (f32[6,16,1,192]{3,1,0,2:T(8,128)S(1)}, f32[6,16,1,192]{3,1,0,2:T(8,128)S(1)}, u32[]{:S(2)}, u32[]{:S(2)}) collective-permute-start(f32[6,16,1,192]{3,1,0,2:T(8,128)S(1)} %get-tuple-element.308), channel_id=1, source_target_pairs={{0,1},{1,2},{2,3},{3,4},{4,5},{5,6},{6,7},{7,8},{8,9},{9,10},{10,1... | collective-permute-start | bytes 221192 | tf_op jit(solution)/shard_map/ppermute | solution.py:22
  161.2 3.4 %collective-permute-start.13 = (f32[6,16,192]{2,1,0:T(8,128)S(1)}, f32[6,16,192]{2,1,0:T(8,128)S(1)}, u32[]{:S(2)}, u32[]{:S(2)}) collective-permute-start(f32[6,16,192]{2,1,0:T(8,128)S(1)} %get-tuple-element.307), channel_id=1, source_target_pairs={{0,2},{1,3},{2,4},{3,5},{4,6},{5,7},{6,8},{7,9},{8,10},{9,11},{10,... | collective-permute-start | bytes 221192 | tf_op jit(solution)/shard_map/ppermute | solution.py:34
  164.6 2.1 collective-permute-start.14
  166.7 5.1 %collective-permute-start.15 = (f32[6,16,192]{2,1,0:T(8,128)S(1)}, f32[6,16,192]{2,1,0:T(8,128)S(1)}, u32[]{:S(2)}, u32[]{:S(2)}) collective-permute-start(f32[6,16,192]{2,1,0:T(8,128)S(1)} %get-tuple-element.305), channel_id=1, source_target_pairs={{0,4},{1,5},{2,6},{3,7},{4,8},{5,9},{6,10},{7,11},{8,12},{9,13},{1... | collective-permute-start | bytes 221192 | tf_op jit(solution)/shard_map/ppermute | solution.py:34
  172.9 3.3 %collective-permute-done.14 = f32[6,16,192]{2,1,0:T(8,128)S(1)} collective-permute-done((f32[6,16,192]{2,1,0:T(8,128)S(1)}, f32[6,16,192]{2,1,0:T(8,128)S(1)}, u32[]{:S(2)}, u32[]{:S(2)}) %collective-permute-start.14) | collective-permute-done | bytes 73760 | tf_op jit(solution)/shard_map/ppermute | solution.py:34
  176.5 1.4 collective-permute-done.15
  178.0 1.2 stack.116
  179.5 5.2 %copy.358 = f32[6,16,2304]{1,0,2:T(8,128)} copy(f32[6,16,2304]{2,1,0:T(8,128)S(1)} %pad_maximum_fusion.1) | data formatting | bytes 1769472 | tf_op jit(solution)/shard_map/concatenate | solution.py:227
  184.7 4.9 %gather_fusion.33 = f32[768,6,16]{2,1,0:T(8,128)S(1)} fusion(f32[6,16,2304]{1,0,2:T(8,128)} %copy.358, s32[1024]{0:T(1024)S(1)} %copy-done.44), kind=kCustom, calls=%fused_computation.5.clone | custom fusion | bytes 592896 | tf_op jit(solution)/shard_map/jit(_take)/gather | solution.py:108
  189.6 0.9 copy.373
  195.8 1.7 fusion.19
  197.6 1.8 convolution_bitcast_fusion.1
  199.4 1.8 convolution_bitcast_fusion.2
  201.2 4.4 %gather_fusion.32 = f32[256,6,16]{2,1,0:T(8,128)S(1)} fusion(f32[6,16,2304]{1,0,2:T(8,128)} %copy.358, s32[1024]{0:T(1024)S(1)} %copy-done.58), kind=kCustom, calls=%fused_computation.4.clone | custom fusion | bytes 197632 | tf_op jit(solution)/shard_map/jit(_take)/gather | solution.py:108
  213.5 4.6 %scatter_fusion.1 = f32[6,16,769]{1,0,2:T(8,128)S(1)} fusion(f32[6,16,769]{1,0,2:T(8,128)S(1)} %broadcast.649, s32[64]{0:T(128)S(1)} %copy-done.107, f32[64,6,16]{2,1,0:T(8,128)} %copy.369), kind=kCustom, calls=%fused_computation.35 | custom fusion | bytes 73984 | tf_op jit(solution)/shard_map/scatter | solution.py:176
  218.1 1.9 slice.1508
  220.2 2.3 %copy.388 = f32[6,16,6,128]{3,1,2,0:T(8,128)S(1)} copy(f32[6,16,6,128]{1,0,3,2:T(8,128)} %bitcast.392) | data formatting | bytes 589824 | tf_op jit(solution)/shard_map/reshape | solution.py:178
  (428 shorter events, 47.0 us)
Async XLA Ops:
  4.8 12.4 %copy-start.55 = (pred[8,192]{1,0:T(8,128)(4,1)}, pred[8,192]{1,0:T(8,128)(4,1)S(1)}, u32[]{:S(2)}) copy-start(pred[8,192]{1,0:T(8,128)(4,1)S(1)} %compare_and_fusion) | copy-start | bytes 4612
  7.0 10.3 %copy-start.40 = (s32[2048]{0:T(1024)}, s32[2048]{0:T(1024)S(1)}, u32[]{:S(2)}) copy-start(s32[2048]{0:T(1024)S(1)} %pad_clamp_fusion) | copy-start | bytes 24580
  17.3 26.4 %copy-start.79 = (s32[4,64]{1,0:T(4,128)S(1)}, s32[4,64]{1,0:T(4,128)}, u32[]{:S(2)}) copy-start(s32[4,64]{1,0:T(4,128)} %param.129) | copy-start | bytes 3076
  17.3 27.0 %copy-start.116 = (s32[128]{0:T(128)S(1)}, s32[128]{0:T(128)}, u32[]{:S(2)}) copy-start(s32[128]{0:T(128)} %param.125) | copy-start | bytes 1540
  17.3 27.0 %copy-start.2 = (f32[6,64,128]{2,1,0:T(8,128)S(1)}, f32[6,64,128]{2,1,0:T(8,128)}, u32[]{:S(2)}) copy-start(f32[6,64,128]{2,1,0:T(8,128)} %param.123) | copy-start | bytes 589828
  17.3 27.0 %copy-start.59 = (s32[6,128]{1,0:T(8,128)S(1)}, s32[6,128]{1,0:T(8,128)}, u32[]{:S(2)}) copy-start(s32[6,128]{1,0:T(8,128)} %param.126) | copy-start | bytes 9220
  17.3 27.1 %copy-start.98 = (s32[6,128]{1,0:T(8,128)S(1)}, s32[6,128]{1,0:T(8,128)}, u32[]{:S(2)}) copy-start(s32[6,128]{1,0:T(8,128)} %param.127) | copy-start | bytes 9220
  17.3 28.9 %copy-start.99 = (s32[4,64]{1,0:T(4,128)S(1)}, s32[4,64]{1,0:T(4,128)}, u32[]{:S(2)}) copy-start(s32[4,64]{1,0:T(4,128)} %param.130) | copy-start | bytes 3076
  17.3 29.5 %copy-start.117 = (s32[64]{0:T(128)S(1)}, s32[64]{0:T(128)}, u32[]{:S(2)}) copy-start(s32[64]{0:T(128)} %param.131) | copy-start | bytes 772
  17.4 30.0 %copy-start.19 = (f32[4,4,1,1,1]{1,0,4,3,2:T(4,128)S(1)}, f32[4,4,1,1,1]{1,0,4,3,2:T(4,128)}, u32[]{:S(2)}) copy-start(f32[4,4,1,1,1]{1,0,4,3,2:T(4,128)} %constant.719) | copy-start | bytes 196
  17.4 32.8 %copy-start.108 = (f32[2,128]{1,0:T(2,128)S(1)}, f32[2,128]{1,0:T(2,128)}, u32[]{:S(2)}) copy-start(f32[2,128]{1,0:T(2,128)} %param.124) | copy-start | bytes 3076
  17.4 34.1 %copy-start.115 = (s32[16]{0:T(128)S(1)}, s32[16]{0:T(128)}, u32[]{:S(2)}) copy-start(s32[16]{0:T(128)} %constant.697) | copy-start | bytes 196
  17.4 34.7 %copy-start.113 = (s32[16]{0:T(128)S(1)}, s32[16]{0:T(128)}, u32[]{:S(2)}) copy-start(s32[16]{0:T(128)} %constant.691) | copy-start | bytes 196
  17.4 34.7 %copy-start.114 = (s32[16]{0:T(128)S(1)}, s32[16]{0:T(128)}, u32[]{:S(2)}) copy-start(s32[16]{0:T(128)} %constant.692) | copy-start | bytes 196
  17.4 35.3 %copy-start.111 = (s32[16]{0:T(128)S(1)}, s32[16]{0:T(128)}, u32[]{:S(2)}) copy-start(s32[16]{0:T(128)} %constant.693) | copy-start | bytes 196
  17.4 35.3 %copy-start.112 = (s32[16]{0:T(128)S(1)}, s32[16]{0:T(128)}, u32[]{:S(2)}) copy-start(s32[16]{0:T(128)} %constant.694) | copy-start | bytes 196
  17.4 37.2 %copy-start.109 = (s32[16]{0:T(128)S(1)}, s32[16]{0:T(128)}, u32[]{:S(2)}) copy-start(s32[16]{0:T(128)} %constant.695) | copy-start | bytes 196
  17.5 37.2 %copy-start.110 = (s32[16]{0:T(128)S(1)}, s32[16]{0:T(128)}, u32[]{:S(2)}) copy-start(s32[16]{0:T(128)} %constant.696) | copy-start | bytes 196
  17.7 37.6 %collective-permute-start = (f32[6,16,192]{2,1,0:T(8,128)S(1)}, f32[6,16,192]{2,1,0:T(8,128)S(1)}, u32[]{:S(2)}, u32[]{:S(2)}) collective-permute-start(f32[6,16,192]{2,1,0:T(8,128)S(1)} %get-tuple-element.320), channel_id=1, source_target_pairs={{4,0},{5,1},{6,2},{7,3},{8,4},{9,5},{10,6},{11,7},{12,8},{13,9},{1... | collective-permute-start | bytes 221192 | tf_op jit(solution)/shard_map/ppermute | solution.py:34
  31.9 26.0 %collective-permute-start.1 = (f32[6,16,192]{2,1,0:T(8,128)S(1)}, f32[6,16,192]{2,1,0:T(8,128)S(1)}, u32[]{:S(2)}, u32[]{:S(2)}) collective-permute-start(f32[6,16,192]{2,1,0:T(8,128)S(1)} %get-tuple-element.319), channel_id=1, source_target_pairs={{3,0},{4,1},{5,2},{6,3},{7,4},{8,5},{9,6},{10,7},{11,8},{12,9},{13... | collective-permute-start | bytes 221192 | tf_op jit(solution)/shard_map/ppermute | solution.py:34
  35.4 25.2 %collective-permute-start.2 = (f32[6,16,192]{2,1,0:T(8,128)S(1)}, f32[6,16,192]{2,1,0:T(8,128)S(1)}, u32[]{:S(2)}, u32[]{:S(2)}) collective-permute-start(f32[6,16,192]{2,1,0:T(8,128)S(1)} %get-tuple-element.318), channel_id=1, source_target_pairs={{2,0},{3,1},{4,2},{5,3},{6,4},{7,5},{8,6},{9,7},{10,8},{11,9},{12,... | collective-permute-start | bytes 221192 | tf_op jit(solution)/shard_map/ppermute | solution.py:34
  38.1 31.9 %collective-permute-start.3 = (f32[6,16,1,192]{3,1,0,2:T(8,128)S(1)}, f32[6,16,1,192]{3,1,0,2:T(8,128)S(1)}, u32[]{:S(2)}, u32[]{:S(2)}) collective-permute-start(f32[6,16,1,192]{3,1,0,2:T(8,128)S(1)} %get-tuple-element.317), channel_id=1, source_target_pairs={{1,0},{2,1},{3,2},{4,3},{5,4},{6,5},{7,6},{8,7},{9,8},{10,9},{11,1... | collective-permute-start | bytes 221192 | tf_op jit(solution)/shard_map/ppermute | solution.py:24
  41.5 28.6 %collective-permute-start.4 = (f32[6,16,1,192]{3,1,0,2:T(8,128)S(1)}, f32[6,16,1,192]{3,1,0,2:T(8,128)S(1)}, u32[]{:S(2)}, u32[]{:S(2)}) collective-permute-start(f32[6,16,1,192]{3,1,0,2:T(8,128)S(1)} %get-tuple-element.316), channel_id=1, source_target_pairs={{0,1},{1,2},{2,3},{3,4},{4,5},{5,6},{6,7},{7,8},{8,9},{9,10},{10,1... | collective-permute-start | bytes 221192 | tf_op jit(solution)/shard_map/ppermute | solution.py:22
  52.1 28.1 %copy-start.43 = (s32[1024]{0:T(1024)}, s32[1024]{0:T(1024)S(1)}, u32[]{:S(2)}) copy-start(s32[1024]{0:T(1024)S(1)} %get-tuple-element.446) | copy-start | bytes 12292
  55.3 10.9 %collective-permute-start.5 = (f32[6,16,192]{2,1,0:T(8,128)S(1)}, f32[6,16,192]{2,1,0:T(8,128)S(1)}, u32[]{:S(2)}, u32[]{:S(2)}) collective-permute-start(f32[6,16,192]{2,1,0:T(8,128)S(1)} %get-tuple-element.315), channel_id=1, source_target_pairs={{0,2},{1,3},{2,4},{3,5},{4,6},{5,7},{6,8},{7,9},{8,10},{9,11},{10,... | collective-permute-start | bytes 221192 | tf_op jit(solution)/shard_map/ppermute | solution.py:34
  57.9 11.9 %collective-permute-start.6 = (f32[6,16,192]{2,1,0:T(8,128)S(1)}, f32[6,16,192]{2,1,0:T(8,128)S(1)}, u32[]{:S(2)}, u32[]{:S(2)}) collective-permute-start(f32[6,16,192]{2,1,0:T(8,128)S(1)} %get-tuple-element.314), channel_id=1, source_target_pairs={{0,3},{1,4},{2,5},{3,6},{4,7},{5,8},{6,9},{7,10},{8,11},{9,12},{10... | collective-permute-start | bytes 221192 | tf_op jit(solution)/shard_map/ppermute | solution.py:34
  60.6 12.8 %collective-permute-start.7 = (f32[6,16,192]{2,1,0:T(8,128)S(1)}, f32[6,16,192]{2,1,0:T(8,128)S(1)}, u32[]{:S(2)}, u32[]{:S(2)}) collective-permute-start(f32[6,16,192]{2,1,0:T(8,128)S(1)} %get-tuple-element.313), channel_id=1, source_target_pairs={{0,4},{1,5},{2,6},{3,7},{4,8},{5,9},{6,10},{7,11},{8,12},{9,13},{1... | collective-permute-start | bytes 221192 | tf_op jit(solution)/shard_map/ppermute | solution.py:34
  86.0 10.2 %copy-start.4 = (f32[6,128,6,16]{1,3,0,2:T(8,128)}, f32[6,128,6,16]{1,3,0,2:T(8,128)S(1)}, u32[]{:S(2)}) copy-start(f32[6,128,6,16]{1,3,0,2:T(8,128)S(1)} %copy.304) | copy-start | bytes 884740
  94.0 14.0 %copy-start.62 = (pred[6,128]{1,0:T(8,128)(4,1)S(1)}, pred[6,128]{1,0:T(8,128)(4,1)}, u32[]{:S(2)}) copy-start(pred[6,128]{1,0:T(8,128)(4,1)} %get-tuple-element.398) | copy-start | bytes 2308
  94.0 14.0 %copy-start.63 = (pred[6,128]{1,0:T(8,128)(4,1)S(1)}, pred[6,128]{1,0:T(8,128)(4,1)}, u32[]{:S(2)}) copy-start(pred[6,128]{1,0:T(8,128)(4,1)} %get-tuple-element.400) | copy-start | bytes 2308
  94.0 14.0 %copy-start.64 = (pred[6,128]{1,0:T(8,128)(4,1)S(1)}, pred[6,128]{1,0:T(8,128)(4,1)}, u32[]{:S(2)}) copy-start(pred[6,128]{1,0:T(8,128)(4,1)} %get-tuple-element.401) | copy-start | bytes 2308
  94.0 14.0 %copy-start.65 = (pred[6,128]{1,0:T(8,128)(4,1)S(1)}, pred[6,128]{1,0:T(8,128)(4,1)}, u32[]{:S(2)}) copy-start(pred[6,128]{1,0:T(8,128)(4,1)} %get-tuple-element.402) | copy-start | bytes 2308
  94.0 14.0 %copy-start.66 = (pred[6,128]{1,0:T(8,128)(4,1)S(1)}, pred[6,128]{1,0:T(8,128)(4,1)}, u32[]{:S(2)}) copy-start(pred[6,128]{1,0:T(8,128)(4,1)} %get-tuple-element.403) | copy-start | bytes 2308
  94.0 14.0 %copy-start.67 = (pred[6,128]{1,0:T(8,128)(4,1)S(1)}, pred[6,128]{1,0:T(8,128)(4,1)}, u32[]{:S(2)}) copy-start(pred[6,128]{1,0:T(8,128)(4,1)} %get-tuple-element.404) | copy-start | bytes 2308
  94.0 14.0 %copy-start.68 = (pred[6,128]{1,0:T(8,128)(4,1)S(1)}, pred[6,128]{1,0:T(8,128)(4,1)}, u32[]{:S(2)}) copy-start(pred[6,128]{1,0:T(8,128)(4,1)} %get-tuple-element.405) | copy-start | bytes 2308
  97.8 10.3 %copy-start.5 = (f32[6,128,6,16]{1,3,0,2:T(8,128)S(1)}, f32[6,128,6,16]{1,3,0,2:T(8,128)}, u32[]{:S(2)}) copy-start(f32[6,128,6,16]{1,3,0,2:T(8,128)} %copy-done.4) | copy-start | bytes 884740
  100.8 9.2 %copy-start.50 = (f32[16,16,1,1]{1,0,3,2:T(8,128)S(1)}, f32[16,16,1,1]{1,0,3,2:T(8,128)}, u32[]{:S(2)}) copy-start(f32[16,16,1,1]{1,0,3,2:T(8,128)} %constant.723) | copy-start | bytes 3076
  102.4 8.7 %copy-start.49 = (f32[16,16,1,1]{1,0,3,2:T(8,128)S(1)}, f32[16,16,1,1]{1,0,3,2:T(8,128)}, u32[]{:S(2)}) copy-start(f32[16,16,1,1]{1,0,3,2:T(8,128)} %constant.722) | copy-start | bytes 3076
  104.0 8.2 %copy-start.90 = (pred[4,64]{1,0:T(4,128)(4,1)S(1)}, pred[4,64]{1,0:T(4,128)(4,1)}, u32[]{:S(2)}) copy-start(pred[4,64]{1,0:T(4,128)(4,1)} %get-tuple-element.413) | copy-start | bytes 772
  104.0 8.2 %copy-start.92 = (pred[4,64]{1,0:T(4,128)(4,1)S(1)}, pred[4,64]{1,0:T(4,128)(4,1)}, u32[]{:S(2)}) copy-start(pred[4,64]{1,0:T(4,128)(4,1)} %get-tuple-element.414) | copy-start | bytes 772
  104.0 8.2 %copy-start.94 = (pred[4,64]{1,0:T(4,128)(4,1)S(1)}, pred[4,64]{1,0:T(4,128)(4,1)}, u32[]{:S(2)}) copy-start(pred[4,64]{1,0:T(4,128)(4,1)} %get-tuple-element.415) | copy-start | bytes 772
  104.1 8.2 %copy-start.96 = (pred[4,64]{1,0:T(4,128)(4,1)S(1)}, pred[4,64]{1,0:T(4,128)(4,1)}, u32[]{:S(2)}) copy-start(pred[4,64]{1,0:T(4,128)(4,1)} %get-tuple-element.416) | copy-start | bytes 772
  145.3 15.0 %copy-start.20 = (f32[2,4,4,128,4]{3,4,2,1,0:T(4,128)S(1)}, f32[2,4,4,128,4]{3,4,2,1,0:T(4,128)}, u32[]{:S(2)}) copy-start(f32[2,4,4,128,4]{3,4,2,1,0:T(4,128)} %fusion.48) | copy-start | bytes 196612
  145.4 15.0 %copy-start.21 = (f32[2,4,4,128,4]{3,4,2,1,0:T(4,128)S(1)}, f32[2,4,4,128,4]{3,4,2,1,0:T(4,128)}, u32[]{:S(2)}) copy-start(f32[2,4,4,128,4]{3,4,2,1,0:T(4,128)} %fusion.50) | copy-start | bytes 196612
  145.4 15.0 %copy-start.22 = (f32[2,4,4,128,4]{3,4,2,1,0:T(4,128)S(1)}, f32[2,4,4,128,4]{3,4,2,1,0:T(4,128)}, u32[]{:S(2)}) copy-start(f32[2,4,4,128,4]{3,4,2,1,0:T(4,128)} %fusion.55) | copy-start | bytes 196612
  145.4 15.0 %copy-start.23 = (f32[2,4,4,128,4]{3,4,2,1,0:T(4,128)S(1)}, f32[2,4,4,128,4]{3,4,2,1,0:T(4,128)}, u32[]{:S(2)}) copy-start(f32[2,4,4,128,4]{3,4,2,1,0:T(4,128)} %fusion.98) | copy-start | bytes 196612
  145.4 15.1 %copy-start.24 = (f32[2,4,4,4,128]{4,1,3,2,0:T(4,128)S(1)}, f32[2,4,4,4,128]{4,1,3,2,0:T(4,128)}, u32[]{:S(2)}) copy-start(f32[2,4,4,4,128]{4,1,3,2,0:T(4,128)} %fusion.58) | copy-start | bytes 196612
  145.4 15.1 %copy-start.25 = (f32[2,4,4,4,128]{4,1,3,2,0:T(4,128)S(1)}, f32[2,4,4,4,128]{4,1,3,2,0:T(4,128)}, u32[]{:S(2)}) copy-start(f32[2,4,4,4,128]{4,1,3,2,0:T(4,128)} %fusion.8) | copy-start | bytes 196612
  145.6 15.6 %collective-permute-start.8 = (f32[6,16,192]{2,1,0:T(8,128)S(1)}, f32[6,16,192]{2,1,0:T(8,128)S(1)}, u32[]{:S(2)}, u32[]{:S(2)}) collective-permute-start(f32[6,16,192]{2,1,0:T(8,128)S(1)} %get-tuple-element.312), channel_id=1, source_target_pairs={{4,0},{5,1},{6,2},{7,3},{8,4},{9,5},{10,6},{11,7},{12,8},{13,9},{1... | collective-permute-start | bytes 221192 | tf_op jit(solution)/shard_map/ppermute | solution.py:34
  147.5 17.1 %collective-permute-start.9 = (f32[6,16,192]{2,1,0:T(8,128)S(1)}, f32[6,16,192]{2,1,0:T(8,128)S(1)}, u32[]{:S(2)}, u32[]{:S(2)}) collective-permute-start(f32[6,16,192]{2,1,0:T(8,128)S(1)} %get-tuple-element.311), channel_id=1, source_target_pairs={{3,0},{4,1},{5,2},{6,3},{7,4},{8,5},{9,6},{10,7},{11,8},{12,9},{13... | collective-permute-start | bytes 221192 | tf_op jit(solution)/shard_map/ppermute | solution.py:34
  152.8 13.9 %collective-permute-start.10 = (f32[6,16,192]{2,1,0:T(8,128)S(1)}, f32[6,16,192]{2,1,0:T(8,128)S(1)}, u32[]{:S(2)}, u32[]{:S(2)}) collective-permute-start(f32[6,16,192]{2,1,0:T(8,128)S(1)} %get-tuple-element.310), channel_id=1, source_target_pairs={{2,0},{3,1},{4,2},{5,3},{6,4},{7,5},{8,6},{9,7},{10,8},{11,9},{12,... | collective-permute-start | bytes 221192 | tf_op jit(solution)/shard_map/ppermute | solution.py:34
  154.7 21.5 %collective-permute-start.11 = (f32[6,16,1,192]{3,1,0,2:T(8,128)S(1)}, f32[6,16,1,192]{3,1,0,2:T(8,128)S(1)}, u32[]{:S(2)}, u32[]{:S(2)}) collective-permute-start(f32[6,16,1,192]{3,1,0,2:T(8,128)S(1)} %get-tuple-element.309), channel_id=1, source_target_pairs={{1,0},{2,1},{3,2},{4,3},{5,4},{6,5},{7,6},{8,7},{9,8},{10,9},{11,1... | collective-permute-start | bytes 221192 | tf_op jit(solution)/shard_map/ppermute | solution.py:24
  157.0 19.4 %collective-permute-start.12 = (f32[6,16,1,192]{3,1,0,2:T(8,128)S(1)}, f32[6,16,1,192]{3,1,0,2:T(8,128)S(1)}, u32[]{:S(2)}, u32[]{:S(2)}) collective-permute-start(f32[6,16,1,192]{3,1,0,2:T(8,128)S(1)} %get-tuple-element.308), channel_id=1, source_target_pairs={{0,1},{1,2},{2,3},{3,4},{4,5},{5,6},{6,7},{7,8},{8,9},{9,10},{10,1... | collective-permute-start | bytes 221192 | tf_op jit(solution)/shard_map/ppermute | solution.py:22
  161.2 11.6 %collective-permute-start.13 = (f32[6,16,192]{2,1,0:T(8,128)S(1)}, f32[6,16,192]{2,1,0:T(8,128)S(1)}, u32[]{:S(2)}, u32[]{:S(2)}) collective-permute-start(f32[6,16,192]{2,1,0:T(8,128)S(1)} %get-tuple-element.307), channel_id=1, source_target_pairs={{0,2},{1,3},{2,4},{3,5},{4,6},{5,7},{6,8},{7,9},{8,10},{9,11},{10,... | collective-permute-start | bytes 221192 | tf_op jit(solution)/shard_map/ppermute | solution.py:34
  164.6 11.6 %collective-permute-start.14 = (f32[6,16,192]{2,1,0:T(8,128)S(1)}, f32[6,16,192]{2,1,0:T(8,128)S(1)}, u32[]{:S(2)}, u32[]{:S(2)}) collective-permute-start(f32[6,16,192]{2,1,0:T(8,128)S(1)} %get-tuple-element.306), channel_id=1, source_target_pairs={{0,3},{1,4},{2,5},{3,6},{4,7},{5,8},{6,9},{7,10},{8,11},{9,12},{10... | collective-permute-start | bytes 221192 | tf_op jit(solution)/shard_map/ppermute | solution.py:34
  166.7 11.2 %collective-permute-start.15 = (f32[6,16,192]{2,1,0:T(8,128)S(1)}, f32[6,16,192]{2,1,0:T(8,128)S(1)}, u32[]{:S(2)}, u32[]{:S(2)}) collective-permute-start(f32[6,16,192]{2,1,0:T(8,128)S(1)} %get-tuple-element.305), channel_id=1, source_target_pairs={{0,4},{1,5},{2,6},{3,7},{4,8},{5,9},{6,10},{7,11},{8,12},{9,13},{1... | collective-permute-start | bytes 221192 | tf_op jit(solution)/shard_map/ppermute | solution.py:34
  195.8 10.2 %copy-start.61 = (pred[4,64]{1,0:T(4,128)(4,1)S(1)}, pred[4,64]{1,0:T(4,128)(4,1)}, u32[]{:S(2)}) copy-start(pred[4,64]{1,0:T(4,128)(4,1)} %compare_and_fusion.2) | copy-start | bytes 772
  197.5 14.3 %copy-start.85 = (pred[4,64]{1,0:T(4,128)(4,1)S(1)}, pred[4,64]{1,0:T(4,128)(4,1)}, u32[]{:S(2)}) copy-start(pred[4,64]{1,0:T(4,128)(4,1)} %get-tuple-element.410) | copy-start | bytes 772
  197.6 14.3 %copy-start.87 = (pred[4,64]{1,0:T(4,128)(4,1)S(1)}, pred[4,64]{1,0:T(4,128)(4,1)}, u32[]{:S(2)}) copy-start(pred[4,64]{1,0:T(4,128)(4,1)} %get-tuple-element.411) | copy-start | bytes 772
  197.6 14.3 %copy-start.89 = (pred[4,64]{1,0:T(4,128)(4,1)S(1)}, pred[4,64]{1,0:T(4,128)(4,1)}, u32[]{:S(2)}) copy-start(pred[4,64]{1,0:T(4,128)(4,1)} %get-tuple-element.412) | copy-start | bytes 772
  197.6 14.3 %copy-start.91 = (pred[4,64]{1,0:T(4,128)(4,1)S(1)}, pred[4,64]{1,0:T(4,128)(4,1)}, u32[]{:S(2)}) copy-start(pred[4,64]{1,0:T(4,128)(4,1)} %get-tuple-element.413) | copy-start | bytes 772
  197.6 14.3 %copy-start.93 = (pred[4,64]{1,0:T(4,128)(4,1)S(1)}, pred[4,64]{1,0:T(4,128)(4,1)}, u32[]{:S(2)}) copy-start(pred[4,64]{1,0:T(4,128)(4,1)} %get-tuple-element.414) | copy-start | bytes 772
  197.6 14.3 %copy-start.95 = (pred[4,64]{1,0:T(4,128)(4,1)S(1)}, pred[4,64]{1,0:T(4,128)(4,1)}, u32[]{:S(2)}) copy-start(pred[4,64]{1,0:T(4,128)(4,1)} %get-tuple-element.415) | copy-start | bytes 772
  197.6 14.3 %copy-start.97 = (pred[4,64]{1,0:T(4,128)(4,1)S(1)}, pred[4,64]{1,0:T(4,128)(4,1)}, u32[]{:S(2)}) copy-start(pred[4,64]{1,0:T(4,128)(4,1)} %get-tuple-element.416) | copy-start | bytes 772
  (70 other events, 225.2 us)
where the time goes:
time: 230 us; the launch traced here: 226 us
  local copies, waits for them, and re-layouts  116 us (50%)
  starting transfers between devices  60.3 us (26%)
  other arithmetic  19.9 us (9%)
  matrix products  14.1 us (6%)
  waiting for transfers between devices  12.3 us (5%)
  between operations  3.45 us (2%)
    ppermute x12, starting transfers between devices, passed_along(): lax.ppermute(value, axis, [(source, source + steps) for source in range(f...  49.1 us
    gather x28, local copies, waits for them, and re-layouts, oriented(): permuted = whole_columns[:, orient_order(code_value)]  27.5 us
    gather x8, local copies, waits for them, and re-layouts, oriented(): whole_columns = jnp.take(trace_table, columns, axis=2)  21.1 us
    gather x4, local copies, waits for them, and re-layouts, local(): outgoing = jnp.take(own_table, send_face, axis=2)  20.7 us
    ppermute x12, waiting for transfers between devices, passed_along(): lax.ppermute(value, axis, [(source, source + steps) for source in range(f...  12.3 us
    concatenate x2, local copies, waits for them, and re-layouts, local(): jnp.concatenate([own_table, incoming.reshape(6, 16, -1)], axis=2)  10.4 us
    scatter x2, local copies, waits for them, and re-layouts, block_rates(): jnp.zeros((6, 16, 6 * elements + 1), jnp.float32).at[:, :, target_column]  9.27 us
    dot_general x8, matrix products, block_rates(): jnp.einsum('mn,fnge->fmge', interpolate[quarter], raw_trace, precision=hi...  7.47 us
  transfers between devices with their start and end apart: 16, of which 5 were waited for; matrix products, arithmetic and copies ran while one was open for 7% of the time, Pallas kernels for 0%

commit v1 on v0

v1 whole, which is shorter than its diff:
```python
import math

import jax
import jax.numpy as jnp
import numpy as np
from jax import lax
from jax.experimental import pallas as pl
from jax.experimental.pallas import tpu as pltpu
from jax.sharding import PartitionSpec as P

STEP_SIZE = 0.02
SECTION_A = (0.0, -567301805773.0 / 1357537059087.0)
SECTION_B = (1432997174477.0 / 9575080441755.0, 5161836677717.0 / 13612068292357.0)
UNIT = 144
LANES = 128
VMEM_LIMIT = 32 * 1024 * 1024


def gll_tables():
    points = np.array([-1.0, -1.0 / math.sqrt(5.0), 1.0 / math.sqrt(5.0), 1.0])
    weights = np.array([1.0, 5.0, 5.0, 1.0]) / 6.0

    def lagrange(where_at):
        values = np.ones((where_at.shape[0], 4))
        for column in range(4):
            for another in range(4):
                if another != column:
                    values[:, column] *= (where_at - points[another]) / (
                        points[column] - points[another]
                    )
        return values

    derivative = np.zeros((4, 4))
    for row_at in range(4):
        for column in range(4):
            summed = 0.0
            for another in range(4):
                if another == column:
                    continue
                factor = 1.0 / (points[column] - points[another])
                for further in range(4):
                    if further != column and further != another:
                        factor *= (points[row_at] - points[further]) / (
                            points[column] - points[further]
                        )
                summed += factor
            derivative[row_at, column] = summed
    halves = [lagrange((points - 1.0) / 2.0), lagrange((points + 1.0) / 2.0)]
    adjoint = [0.5 * halfway.T * weights[None, :] / weights[:, None] for halfway in halves]
    return derivative, halves, adjoint


def face_nodes(face):
    grid = np.arange(64).reshape(4, 4, 4)
    at = 3 if face % 2 else 0
    return [grid[at], grid[:, at], grid[:, :, at]][face // 2].reshape(16)


def volume_map():
    derivative, _, _ = gll_tables()
    eye = np.eye(4)
    along = [
        np.kron(np.kron(derivative, eye), eye),
        np.kron(np.kron(eye, derivative), eye),
        np.kron(np.kron(eye, eye), derivative),
    ]
    whole = np.zeros((6, 64, 6, 64))
    for a in range(3):
        b, c = (a + 1) % 3, (a + 2) % 3
        whole[a, :, 3 + c] += along[b]
        whole[a, :, 3 + b] -= along[c]
        whole[3 + a, :, c] -= along[b]
        whole[3 + a, :, b] += along[c]
    for face in range(6):
        a = face // 2
        b, c = (a + 1) % 3, (a + 2) % 3
        s = 1.0 if face % 2 else -1.0
        for n in face_nodes(face):
            whole[b, n, b, n] += 3.0
            whole[b, n, 3 + c, n] += 3.0 * s
            whole[c, n, c, n] += 3.0
            whole[c, n, 3 + b, n] -= 3.0 * s
            whole[3 + b, n, 3 + b, n] += 3.0
            whole[3 + b, n, c, n] -= 3.0 * s
            whole[3 + c, n, 3 + c, n] += 3.0
            whole[3 + c, n, b, n] += 3.0 * s
    return whole.reshape(384, 384)


def volume_operand():
    whole = volume_map().astype(np.float32)
    high = whole.astype(jnp.bfloat16)
    low = (whole - high.astype(np.float32)).astype(jnp.bfloat16)
    return np.concatenate([high, high, low], axis=1)


def halves_of(value):
    high = value.astype(jnp.bfloat16)
    low = (value - high.astype(jnp.float32)).astype(jnp.bfloat16)
    return high, low


def one_hot(rows, columns):
    at = lax.broadcasted_iota(jnp.int32, (rows, columns.shape[1]), 0)
    return jnp.where(at == columns, 1.0, 0.0).astype(jnp.bfloat16)


def picked(table, columns):
    rows = table.shape[0]
    both = jnp.concatenate(halves_of(table), axis=0)
    out = jnp.dot(both, columns, preferred_element_type=jnp.float32)
    return out[:rows] + out[rows:]


def write_table(u_ref, t_ref):
    for f in range(6):
        base = 64 * f
        rows = slice(16 * f, 16 * f + 16)
        t_ref[rows, 0:128] = u_ref[base : base + 16, :]
        t_ref[rows, 128:256] = u_ref[base + 48 : base + 64, :]
        for side, at in ((2, 0), (3, 12)):
            for i in range(4):
                start = base + 16 * i + at
                t_ref[16 * f + 4 * i : 16 * f + 4 * i + 4, 128 * side : 128 * side + 128] = u_ref[
                    start : start + 4, :
                ]
        t_ref[rows, 512:640] = u_ref[pl.ds(base, 16, stride=4), :]
        t_ref[rows, 640:768] = u_ref[pl.ds(base + 3, 16, stride=4), :]


def write_lists(core, t_ref, send_ref, swap_ref, own_ref):
    def listed(k, lanes):
        return jnp.where(core == 0, send_ref[k : k + 1, lanes], send_ref[7 - k : 8 - k, lanes])

    columns = [listed(k, slice(0, 128)) for k in range(8)]
    for pair in range(4):
        columns.append(
            jnp.concatenate(
                [listed(2 * pair, slice(128, 192)), listed(2 * pair + 1, slice(128, 192))], axis=1
            )
        )
    spread = jnp.concatenate([one_hot(768, column) for column in columns], axis=1)
    out = picked(t_ref[...], spread)
    first = lax.broadcasted_iota(jnp.int32, (48, LANES), 1) < 64
    places = {4 - d: (swap_ref, d - 1) for d in range(1, 5)}
    places[4] = (swap_ref, 4)
    places.update({3 + d: (own_ref, d - 2) for d in range(2, 5)})
    for k in range(8):
        ref, place = places[k]
        ref[UNIT * place : UNIT * place + 96, :] = out[:, 128 * k : 128 * k + 128]
        at = 1024 + 128 * (k // 2)
        upper, lower = out[0:48, at : at + 128], out[48:96, at : at + 128]
        if k % 2 == 0:
            packed = jnp.where(first, upper, pltpu.roll(lower, 64, 1))
        else:
            packed = jnp.where(first, pltpu.roll(upper, 64, 1), lower)
        ref[UNIT * place + 96 : UNIT * place + UNIT, :] = packed


def lists_kernel(core_ref, u_ref, send_ref, swap_ref, own_ref, t_ref):
    write_table(u_ref, t_ref)
    write_lists(core_ref[0], t_ref, send_ref, swap_ref, own_ref)


def mortar_row(ref):
    return jnp.concatenate([ref[q : q + 1, :] for q in range(4)], axis=1)


def local_kernel(u_ref, volume_ref, face_ref, mortar_ref, rate_ref, part_ref, t_ref):
    high, low = halves_of(u_ref[...])
    rate_ref[...] = jnp.dot(
        volume_ref[...],
        jnp.concatenate([high, low, high], axis=0),
        preferred_element_type=jnp.float32,
    )
    write_table(u_ref, t_ref)
    columns = [face_ref[face : face + 1, :] for face in range(6)] + [mortar_row(mortar_ref)]
    spread = jnp.concatenate([one_hot(768, column) for column in columns], axis=1)
    part_ref[...] = picked(t_ref[...], spread)


def write_received(core, swapped_ref, near_ref, far_ref, shared_ref, r_ref):
    other = 1 - core
    swapped = pl.multiple_of(other * (5 * UNIT) + 4 * UNIT, 8)
    shared = [pl.multiple_of(other * (3 * UNIT) + UNIT * place, 8) for place in range(3)]
    sources = [
        (shared_ref, shared[2]),
        (shared_ref, shared[0]),
        (shared_ref, shared[1]),
        (swapped_ref, swapped),
        (near_ref, UNIT),
        (near_ref, 0),
        (far_ref, UNIT),
        (far_ref, 0),
    ]
    first = lax.broadcasted_iota(jnp.int32, (48, LANES), 1) < 64
    rests = []
    for k, (ref, start) in enumerate(sources):
        r_ref[:, 128 * k : 128 * k + 128] = ref[pl.ds(start, 96), :]
        rests.append(ref[pl.ds(start + 96, 48), :])
    for pair in range(4):
        even, odd = rests[2 * pair], rests[2 * pair + 1]
        at = 1024 + 128 * pair
        r_ref[0:48, at : at + 128] = jnp.where(first, even, pltpu.roll(odd, 64, 1))
        r_ref[48:96, at : at + 128] = jnp.where(first, pltpu.roll(even, 64, 1), odd)


def received_column(core, source):
    remote = source - 768
    list_at = jnp.zeros_like(source)
    for k in range(1, 8):
        list_at = list_at + jnp.where(remote >= 192 * k, 1, 0)
    slot = remote - 192 * list_at
    seen = list_at + core * (7 - 2 * list_at)
    rest = 1024 + 64 * seen + slot - 128
    return jnp.where(remote < 0, -1, jnp.where(slot < 128, 128 * seen + slot, rest))


def turned(nodes, code):
    swap = code >= 4
    flip_a = (code & 1) == 1
    flip_b = (code & 2) == 2
    out = [
        [nodes[a][b] if a == b else jnp.where(swap, nodes[b][a], nodes[a][b]) for b in range(4)]
        for a in range(4)
    ]
    out = [[jnp.where(flip_a, out[3 - a][b], out[a][b]) for b in range(4)] for a in range(4)]
    return [[jnp.where(flip_b, out[a][3 - b], out[a][b]) for b in range(4)] for a in range(4)]


def applied(nodes, along_a, along_b):
    def summed(terms):
        return (terms[0] + terms[1]) + (terms[2] + terms[3])

    half = [
        [summed([along_a[a][x] * nodes[x][b] for x in range(4)]) for b in range(4)]
        for a in range(4)
    ]
    return [
        [summed([along_b[b][y] * half[a][y] for y in range(4)]) for b in range(4)]
        for a in range(4)
    ]


def exterior(core, gathered, code_ref, mortar_code_ref, target_ref, g_ref, m_ref):
    _, halves, adjoint = gll_tables()
    for face in range(6):
        a = face // 2
        b, c = (a + 1) % 3, (a + 2) % 3
        s = 1.0 if face % 2 else -1.0
        boundary = (code_ref[face : face + 1, :] >> 3) == 1
        sign = jnp.where(boundary, -1.0, 1.0)

        def field(index):
            return gathered[16 * index : 16 * index + 16, 128 * face : 128 * face + 128]

        g_ref[16 * face : 16 * face + 16, :] = sign * field(b) + s * field(3 + c)
        g_ref[96 + 16 * face : 96 + 16 * face + 16, :] = sign * field(c) - s * field(3 + b)
    code = code_ref[...]
    kind = code >> 3
    quarter = kind - 2
    plain = kind < 2
    live = kind < 6

    def chosen(which, row, column):
        refined = jnp.where(
            which == 1, float(halves[1][row, column]), float(halves[0][row, column])
        )
        kept = jnp.where(plain, 1.0 if row == column else 0.0, refined)
        return jnp.where(live, kept, 0.0)

    along_a = [[chosen(quarter & 1, i, j) for j in range(4)] for i in range(4)]
    along_b = [[chosen(quarter >> 1, i, j) for j in range(4)] for i in range(4)]
    for w in range(2):
        nodes = [
            [g_ref[pl.ds(96 * w + 4 * a + b, 6, stride=16), :] for b in range(4)] for a in range(4)
        ]
        out = applied(turned(nodes, code & 7), along_a, along_b)
        for a in range(4):
            for b in range(4):
                g_ref[pl.ds(96 * w + 4 * a + b, 6, stride=16), :] = out[a][b]

    target = jnp.concatenate([target_ref[...]] * 4, axis=1)
    face = jnp.zeros_like(target)
    for k in range(1, 6):
        face = face + jnp.where(target >= 128 * k, 1, 0)
    axis = face >> 1
    s = jnp.where((face & 1) == 1, 1.0, -1.0)

    def tangential(base, first):
        parts = [gathered[16 * (base + f) : 16 * (base + f) + 16, 768:1024] for f in range(3)]
        x, y, z = (parts[(first + k) % 3] for k in range(3))
        return jnp.where(axis == 0, x, jnp.where(axis == 1, y, z))

    for w, value in enumerate(
        (tangential(0, 1) + s * tangential(3, 2), tangential(0, 2) - s * tangential(3, 1))
    ):
        for half in range(2):
            rows = slice(32 * half + 16 * w, 32 * half + 16 * w + 16)
            m_ref[rows, :] = value[:, 128 * half : 128 * half + 128]
    lane = lax.broadcasted_iota(jnp.int32, (4, LANES), 1)
    row = lax.broadcasted_iota(jnp.int32, (4, LANES), 0)

    def weight(second, i, j):
        return jnp.where(second, float(adjoint[1][i, j]), float(adjoint[0][i, j]))

    project_a = [[weight(lane >= 64, i, j) for j in range(4)] for i in range(4)]
    project_b = [[weight(row >= 2, i, j) for j in range(4)] for i in range(4)]
    nodes = [[m_ref[pl.ds(4 * a + b, 4, stride=16), :] for b in range(4)] for a in range(4)]
    codes = mortar_row(mortar_code_ref)
    codes = jnp.where(row >= 2, codes[:, 128:256], codes[:, 0:128])
    out = applied(turned(nodes, codes), project_a, project_b)
    for a in range(4):
        for b in range(4):
            m_ref[pl.ds(4 * a + b, 4, stride=16), :] = out[a][b]
    pieces = jnp.concatenate([m_ref[0:32, :], m_ref[32:64, :]], axis=1)
    both = jnp.concatenate(halves_of(pieces), axis=0)
    placed = lax.dot_general(
        both, one_hot(768, target), (((1,), (1,)), ((), ())), preferred_element_type=jnp.float32
    )
    placed = placed[0:32] + placed[32:64]
    for w in range(2):
        for at in range(6):
            rows = slice(96 * w + 16 * at, 96 * w + 16 * at + 16)
            g_ref[rows, :] = (
                g_ref[rows, :] + placed[16 * w : 16 * w + 16, 128 * at : 128 * at + 128]
            )


def add_lift(rate_ref, g_ref):
    for face in range(6):
        a = face // 2
        b, c = (a + 1) % 3, (a + 2) % 3
        s = 3.0 if face % 2 else -3.0
        p = g_ref[16 * face : 16 * face + 16, :]
        q = g_ref[96 + 16 * face : 96 + 16 * face + 16, :]
        for f, value in ((b, -3.0 * p), (c, -3.0 * q), (3 + b, s * q), (3 + c, -s * p)):
            base = 64 * f
            if a == 0:
                at = base + (48 if face % 2 else 0)
                rate_ref[at : at + 16, :] = rate_ref[at : at + 16, :] + value
            elif a == 1:
                for i in range(4):
                    at = base + 16 * i + (12 if face % 2 else 0)
                    rate_ref[at : at + 4, :] = rate_ref[at : at + 4, :] + value[4 * i : 4 * i + 4]
            else:
                at = pl.ds(base + (3 if face % 2 else 0), 16, stride=4)
                rate_ref[at, :] = rate_ref[at, :] + value


def section_kernel(section, *refs):
    refs = list(refs)
    core_ref, u_ref = refs[0:2]
    del refs[0:2]
    register_ref = refs.pop(0) if section else None
    (
        rate_in_ref,
        part_ref,
        swapped_ref,
        near_ref,
        far_ref,
        shared_ref,
        material_ref,
        refinement_ref,
        face_ref,
        code_ref,
        mortar_ref,
        mortar_code_ref,
        target_ref,
    ) = refs[0:13]
    del refs[0:13]
    send_ref = None if section else refs.pop(0)
    new_u_ref, new_register_ref = refs[0:2]
    del refs[0:2]
    if section == 0:
        swap_ref, own_ref = refs[0:2]
        del refs[0:2]
    r_ref, g_ref, m_ref, rate_ref, t_ref = refs
    core = core_ref[0]
    write_received(core, swapped_ref, near_ref, far_ref, shared_ref, r_ref)
    at = received_column(core, face_ref[...])
    columns = [at[face : face + 1, :] for face in range(6)]
    columns.append(received_column(core, mortar_row(mortar_ref)))
    spread = jnp.concatenate([one_hot(1536, column) for column in columns], axis=1)
    gathered = part_ref[...] + picked(r_ref[...], spread)
    exterior(core, gathered, code_ref, mortar_code_ref, target_ref, g_ref, m_ref)
    rate_ref[...] = rate_in_ref[...]
    add_lift(rate_ref, g_ref)
    metric = jnp.where(
        refinement_ref[...] == 0, 1.0, jnp.where(refinement_ref[...] == 1, 2.0, 4.0)
    )
    for half in range(2):
        rows = slice(192 * half, 192 * half + 192)
        scale = STEP_SIZE * metric * material_ref[half : half + 1, :]
        register = scale * rate_ref[rows, :]
        if section:
            register = register + SECTION_A[section] * register_ref[rows, :]
        new_register_ref[rows, :] = register
        new_u_ref[rows, :] = u_ref[rows, :] + SECTION_B[section] * register
    if section == 0:
        write_table(new_u_ref, t_ref)
        write_lists(core, t_ref, send_ref, swap_ref, own_ref)


def vmem(count):
    return [pl.BlockSpec(memory_space=pltpu.VMEM)] * count


def floats(rows, columns=LANES):
    return jax.ShapeDtypeStruct((rows, columns), jnp.float32)


def called(kernel, core, operands, outputs, scratch):
    first = [] if core is None else [pl.BlockSpec(memory_space=pltpu.SMEM)]
    given = list(operands) if core is None else [core, *operands]
    return pl.pallas_call(
        kernel,
        in_specs=first + vmem(len(operands)),
        out_specs=vmem(len(outputs)),
        out_shape=outputs,
        scratch_shapes=[pltpu.VMEM(shape, jnp.float32) for shape in scratch],
        compiler_params=pltpu.CompilerParams(vmem_limit_bytes=VMEM_LIMIT),
    )(*given)


LIST_OUTPUTS = [floats(5 * UNIT), floats(3 * UNIT)]


def exchanged(core, swap, own):
    count = lax.axis_size("sfc")
    pairs = [[2 * chip, 2 * chip + 1] for chip in range(count // 2)]

    def ahead(chips):
        ends = [(i, i + 2 * chips if i % 2 == 0 else i - 2 * chips) for i in range(count)]
        return [(source, end) for source, end in ends if 0 <= end < count]

    swapped = lax.all_gather(swap, "sfc", axis_index_groups=pairs, tiled=True)
    theirs = lax.dynamic_slice_in_dim(swapped, (1 - core) * (5 * UNIT), 4 * UNIT)
    u = UNIT
    near = jnp.concatenate([own[0:u], theirs[0:u], own[u : 2 * u], theirs[u : 2 * u]])
    far = jnp.concatenate([own[2 * u : 3 * u], theirs[2 * u : 4 * u]])
    near = lax.ppermute(near, "sfc", ahead(1))
    far = lax.ppermute(far, "sfc", ahead(2))
    shared = jnp.concatenate([near[2 * u : 4 * u], far[2 * u : 3 * u]])
    shared = lax.all_gather(shared, "sfc", axis_index_groups=pairs, tiled=True)
    return swapped, near, far, shared


def local(
    fields,
    material,
    refinement,
    face_source,
    face_code,
    send_face,
    mortar_source,
    mortar_code,
    mortar_target,
):
    core = lax.rem(lax.axis_index("sfc"), 2).astype(jnp.int32)
    core_at = core.reshape(1)
    volume = jnp.asarray(volume_operand())
    solution = fields.reshape(384, LANES)
    refinement = refinement.reshape(1, LANES)
    target = mortar_target.reshape(1, 64)
    table = (96, 768)
    swap, own = called(lists_kernel, core_at, [solution, send_face], LIST_OUTPUTS, [table])
    register = None
    for section in range(2):
        received = exchanged(core, swap, own)
        rate, part = called(
            local_kernel,
            None,
            [solution, volume, face_source, mortar_source],
            [floats(384), floats(96, 1024)],
            [table],
        )
        operands = [solution] + ([register] if section else [])
        operands += [rate, part, *received, material, refinement]
        operands += [face_source, face_code, mortar_source, mortar_code, target]
        outputs = [floats(384), floats(384)]
        if section == 0:
            operands.append(send_face)
            outputs = outputs + LIST_OUTPUTS

        def kernel(*refs, section=section):
            section_kernel(section, *refs)

        results = called(
            kernel,
            core_at,
            operands,
            outputs,
            [(96, 1536), (192, LANES), (64, LANES), (384, LANES), table],
        )
        solution, register = results[0:2]
        if section == 0:
            swap, own = results[2:4]
    return (solution.reshape(6, 64, LANES), register.reshape(6, 64, LANES))


def solution(mesh):
    return jax.shard_map(
        local,
        mesh=mesh,
        in_specs=(
            P(None, None, "sfc"),
            P(None, "sfc"),
            P("sfc"),
            P(None, "sfc"),
            P(None, "sfc"),
            P(None, "sfc"),
            P(None, "sfc"),
            P(None, "sfc"),
            P("sfc"),
        ),
        out_specs=(P(None, None, "sfc"), P(None, None, "sfc")),
        check_vma=False,
    )
```

time: 230 us -> 59.1 us (0.26); the launches traced: 226 us -> 58.4 us
  local copies, waits for them, and re-layouts: 116 us -> 2.47 us
  starting transfers between devices: 60.3 us -> 25.8 us
  other arithmetic: 19.9 us -> 0.11 us
  matrix products: 14.1 us -> 0 us
  blocking collectives: 0 us -> 12.6 us
  Pallas kernels: 0 us -> 6.21 us
  between operations: 3.45 us -> 0.89 us
    gather x40 -> x0, local copies, waits for them, and re-layouts: 69.2 us -> none  [the longest x28 27.5 us: oriented(): permuted = whole_columns[:, orient_order(code_value)]]
    ppermute x16 -> x4, starting transfers between devices: 60.3 us -> 25.8 us  [the longest x2 20.6 us: exchanged(): near = lax.ppermute(near, 'sfc', ahead(1))]
    dot_general x22 -> x0, matrix products: 14.1 us -> none  [the longest x8 7.47 us: block_rates(): jnp.einsum('mn,fnge->fmge', interpolate[quarter], raw_trace, precision=hi...]
    all_gather x0 -> x4, blocking collectives: none -> 12.6 us  [the longest x2 7.62 us: exchanged(): shared = lax.all_gather(shared, 'sfc', axis_index_groups=pairs, tiled=True)]
    concatenate x2 -> x0, local copies, waits for them, and re-layouts: 10.4 us -> none  [local(): jnp.concatenate([own_table, incoming.reshape(6, 16, -1)], axis=2)]
    scatter x2 -> x0, local copies, waits for them, and re-layouts: 9.27 us -> none  [block_rates(): jnp.zeros((6, 16, 6 * elements + 1), jnp.float32).at[:, :, target_column]]
    reshape x8 -> x0, local copies, waits for them, and re-layouts: 7.7 us -> none  [the longest x2 4.69 us: block_rates(): placed = placed[:, :, :6 * elements].reshape(6, 16, 6, elements)]
    select_n x13 -> x0, other arithmetic: 6.83 us -> none  [the longest x4 5.26 us: oriented(): result = jnp.where(orient_codes[None, None] == code_value, permuted, result)]
  transfers between devices with their start and end apart: 16 -> 4, of which waited for: 5 -> 2; matrix products, arithmetic and copies ran while one was open for 7% -> 0% of each run, Pallas kernels for 0% -> 2%
where the time goes in v1:
time: 59.1 us; the launch traced here: 58.4 us
  starting transfers between devices  25.8 us (44%)
  blocking collectives  12.6 us (21%)
  waiting for transfers between devices  10.3 us (17%)
  Pallas kernels  6.21 us (11%)
  local copies, waits for them, and re-layouts  2.47 us (4%)
  between operations  0.89 us (2%)
    ppermute x2, starting transfers between devices, exchanged(): near = lax.ppermute(near, 'sfc', ahead(1))  20.6 us
    ppermute x2, waiting for transfers between devices, exchanged(): far = lax.ppermute(far, 'sfc', ahead(2))  10.3 us
    all_gather x2, blocking collectives, exchanged(): shared = lax.all_gather(shared, 'sfc', axis_index_groups=pairs, tiled=True)  7.62 us
    pallas_call x5, Pallas kernels, called(): pl.pallas_call(kernel, in_specs=first + vmem(len(operands)), out_specs=vm...  6.21 us
    ppermute x2, starting transfers between devices, exchanged(): far = lax.ppermute(far, 'sfc', ahead(2))  5.13 us
    all_gather x2, blocking collectives, exchanged(): swapped = lax.all_gather(swap, 'sfc', axis_index_groups=pairs, tiled=True)  4.97 us
    unnamed x22, local copies, waits for them, and re-layouts  2.35 us
  transfers between devices with their start and end apart: 4, of which 2 were waited for; matrix products, arithmetic and copies ran while one was open for 0% of the time, Pallas kernels for 2%

profile of v1, /device:TPU:7, one launch (start us, length us, event | category | flops | bytes accessed | tf_op | source)
XLA Modules:
  0.0 58.4 jit_solution(14167335412388355463)
XLA Ops:
  0.6 0.0 copy-start.5
  0.6 0.7 %copy-done.5 = s32[8,192]{1,0:T(8,128)S(1)} copy-done((s32[8,192]{1,0:T(8,128)S(1)}, s32[8,192]{1,0:T(8,128)}, u32[]{:S(2)}) %copy-start.5) | copy-done | bytes 6168
  1.3 0.0 copy-start.1
  1.3 0.9 %copy-done.1 = f32[6,64,128]{2,1,0:T(8,128)S(1)} copy-done((f32[6,64,128]{2,1,0:T(8,128)S(1)}, f32[6,64,128]{2,1,0:T(8,128)}, u32[]{:S(2)}) %copy-start.1) | copy-done | bytes 196632
  2.3 0.8 %shard_map.114 = (f32[720,128]{1,0:T(8,128)S(1)}, f32[432,128]{1,0:T(8,128)S(1)}) custom-call(s32[1]{0:T(128)} %bitcast.core_ref.refs_0_, f32[384,128]{1,0:T(8,128)S(1)} %bitcast.6, s32[8,192]{1,0:T(8,128)S(1)} %copy-done.5), custom_call_target="tpu_custom_call" | custom-call | tf_op jit(solution)/shard_map/pallas_call | solution.py:416
  3.1 2.6 %all_gather.12.refs_4_ = f32[1440,128]{1,0:T(8,128)S(1)} all-gather(f32[720,128]{1,0:T(8,128)S(1)} %get-tuple-element.16), channel_id=1, replica_groups={{0,1},{2,3},{4,5},{6,7},{8,9},{10,11},{12,13},{14,15},{16,17},{18,19},{..., dimensions={0}, use_global_device_ids=true | all-gather | bytes 1105920 | tf_op jit(solution)/shard_map/all_gather | solution.py:437
  5.7 0.0 copy-start
  5.8 14.0 %collective-permute-start = (f32[576,128]{1,0:T(8,128)S(1)}, f32[576,128]{1,0:T(8,128)S(1)}, u32[]{:S(2)}, u32[]{:S(2)}) collective-permute-start(f32[576,128]{1,0:T(8,128)S(1)} %pad_maximum_fusion), channel_id=1, source_target_pairs={{0,2},{2,4},{3,1},{4,6},{5,3},{6,8},{7,5},{8,10},{9,7},{10,12},{11... | collective-permute-start | bytes 884744 | tf_op jit(solution)/shard_map/ppermute | solution.py:442
  19.7 0.0 copy-start.2
  19.8 0.0 copy-start.3
  19.8 0.0 copy-start.4
  19.8 3.2 %collective-permute-start.1 = (f32[432,128]{1,0:T(8,128)S(1)}, f32[432,128]{1,0:T(8,128)S(1)}, u32[]{:S(2)}, u32[]{:S(2)}) collective-permute-start(f32[432,128]{1,0:T(8,128)S(1)} %pad_maximum_fusion.2), channel_id=1, source_target_pairs={{0,4},{2,6},{4,8},{5,1},{6,10},{7,3},{8,12},{9,5},{10,14},{11,7},{... | collective-permute-start | bytes 663560 | tf_op jit(solution)/shard_map/ppermute | solution.py:443
  23.0 0.0 copy-done
  23.0 0.0 copy-done.2
  23.1 0.0 copy-done.3
  23.1 0.0 copy-done.4
  23.1 0.7 %shard_map.113 = (f32[384,128]{1,0:T(8,128)S(1)}, f32[96,1024]{1,0:T(8,128)S(1)}) custom-call(f32[384,128]{1,0:T(8,128)S(1)} %bitcast.7, bf16[384,1152]{1,0:T(8,128)(2,1)S(1)} %copy-done, s32[6,128]{1,0:T(8,128)S(1)} %copy-done.3, s32[4,64]{1,0:T(4,128)S(1)} %copy-done.4), custom_call_target="tpu_custom_call" | custom-call | tf_op jit(solution)/shard_map/pallas_call | solution.py:416
  23.8 4.1 %collective-permute-done.1.refs_6_ = f32[432,128]{1,0:T(8,128)S(1)} collective-permute-done((f32[432,128]{1,0:T(8,128)S(1)}, f32[432,128]{1,0:T(8,128)S(1)}, u32[]{:S(2)}, u32[]{:S(2)}) %collective-permute-start.1) | collective-permute-done | bytes 221216 | tf_op jit(solution)/shard_map/ppermute | solution.py:443
  27.9 0.0 collective-permute-done.refs_5_
  27.9 0.0 copy-start.10
  27.9 4.4 %all_gather.13.refs_7_ = f32[864,128]{1,0:T(8,128)S(1)} all-gather(f32[432,128]{1,0:T(8,128)S(1)} %pad_maximum_fusion.3), channel_id=1, replica_groups={{0,1},{2,3},{4,5},{6,7},{8,9},{10,11},{12,13},{14,15},{16,17},{18,19},{..., dimensions={0}, use_global_device_ids=true | all-gather | bytes 663552 | tf_op jit(solution)/shard_map/all_gather | solution.py:445
  32.3 0.0 copy-start.6
  32.3 0.0 copy-start.7
  32.3 0.0 copy-start.8
  32.3 0.0 copy-start.9
  32.3 0.0 copy-done.10
  32.3 0.7 %copy-done.6 = s32[6,128]{1,0:T(8,128)S(1)} copy-done((s32[6,128]{1,0:T(8,128)S(1)}, s32[6,128]{1,0:T(8,128)}, u32[]{:S(2)}) %copy-start.6) | copy-done | bytes 3096
  33.0 0.0 copy-done.7
  33.0 0.0 copy-done.8
  33.0 0.0 copy-done.9
  33.0 2.0 %shard_map.115 = (f32[384,128]{1,0:T(8,128)S(1)}, f32[384,128]{1,0:T(8,128)S(1)}, f32[720,128]{1,0:T(8,128)S(1)}, f32[432,128]{1,0:T(8,128)S(1)}) custom-call(s32[1]{0:T(128)} %bitcast.core_ref.refs_0_, f32[384,128]{1,0:T(8,128)S(1)} %bitcast.8, f32[384,128]{1,0:T(8,128)S(1)} %get-tuple-element.14.refs_2_, f32[96,1024]{1,0:T(8,128)S(1)} %get-tuple-element.15.refs_3_, ...), custom_call_target="tpu_custom_call" | custom-call | tf_op jit(solution)/shard_map/pallas_call | solution.py:416
  35.0 2.3 %all_gather.14.refs_5_ = f32[1440,128]{1,0:T(8,128)S(1)} all-gather(f32[720,128]{1,0:T(8,128)S(1)} %get-tuple-element.22), channel_id=1, replica_groups={{0,1},{2,3},{4,5},{6,7},{8,9},{10,11},{12,13},{14,15},{16,17},{18,19},{..., dimensions={0}, use_global_device_ids=true | all-gather | bytes 1105920 | tf_op jit(solution)/shard_map/all_gather | solution.py:437
  37.5 6.7 %collective-permute-start.2 = (f32[576,128]{1,0:T(8,128)S(1)}, f32[576,128]{1,0:T(8,128)S(1)}, u32[]{:S(2)}, u32[]{:S(2)}) collective-permute-start(f32[576,128]{1,0:T(8,128)S(1)} %pad_maximum_fusion.1), channel_id=1, source_target_pairs={{0,2},{2,4},{3,1},{4,6},{5,3},{6,8},{7,5},{8,10},{9,7},{10,12},{11... | collective-permute-start | bytes 884744 | tf_op jit(solution)/shard_map/ppermute | solution.py:442
  44.2 1.9 %collective-permute-start.3 = (f32[432,128]{1,0:T(8,128)S(1)}, f32[432,128]{1,0:T(8,128)S(1)}, u32[]{:S(2)}, u32[]{:S(2)}) collective-permute-start(f32[432,128]{1,0:T(8,128)S(1)} %pad_maximum_fusion.4), channel_id=1, source_target_pairs={{0,4},{2,6},{4,8},{5,1},{6,10},{7,3},{8,12},{9,5},{10,14},{11,7},{... | collective-permute-start | bytes 663560 | tf_op jit(solution)/shard_map/ppermute | solution.py:443
  46.1 0.7 %shard_map.116 = (f32[384,128]{1,0:T(8,128)S(1)}, f32[96,1024]{1,0:T(8,128)S(1)}) custom-call(f32[384,128]{1,0:T(8,128)S(1)} %get-tuple-element.18.u_ref.refs_1_, bf16[384,1152]{1,0:T(8,128)(2,1)S(1)} %copy-done, s32[6,128]{1,0:T(8,128)S(1)} %copy-done.3, s32[4,64]{1,0:T(4,128)S(1)} %copy-done.4), custom_call_target="tpu_custom_call" | custom-call | tf_op jit(solution)/shard_map/pallas_call | solution.py:416
  46.8 6.2 %collective-permute-done.3.refs_7_ = f32[432,128]{1,0:T(8,128)S(1)} collective-permute-done((f32[432,128]{1,0:T(8,128)S(1)}, f32[432,128]{1,0:T(8,128)S(1)}, u32[]{:S(2)}, u32[]{:S(2)}) %collective-permute-start.3) | collective-permute-done | bytes 221216 | tf_op jit(solution)/shard_map/ppermute | solution.py:443
  53.0 0.0 collective-permute-done.2.refs_6_
  53.1 3.3 %all_gather.15.refs_8_ = f32[864,128]{1,0:T(8,128)S(1)} all-gather(f32[432,128]{1,0:T(8,128)S(1)} %pad_maximum_fusion.5), channel_id=1, replica_groups={{0,1},{2,3},{4,5},{6,7},{8,9},{10,11},{12,13},{14,15},{16,17},{18,19},{..., dimensions={0}, use_global_device_ids=true | all-gather | bytes 663552 | tf_op jit(solution)/shard_map/all_gather | solution.py:445
  56.4 2.0 %shard_map.117 = (f32[384,128]{1,0:T(8,128)}, f32[384,128]{1,0:T(8,128)}) custom-call(s32[1]{0:T(128)} %bitcast.core_ref.refs_0_, f32[384,128]{1,0:T(8,128)S(1)} %get-tuple-element.18.u_ref.refs_1_, f32[384,128]{1,0:T(8,128)S(1)} %get-tuple-element.19.refs_2_, f32[384,128]{1,0:T(8,128)S(1)} %get-tuple-element.20.refs_3_, ...), custom_call_target="tpu_custom_call" | custom-call | tf_op jit(solution)/shard_map/pallas_call | solution.py:416
  (16 shorter events, 0.2 us)
Async XLA Ops:
  0.6 0.7 %copy-start.5 = (s32[8,192]{1,0:T(8,128)S(1)}, s32[8,192]{1,0:T(8,128)}, u32[]{:S(2)}) copy-start(s32[8,192]{1,0:T(8,128)} %refs_15_.1) | copy-start | bytes 18436
  1.3 0.9 %copy-start.1 = (f32[6,64,128]{2,1,0:T(8,128)S(1)}, f32[6,64,128]{2,1,0:T(8,128)}, u32[]{:S(2)}) copy-start(f32[6,64,128]{2,1,0:T(8,128)} %param.10) | copy-start | bytes 589828
  5.7 17.3 %copy-start = (bf16[384,1152]{1,0:T(8,128)(2,1)S(1)}, bf16[384,1152]{1,0:T(8,128)(2,1)}, u32[]{:S(2)}) copy-start(bf16[384,1152]{1,0:T(8,128)(2,1)} %constant.17.clone.volume_ref) | copy-start | bytes 2654212
  5.8 22.1 %collective-permute-start = (f32[576,128]{1,0:T(8,128)S(1)}, f32[576,128]{1,0:T(8,128)S(1)}, u32[]{:S(2)}, u32[]{:S(2)}) collective-permute-start(f32[576,128]{1,0:T(8,128)S(1)} %pad_maximum_fusion), channel_id=1, source_target_pairs={{0,2},{2,4},{3,1},{4,6},{5,3},{6,8},{7,5},{8,10},{9,7},{10,12},{11... | collective-permute-start | bytes 884744 | tf_op jit(solution)/shard_map/ppermute | solution.py:442
  19.7 3.3 %copy-start.2 = (f32[6,64,128]{2,1,0:T(8,128)S(1)}, f32[6,64,128]{2,1,0:T(8,128)}, u32[]{:S(2)}) copy-start(f32[6,64,128]{2,1,0:T(8,128)} %param.10) | copy-start | bytes 589828
  19.8 3.3 %copy-start.3 = (s32[6,128]{1,0:T(8,128)S(1)}, s32[6,128]{1,0:T(8,128)}, u32[]{:S(2)}) copy-start(s32[6,128]{1,0:T(8,128)} %refs_11_.3) | copy-start | bytes 9220
  19.8 3.3 %copy-start.4 = (s32[4,64]{1,0:T(4,128)S(1)}, s32[4,64]{1,0:T(4,128)}, u32[]{:S(2)}) copy-start(s32[4,64]{1,0:T(4,128)} %refs_13_.3) | copy-start | bytes 3076
  19.8 8.0 %collective-permute-start.1 = (f32[432,128]{1,0:T(8,128)S(1)}, f32[432,128]{1,0:T(8,128)S(1)}, u32[]{:S(2)}, u32[]{:S(2)}) collective-permute-start(f32[432,128]{1,0:T(8,128)S(1)} %pad_maximum_fusion.2), channel_id=1, source_target_pairs={{0,4},{2,6},{4,8},{5,1},{6,10},{7,3},{8,12},{9,5},{10,14},{11,7},{... | collective-permute-start | bytes 663560 | tf_op jit(solution)/shard_map/ppermute | solution.py:443
  27.9 4.4 %copy-start.10 = (s32[64]{0:T(128)S(1)}, s32[64]{0:T(128)}, u32[]{:S(2)}) copy-start(s32[64]{0:T(128)} %param.18) | copy-start | bytes 772
  32.3 0.7 %copy-start.6 = (s32[6,128]{1,0:T(8,128)S(1)}, s32[6,128]{1,0:T(8,128)}, u32[]{:S(2)}) copy-start(s32[6,128]{1,0:T(8,128)} %refs_12_.3) | copy-start | bytes 9220
  32.3 0.7 %copy-start.7 = (s32[4,64]{1,0:T(4,128)S(1)}, s32[4,64]{1,0:T(4,128)}, u32[]{:S(2)}) copy-start(s32[4,64]{1,0:T(4,128)} %refs_14_.1) | copy-start | bytes 3076
  32.3 0.7 %copy-start.8 = (f32[2,128]{1,0:T(2,128)S(1)}, f32[2,128]{1,0:T(2,128)}, u32[]{:S(2)}) copy-start(f32[2,128]{1,0:T(2,128)} %refs_9_.1) | copy-start | bytes 3076
  32.3 0.7 %copy-start.9 = (s32[128]{0:T(128)S(1)}, s32[128]{0:T(128)}, u32[]{:S(2)}) copy-start(s32[128]{0:T(128)} %param.12) | copy-start | bytes 1540
  37.5 15.6 %collective-permute-start.2 = (f32[576,128]{1,0:T(8,128)S(1)}, f32[576,128]{1,0:T(8,128)S(1)}, u32[]{:S(2)}, u32[]{:S(2)}) collective-permute-start(f32[576,128]{1,0:T(8,128)S(1)} %pad_maximum_fusion.1), channel_id=1, source_target_pairs={{0,2},{2,4},{3,1},{4,6},{5,3},{6,8},{7,5},{8,10},{9,7},{10,12},{11... | collective-permute-start | bytes 884744 | tf_op jit(solution)/shard_map/ppermute | solution.py:442
  44.2 8.9 %collective-permute-start.3 = (f32[432,128]{1,0:T(8,128)S(1)}, f32[432,128]{1,0:T(8,128)S(1)}, u32[]{:S(2)}, u32[]{:S(2)}) collective-permute-start(f32[432,128]{1,0:T(8,128)S(1)} %pad_maximum_fusion.4), channel_id=1, source_target_pairs={{0,4},{2,6},{4,8},{5,1},{6,10},{7,3},{8,12},{9,5},{10,14},{11,7},{... | collective-permute-start | bytes 663560 | tf_op jit(solution)/shard_map/ppermute | solution.py:443

commit v2 on v1

--- a/solution.py
+++ b/solution.py
@@ -13,7 +13,7 @@
 SECTION_B = (1432997174477.0 / 9575080441755.0, 5161836677717.0 / 13612068292357.0)
 UNIT = 144
 LANES = 128
-VMEM_LIMIT = 32 * 1024 * 1024
+VMEM_LIMIT = 24 * 1024 * 1024
 
 
 def gll_tables():
@@ -128,18 +128,18 @@
         t_ref[rows, 640:768] = u_ref[pl.ds(base + 3, 16, stride=4), :]
 
 
-def write_lists(core, t_ref, send_ref, swap_ref, own_ref):
+def list_spread(core, send_ref):
     def listed(k, lanes):
         return jnp.where(core == 0, send_ref[k : k + 1, lanes], send_ref[7 - k : 8 - k, lanes])
 
     columns = [listed(k, slice(0, 128)) for k in range(8)]
     for pair in range(4):
-        columns.append(
-            jnp.concatenate(
-                [listed(2 * pair, slice(128, 192)), listed(2 * pair + 1, slice(128, 192))], axis=1
-            )
-        )
-    spread = jnp.concatenate([one_hot(768, column) for column in columns], axis=1)
+        rests = [listed(2 * pair + k, slice(128, 192)) for k in range(2)]
+        columns.append(jnp.concatenate(rests, axis=1))
+    return jnp.concatenate([one_hot(768, column) for column in columns], axis=1)
+
+
+def write_lists(t_ref, spread, swap_ref, own_ref):
     out = picked(t_ref[...], spread)
     first = lax.broadcasted_iota(jnp.int32, (48, LANES), 1) < 64
     places = {4 - d: (swap_ref, d - 1) for d in range(1, 5)}
@@ -159,14 +159,14 @@
 
 def lists_kernel(core_ref, u_ref, send_ref, swap_ref, own_ref, t_ref):
     write_table(u_ref, t_ref)
-    write_lists(core_ref[0], t_ref, send_ref, swap_ref, own_ref)
+    write_lists(t_ref, list_spread(core_ref[0], send_ref), swap_ref, own_ref)
 
 
 def mortar_row(ref):
     return jnp.concatenate([ref[q : q + 1, :] for q in range(4)], axis=1)
 
 
-def local_kernel(u_ref, volume_ref, face_ref, mortar_ref, rate_ref, part_ref, t_ref):
+def local_part(u_ref, volume_ref, face_ref, mortar_ref, rate_ref, part_ref, t_ref):
     high, low = halves_of(u_ref[...])
     rate_ref[...] = jnp.dot(
         volume_ref[...],
@@ -177,6 +177,50 @@
     columns = [face_ref[face : face + 1, :] for face in range(6)] + [mortar_row(mortar_ref)]
     spread = jnp.concatenate([one_hot(768, column) for column in columns], axis=1)
     part_ref[...] = picked(t_ref[...], spread)
+
+
+def first_kernel(
+    core_ref,
+    u_ref,
+    volume_ref,
+    face_ref,
+    mortar_ref,
+    code_ref,
+    mortar_code_ref,
+    target_ref,
+    material_ref,
+    refinement_ref,
+    send_ref,
+    rate_ref,
+    part_ref,
+    list_spread_ref,
+    spread_ref,
+    place_ref,
+    codes_ref,
+    scale_ref,
+    t_ref,
+):
+    local_part(u_ref, volume_ref, face_ref, mortar_ref, rate_ref, part_ref, t_ref)
+    core = core_ref[0]
+    list_spread_ref[...] = list_spread(core, send_ref)
+    at = received_column(core, face_ref[...])
+    columns = [at[face : face + 1, :] for face in range(6)]
+    columns.append(received_column(core, mortar_row(mortar_ref)))
+    spread_ref[...] = jnp.concatenate([one_hot(1536, column) for column in columns], axis=1)
+    target = jnp.concatenate([target_ref[...]] * 4, axis=1)
+    place_ref[...] = one_hot(768, target)
+    face = jnp.zeros_like(target)
+    for k in range(1, 6):
+        face = face + jnp.where(target >= 128 * k, 1, 0)
+    row = lax.broadcasted_iota(jnp.int32, (4, LANES), 0)
+    codes = mortar_row(mortar_code_ref)
+    codes_ref[0:6, :] = code_ref[...]
+    codes_ref[6:8, :] = jnp.zeros((2, LANES), jnp.int32)
+    codes_ref[8:12, :] = jnp.where(row >= 2, codes[:, 128:256], codes[:, 0:128])
+    codes_ref[12:16, :] = jnp.where(row >= 2, face[:, 128:256], face[:, 0:128])
+    level = refinement_ref[...]
+    metric = jnp.where(level == 0, 1.0, jnp.where(level == 1, 2.0, 4.0))
+    scale_ref[...] = STEP_SIZE * metric * material_ref[...]
 
 
 def write_received(core, swapped_ref, near_ref, far_ref, shared_ref, r_ref):
@@ -242,13 +286,13 @@
     ]
 
 
-def exterior(core, gathered, code_ref, mortar_code_ref, target_ref, g_ref, m_ref):
+def exterior(gathered, codes_ref, place_ref, g_ref, m_ref):
     _, halves, adjoint = gll_tables()
     for face in range(6):
         a = face // 2
         b, c = (a + 1) % 3, (a + 2) % 3
         s = 1.0 if face % 2 else -1.0
-        boundary = (code_ref[face : face + 1, :] >> 3) == 1
+        boundary = (codes_ref[face : face + 1, :] >> 3) == 1
         sign = jnp.where(boundary, -1.0, 1.0)
 
         def field(index):
@@ -256,7 +300,7 @@
 
         g_ref[16 * face : 16 * face + 16, :] = sign * field(b) + s * field(3 + c)
         g_ref[96 + 16 * face : 96 + 16 * face + 16, :] = sign * field(c) - s * field(3 + b)
-    code = code_ref[...]
+    code = codes_ref[0:6, :]
     kind = code >> 3
     quarter = kind - 2
     plain = kind < 2
@@ -280,24 +324,21 @@
             for b in range(4):
                 g_ref[pl.ds(96 * w + 4 * a + b, 6, stride=16), :] = out[a][b]
 
-    target = jnp.concatenate([target_ref[...]] * 4, axis=1)
-    face = jnp.zeros_like(target)
-    for k in range(1, 6):
-        face = face + jnp.where(target >= 128 * k, 1, 0)
-    axis = face >> 1
-    s = jnp.where((face & 1) == 1, 1.0, -1.0)
-
-    def tangential(base, first):
-        parts = [gathered[16 * (base + f) : 16 * (base + f) + 16, 768:1024] for f in range(3)]
-        x, y, z = (parts[(first + k) % 3] for k in range(3))
-        return jnp.where(axis == 0, x, jnp.where(axis == 1, y, z))
-
-    for w, value in enumerate(
-        (tangential(0, 1) + s * tangential(3, 2), tangential(0, 2) - s * tangential(3, 1))
-    ):
-        for half in range(2):
-            rows = slice(32 * half + 16 * w, 32 * half + 16 * w + 16)
-            m_ref[rows, :] = value[:, 128 * half : 128 * half + 128]
+    for half in range(2):
+        face = codes_ref[13 + half : 14 + half, :]
+        axis = face >> 1
+        s = jnp.where((face & 1) == 1, 1.0, -1.0)
+        lanes = slice(768 + 128 * half, 896 + 128 * half)
+
+        def tangential(base, first):
+            x, y, z = (
+                gathered[16 * f : 16 * f + 16, lanes]
+                for f in (base + (first + k) % 3 for k in range(3))
+            )
+            return jnp.where(axis == 0, x, jnp.where(axis == 1, y, z))
+
+        m_ref[32 * half : 32 * half + 16, :] = tangential(0, 1) + s * tangential(3, 2)
+        m_ref[32 * half + 16 : 32 * half + 32, :] = tangential(0, 2) - s * tangential(3, 1)
     lane = lax.broadcasted_iota(jnp.int32, (4, LANES), 1)
     row = lax.broadcasted_iota(jnp.int32, (4, LANES), 0)
 
@@ -307,16 +348,14 @@
     project_a = [[weight(lane >= 64, i, j) for j in range(4)] for i in range(4)]
     project_b = [[weight(row >= 2, i, j) for j in range(4)] for i in range(4)]
     nodes = [[m_ref[pl.ds(4 * a + b, 4, stride=16), :] for b in range(4)] for a in range(4)]
-    codes = mortar_row(mortar_code_ref)
-    codes = jnp.where(row >= 2, codes[:, 128:256], codes[:, 0:128])
-    out = applied(turned(nodes, codes), project_a, project_b)
+    out = applied(turned(nodes, codes_ref[8:12, :]), project_a, project_b)
     for a in range(4):
         for b in range(4):
             m_ref[pl.ds(4 * a + b, 4, stride=16), :] = out[a][b]
     pieces = jnp.concatenate([m_ref[0:32, :], m_ref[32:64, :]], axis=1)
     both = jnp.concatenate(halves_of(pieces), axis=0)
     placed = lax.dot_general(
-        both, one_hot(768, target), (((1,), (1,)), ((), ())), preferred_element_type=jnp.float32
+        both, place_ref[...], (((1,), (1,)), ((), ())), preferred_element_type=jnp.float32
     )
     placed = placed[0:32] + placed[32:64]
     for w in range(2):
@@ -353,23 +392,10 @@
     core_ref, u_ref = refs[0:2]
     del refs[0:2]
     register_ref = refs.pop(0) if section else None
-    (
-        rate_in_ref,
-        part_ref,
-        swapped_ref,
-        near_ref,
-        far_ref,
-        shared_ref,
-        material_ref,
-        refinement_ref,
-        face_ref,
-        code_ref,
-        mortar_ref,
-        mortar_code_ref,
-        target_ref,
-    ) = refs[0:13]
-    del refs[0:13]
-    send_ref = None if section else refs.pop(0)
+    rate_in_ref, part_ref, swapped_ref, near_ref, far_ref, shared_ref = refs[0:6]
+    spread_ref, place_ref, codes_ref, scale_ref = refs[6:10]
+    del refs[0:10]
+    list_spread_ref = None if section else refs.pop(0)
     new_u_ref, new_register_ref = refs[0:2]
     del refs[0:2]
     if section == 0:
@@ -378,36 +404,24 @@
     r_ref, g_ref, m_ref, rate_ref, t_ref = refs
     core = core_ref[0]
     write_received(core, swapped_ref, near_ref, far_ref, shared_ref, r_ref)
-    at = received_column(core, face_ref[...])
-    columns = [at[face : face + 1, :] for face in range(6)]
-    columns.append(received_column(core, mortar_row(mortar_ref)))
-    spread = jnp.concatenate([one_hot(1536, column) for column in columns], axis=1)
-    gathered = part_ref[...] + picked(r_ref[...], spread)
-    exterior(core, gathered, code_ref, mortar_code_ref, target_ref, g_ref, m_ref)
+    gathered = part_ref[...] + picked(r_ref[...], spread_ref[...])
+    exterior(gathered, codes_ref, place_ref, g_ref, m_ref)
     rate_ref[...] = rate_in_ref[...]
     add_lift(rate_ref, g_ref)
-    metric = jnp.where(
-        refinement_ref[...] == 0, 1.0, jnp.where(refinement_ref[...] == 1, 2.0, 4.0)
-    )
     for half in range(2):
         rows = slice(192 * half, 192 * half + 192)
-        scale = STEP_SIZE * metric * material_ref[half : half + 1, :]
-        register = scale * rate_ref[rows, :]
+        register = scale_ref[half : half + 1, :] * rate_ref[rows, :]
         if section:
             register = register + SECTION_A[section] * register_ref[rows, :]
         new_register_ref[rows, :] = register
         new_u_ref[rows, :] = u_ref[rows, :] + SECTION_B[section] * register
     if section == 0:
         write_table(new_u_ref, t_ref)
-        write_lists(core, t_ref, send_ref, swap_ref, own_ref)
-
-
-def vmem(count):
-    return [pl.BlockSpec(memory_space=pltpu.VMEM)] * count
-
-
-def floats(rows, columns=LANES):
-    return jax.ShapeDtypeStruct((rows, columns), jnp.float32)
+        write_lists(t_ref, list_spread_ref[...], swap_ref, own_ref)
+
+
+def shaped(rows, columns=LANES, dtype=jnp.float32):
+    return jax.ShapeDtypeStruct((rows, columns), dtype)
 
 
 def called(kernel, core, operands, outputs, scratch):
@@ -415,15 +429,15 @@
     given = list(operands) if core is None else [core, *operands]
     return pl.pallas_call(
         kernel,
-        in_specs=first + vmem(len(operands)),
-        out_specs=vmem(len(outputs)),
+        in_specs=first + [pl.BlockSpec(memory_space=pltpu.VMEM)] * len(operands),
+        out_specs=[pl.BlockSpec(memory_space=pltpu.VMEM)] * len(outputs),
         out_shape=outputs,
         scratch_shapes=[pltpu.VMEM(shape, jnp.float32) for shape in scratch],
         compiler_params=pltpu.CompilerParams(vmem_limit_bytes=VMEM_LIMIT),
     )(*given)
 
 
-LIST_OUTPUTS = [floats(5 * UNIT), floats(3 * UNIT)]
+LIST_OUTPUTS = [shaped(5 * UNIT), shaped(3 * UNIT)]
 
 
 def exchanged(core, swap, own):
@@ -464,23 +478,56 @@
     refinement = refinement.reshape(1, LANES)
     target = mortar_target.reshape(1, 64)
     table = (96, 768)
-    swap, own = called(lists_kernel, core_at, [solution, send_face], LIST_OUTPUTS, [table])
+    swap, own = called(
+        lists_kernel,
+        core_at,
+        [solution, send_face],
+        LIST_OUTPUTS,
+        [table],
+    )
     register = None
     for section in range(2):
         received = exchanged(core, swap, own)
-        rate, part = called(
-            local_kernel,
-            None,
-            [solution, volume, face_source, mortar_source],
-            [floats(384), floats(96, 1024)],
-            [table],
-        )
+        if section == 0:
+            rate, part, list_spread_made, *made = called(
+                first_kernel,
+                core_at,
+                [
+                    solution,
+                    volume,
+                    face_source,
+                    mortar_source,
+                    face_code,
+                    mortar_code,
+                    target,
+                    material,
+                    refinement,
+                    send_face,
+                ],
+                [
+                    shaped(384),
+                    shaped(96, 1024),
+                    shaped(768, 1536, jnp.bfloat16),
+                    shaped(1536, 1024, jnp.bfloat16),
+                    shaped(768, 256, jnp.bfloat16),
+                    shaped(16, LANES, jnp.int32),
+                    shaped(2, LANES),
+                ],
+                [table],
+            )
+        else:
+            rate, part = called(
+                local_part,
+                None,
+                [solution, volume, face_source, mortar_source],
+                [shaped(384), shaped(96, 1024)],
+                [table],
+            )
         operands = [solution] + ([register] if section else [])
-        operands += [rate, part, *received, material, refinement]
-        operands += [face_source, face_code, mortar_source, mortar_code, target]
-        outputs = [floats(384), floats(384)]
+        operands += [rate, part, *received, *made]
+        outputs = [shaped(384), shaped(384)]
         if section == 0:
-            operands.append(send_face)
+            operands.append(list_spread_made)
             outputs = outputs + LIST_OUTPUTS
 
         def kernel(*refs, section=section):

time: 59.1 us -> 58 us (0.981)
  waiting for transfers between devices: 10.3 us -> 7.42 us
  Pallas kernels: 6.21 us -> 8.28 us
  blocking collectives: 12.6 us -> 13.6 us
  local copies, waits for them, and re-layouts: 2.47 us -> 1.86 us
    ppermute x2, waiting for transfers between devices: 10.3 us -> 7.41 us  [exchanged(): far = lax.ppermute(far, 'sfc', ahead(2))]
    pallas_call x5, Pallas kernels: 6.21 us -> 8.28 us  [called(): pl.pallas_call(kernel, in_specs=first + [pl.BlockSpec(memory_space=pltpu....]
    all_gather x2, blocking collectives: 7.62 us -> 8.62 us  [exchanged(): shared = lax.all_gather(shared, 'sfc', axis_index_groups=pairs, tiled=True)]
    unnamed x22 -> x24, local copies, waits for them, and re-layouts: 2.35 us -> 1.74 us
  transfers between devices with their start and end apart: 4 -> 4, of which waited for: 2 -> 2; matrix products, arithmetic and copies ran while one was open for 0% -> 0% of each run, Pallas kernels for 2% -> 6%
where the time goes in v2:
time: 58 us; the launch traced here: 57.7 us
  starting transfers between devices  25.5 us (44%)
  blocking collectives  13.6 us (23%)
  Pallas kernels  8.28 us (14%)
  waiting for transfers between devices  7.42 us (13%)
  local copies, waits for them, and re-layouts  1.86 us (3%)
  between operations  0.96 us (2%)
    ppermute x2, starting transfers between devices, exchanged(): near = lax.ppermute(near, 'sfc', ahead(1))  20.5 us
    all_gather x2, blocking collectives, exchanged(): shared = lax.all_gather(shared, 'sfc', axis_index_groups=pairs, tiled=True)  8.62 us
    pallas_call x5, Pallas kernels, called(): pl.pallas_call(kernel, in_specs=first + [pl.BlockSpec(memory_space=pltpu....  8.28 us
    ppermute x2, waiting for transfers between devices, exchanged(): far = lax.ppermute(far, 'sfc', ahead(2))  7.41 us
    ppermute x2, starting transfers between devices, exchanged(): far = lax.ppermute(far, 'sfc', ahead(2))  5.01 us
    all_gather x2, blocking collectives, exchanged(): swapped = lax.all_gather(swap, 'sfc', axis_index_groups=pairs, tiled=True)  4.98 us
    unnamed x24, local copies, waits for them, and re-layouts  1.74 us
  transfers between devices with their start and end apart: 4, of which 2 were waited for; matrix products, arithmetic and copies ran while one was open for 0% of the time, Pallas kernels for 6%

profile of v2, /device:TPU:7, one launch (start us, length us, event | category | flops | bytes accessed | tf_op | source)
XLA Modules:
  0.0 57.7 jit_solution(10604319370437511428)
XLA Ops:
  0.6 0.0 copy-start
  0.7 0.0 copy-start.1
  0.7 1.0 %copy-done.1 = f32[6,64,128]{2,1,0:T(8,128)S(1)} copy-done((f32[6,64,128]{2,1,0:T(8,128)S(1)}, f32[6,64,128]{2,1,0:T(8,128)}, u32[]{:S(2)}) %copy-start.1) | copy-done | bytes 196632
  1.7 0.0 copy-start.3
  1.7 0.7 %copy-done.3 = s32[8,192]{1,0:T(8,128)S(1)} copy-done((s32[8,192]{1,0:T(8,128)S(1)}, s32[8,192]{1,0:T(8,128)}, u32[]{:S(2)}) %copy-start.3) | copy-done | bytes 6168
  2.4 0.0 copy-start.2
  2.4 0.0 copy-start.4
  2.4 0.0 copy-start.5
  2.4 0.0 copy-start.6
  2.4 0.0 copy-start.7
  2.4 0.0 copy-start.8
  2.4 0.0 copy-start.9
  2.4 0.0 copy-start.10
  2.4 0.0 copy-start.11
  2.4 0.8 %shard_map.114 = (f32[720,128]{1,0:T(8,128)S(1)}, f32[432,128]{1,0:T(8,128)S(1)}) custom-call(s32[1]{0:T(128)} %bitcast.core_ref.refs_0_, f32[384,128]{1,0:T(8,128)S(1)} %bitcast.6, s32[8,192]{1,0:T(8,128)S(1)} %copy-done.3), custom_call_target="tpu_custom_call" | custom-call | tf_op jit(solution)/shard_map/pallas_call | solution.py:430
  3.2 2.6 %all_gather.12.refs_4_ = f32[1440,128]{1,0:T(8,128)S(1)} all-gather(f32[720,128]{1,0:T(8,128)S(1)} %get-tuple-element.21), channel_id=1, replica_groups={{0,1},{2,3},{4,5},{6,7},{8,9},{10,11},{12,13},{14,15},{16,17},{18,19},{..., dimensions={0}, use_global_device_ids=true | all-gather | bytes 1105920 | tf_op jit(solution)/shard_map/all_gather | solution.py:451
  5.9 13.8 %collective-permute-start = (f32[576,128]{1,0:T(8,128)S(1)}, f32[576,128]{1,0:T(8,128)S(1)}, u32[]{:S(2)}, u32[]{:S(2)}) collective-permute-start(f32[576,128]{1,0:T(8,128)S(1)} %pad_maximum_fusion), channel_id=1, source_target_pairs={{0,2},{2,4},{3,1},{4,6},{5,3},{6,8},{7,5},{8,10},{9,7},{10,12},{11... | collective-permute-start | bytes 884744 | tf_op jit(solution)/shard_map/ppermute | solution.py:456
  19.8 3.1 %collective-permute-start.1 = (f32[432,128]{1,0:T(8,128)S(1)}, f32[432,128]{1,0:T(8,128)S(1)}, u32[]{:S(2)}, u32[]{:S(2)}) collective-permute-start(f32[432,128]{1,0:T(8,128)S(1)} %pad_maximum_fusion.2), channel_id=1, source_target_pairs={{0,4},{2,6},{4,8},{5,1},{6,10},{7,3},{8,12},{9,5},{10,14},{11,7},{... | collective-permute-start | bytes 663560 | tf_op jit(solution)/shard_map/ppermute | solution.py:457
  22.9 0.0 copy-done
  22.9 0.0 copy-done.2
  22.9 0.0 copy-done.4
  22.9 0.0 copy-done.5
  22.9 0.0 copy-done.6
  22.9 0.0 copy-done.7
  23.0 0.0 copy-done.8
  23.0 0.0 copy-done.9
  23.0 0.0 copy-done.10
  23.0 0.0 copy-done.11
  23.0 3.0 %shard_map.113 = (f32[384,128]{1,0:T(8,128)S(1)}, f32[96,1024]{1,0:T(8,128)S(1)}, bf16[768,1536]{1,0:T(8,128)(2,1)S(1)}, bf16[1536,1024]{1,0:T(8,128)(2,1)S(1)},...) custom-call(s32[1]{0:T(128)} %bitcast.core_ref.refs_0_, f32[384,128]{1,0:T(8,128)S(1)} %bitcast.7, ...), custom_call_target="tpu_custom_call" | custom-call | tf_op jit(solution)/shard_map/pallas_call | solution.py:430
  26.0 1.7 %collective-permute-done.1.refs_6_ = f32[432,128]{1,0:T(8,128)S(1)} collective-permute-done((f32[432,128]{1,0:T(8,128)S(1)}, f32[432,128]{1,0:T(8,128)S(1)}, u32[]{:S(2)}, u32[]{:S(2)}) %collective-permute-start.1) | collective-permute-done | bytes 221216 | tf_op jit(solution)/shard_map/ppermute | solution.py:457
  27.7 0.0 collective-permute-done.refs_5_
  27.8 4.4 %all_gather.13.refs_7_ = f32[864,128]{1,0:T(8,128)S(1)} all-gather(f32[432,128]{1,0:T(8,128)S(1)} %pad_maximum_fusion.3), channel_id=1, replica_groups={{0,1},{2,3},{4,5},{6,7},{8,9},{10,11},{12,13},{14,15},{16,17},{18,19},{..., dimensions={0}, use_global_device_ids=true | all-gather | bytes 663552 | tf_op jit(solution)/shard_map/all_gather | solution.py:459
  32.1 1.9 %shard_map.115 = (f32[384,128]{1,0:T(8,128)S(1)}, f32[384,128]{1,0:T(8,128)S(1)}, f32[720,128]{1,0:T(8,128)S(1)}, f32[432,128]{1,0:T(8,128)S(1)}) custom-call(s32[1]{0:T(128)} %bitcast.core_ref.refs_0_, f32[384,128]{1,0:T(8,128)S(1)} %bitcast.8, f32[384,128]{1,0:T(8,128)S(1)} %get-tuple-element.19.refs_2_, f32[96,1024]{1,0:T(8,128)S(1)} %get-tuple-element.20.refs_3_, ...), custom_call_target="tpu_custom_call" | custom-call | tf_op jit(solution)/shard_map/pallas_call | solution.py:430
  34.0 2.3 %all_gather.14.refs_5_ = f32[1440,128]{1,0:T(8,128)S(1)} all-gather(f32[720,128]{1,0:T(8,128)S(1)} %get-tuple-element.32), channel_id=1, replica_groups={{0,1},{2,3},{4,5},{6,7},{8,9},{10,11},{12,13},{14,15},{16,17},{18,19},{..., dimensions={0}, use_global_device_ids=true | all-gather | bytes 1105920 | tf_op jit(solution)/shard_map/all_gather | solution.py:451
  36.5 6.6 %collective-permute-start.2 = (f32[576,128]{1,0:T(8,128)S(1)}, f32[576,128]{1,0:T(8,128)S(1)}, u32[]{:S(2)}, u32[]{:S(2)}) collective-permute-start(f32[576,128]{1,0:T(8,128)S(1)} %pad_maximum_fusion.1), channel_id=1, source_target_pairs={{0,2},{2,4},{3,1},{4,6},{5,3},{6,8},{7,5},{8,10},{9,7},{10,12},{11... | collective-permute-start | bytes 884744 | tf_op jit(solution)/shard_map/ppermute | solution.py:456
  43.1 1.9 %collective-permute-start.3 = (f32[432,128]{1,0:T(8,128)S(1)}, f32[432,128]{1,0:T(8,128)S(1)}, u32[]{:S(2)}, u32[]{:S(2)}) collective-permute-start(f32[432,128]{1,0:T(8,128)S(1)} %pad_maximum_fusion.4), channel_id=1, source_target_pairs={{0,4},{2,6},{4,8},{5,1},{6,10},{7,3},{8,12},{9,5},{10,14},{11,7},{... | collective-permute-start | bytes 663560 | tf_op jit(solution)/shard_map/ppermute | solution.py:457
  45.1 0.7 %shard_map.116 = (f32[384,128]{1,0:T(8,128)S(1)}, f32[96,1024]{1,0:T(8,128)S(1)}) custom-call(f32[384,128]{1,0:T(8,128)S(1)} %get-tuple-element.28.u_ref.refs_1_, bf16[384,1152]{1,0:T(8,128)(2,1)S(1)} %copy-done, s32[6,128]{1,0:T(8,128)S(1)} %copy-done.5, s32[4,64]{1,0:T(4,128)S(1)} %copy-done.6), custom_call_target="tpu_custom_call" | custom-call | tf_op jit(solution)/shard_map/pallas_call | solution.py:430
  45.8 5.7 %collective-permute-done.3.refs_7_ = f32[432,128]{1,0:T(8,128)S(1)} collective-permute-done((f32[432,128]{1,0:T(8,128)S(1)}, f32[432,128]{1,0:T(8,128)S(1)}, u32[]{:S(2)}, u32[]{:S(2)}) %collective-permute-start.3) | collective-permute-done | bytes 221216 | tf_op jit(solution)/shard_map/ppermute | solution.py:457
  51.5 0.0 collective-permute-done.2.refs_6_
  51.5 4.3 %all_gather.15.refs_8_ = f32[864,128]{1,0:T(8,128)S(1)} all-gather(f32[432,128]{1,0:T(8,128)S(1)} %pad_maximum_fusion.5), channel_id=1, replica_groups={{0,1},{2,3},{4,5},{6,7},{8,9},{10,11},{12,13},{14,15},{16,17},{18,19},{..., dimensions={0}, use_global_device_ids=true | all-gather | bytes 663552 | tf_op jit(solution)/shard_map/all_gather | solution.py:459
  55.8 1.9 %shard_map.117 = (f32[384,128]{1,0:T(8,128)}, f32[384,128]{1,0:T(8,128)}) custom-call(s32[1]{0:T(128)} %bitcast.core_ref.refs_0_, f32[384,128]{1,0:T(8,128)S(1)} %get-tuple-element.28.u_ref.refs_1_, f32[384,128]{1,0:T(8,128)S(1)} %get-tuple-element.29.refs_2_, f32[384,128]{1,0:T(8,128)S(1)} %get-tuple-element.30.refs_3_, ...), custom_call_target="tpu_custom_call" | custom-call | tf_op jit(solution)/shard_map/pallas_call | solution.py:430
  (16 shorter events, 0.2 us)
Async XLA Ops:
  0.6 22.3 %copy-start = (bf16[384,1152]{1,0:T(8,128)(2,1)S(1)}, bf16[384,1152]{1,0:T(8,128)(2,1)}, u32[]{:S(2)}) copy-start(bf16[384,1152]{1,0:T(8,128)(2,1)} %constant.17.clone.volume_ref) | copy-start | bytes 2654212
  0.7 1.0 %copy-start.1 = (f32[6,64,128]{2,1,0:T(8,128)S(1)}, f32[6,64,128]{2,1,0:T(8,128)}, u32[]{:S(2)}) copy-start(f32[6,64,128]{2,1,0:T(8,128)} %param.10) | copy-start | bytes 589828
  1.7 0.7 %copy-start.3 = (s32[8,192]{1,0:T(8,128)S(1)}, s32[8,192]{1,0:T(8,128)}, u32[]{:S(2)}) copy-start(s32[8,192]{1,0:T(8,128)} %send_ref.3) | copy-start | bytes 18436
  2.4 20.6 %copy-start.2 = (f32[6,64,128]{2,1,0:T(8,128)S(1)}, f32[6,64,128]{2,1,0:T(8,128)}, u32[]{:S(2)}) copy-start(f32[6,64,128]{2,1,0:T(8,128)} %param.10) | copy-start | bytes 589828
  2.4 20.6 %copy-start.4 = (s32[8,192]{1,0:T(8,128)S(1)}, s32[8,192]{1,0:T(8,128)}, u32[]{:S(2)}) copy-start(s32[8,192]{1,0:T(8,128)} %send_ref.3) | copy-start | bytes 18436
  2.4 20.6 %copy-start.5 = (s32[6,128]{1,0:T(8,128)S(1)}, s32[6,128]{1,0:T(8,128)}, u32[]{:S(2)}) copy-start(s32[6,128]{1,0:T(8,128)} %face_ref.3) | copy-start | bytes 9220
  2.4 20.6 %copy-start.6 = (s32[4,64]{1,0:T(4,128)S(1)}, s32[4,64]{1,0:T(4,128)}, u32[]{:S(2)}) copy-start(s32[4,64]{1,0:T(4,128)} %mortar_ref.3) | copy-start | bytes 3076
  2.4 20.6 %copy-start.7 = (s32[6,128]{1,0:T(8,128)S(1)}, s32[6,128]{1,0:T(8,128)}, u32[]{:S(2)}) copy-start(s32[6,128]{1,0:T(8,128)} %code_ref.1) | copy-start | bytes 9220
  2.4 20.6 %copy-start.8 = (s32[4,64]{1,0:T(4,128)S(1)}, s32[4,64]{1,0:T(4,128)}, u32[]{:S(2)}) copy-start(s32[4,64]{1,0:T(4,128)} %mortar_code_ref.1) | copy-start | bytes 3076
  2.4 20.6 %copy-start.9 = (f32[2,128]{1,0:T(2,128)S(1)}, f32[2,128]{1,0:T(2,128)}, u32[]{:S(2)}) copy-start(f32[2,128]{1,0:T(2,128)} %material_ref.1) | copy-start | bytes 3076
  2.4 20.6 %copy-start.10 = (s32[64]{0:T(128)S(1)}, s32[64]{0:T(128)}, u32[]{:S(2)}) copy-start(s32[64]{0:T(128)} %param.18) | copy-start | bytes 772
  2.4 20.6 %copy-start.11 = (s32[128]{0:T(128)S(1)}, s32[128]{0:T(128)}, u32[]{:S(2)}) copy-start(s32[128]{0:T(128)} %param.12) | copy-start | bytes 1540
  5.9 21.8 %collective-permute-start = (f32[576,128]{1,0:T(8,128)S(1)}, f32[576,128]{1,0:T(8,128)S(1)}, u32[]{:S(2)}, u32[]{:S(2)}) collective-permute-start(f32[576,128]{1,0:T(8,128)S(1)} %pad_maximum_fusion), channel_id=1, source_target_pairs={{0,2},{2,4},{3,1},{4,6},{5,3},{6,8},{7,5},{8,10},{9,7},{10,12},{11... | collective-permute-start | bytes 884744 | tf_op jit(solution)/shard_map/ppermute | solution.py:456
  19.8 7.9 %collective-permute-start.1 = (f32[432,128]{1,0:T(8,128)S(1)}, f32[432,128]{1,0:T(8,128)S(1)}, u32[]{:S(2)}, u32[]{:S(2)}) collective-permute-start(f32[432,128]{1,0:T(8,128)S(1)} %pad_maximum_fusion.2), channel_id=1, source_target_pairs={{0,4},{2,6},{4,8},{5,1},{6,10},{7,3},{8,12},{9,5},{10,14},{11,7},{... | collective-permute-start | bytes 663560 | tf_op jit(solution)/shard_map/ppermute | solution.py:457
  36.5 15.0 %collective-permute-start.2 = (f32[576,128]{1,0:T(8,128)S(1)}, f32[576,128]{1,0:T(8,128)S(1)}, u32[]{:S(2)}, u32[]{:S(2)}) collective-permute-start(f32[576,128]{1,0:T(8,128)S(1)} %pad_maximum_fusion.1), channel_id=1, source_target_pairs={{0,2},{2,4},{3,1},{4,6},{5,3},{6,8},{7,5},{8,10},{9,7},{10,12},{11... | collective-permute-start | bytes 884744 | tf_op jit(solution)/shard_map/ppermute | solution.py:456
  43.1 8.3 %collective-permute-start.3 = (f32[432,128]{1,0:T(8,128)S(1)}, f32[432,128]{1,0:T(8,128)S(1)}, u32[]{:S(2)}, u32[]{:S(2)}) collective-permute-start(f32[432,128]{1,0:T(8,128)S(1)} %pad_maximum_fusion.4), channel_id=1, source_target_pairs={{0,4},{2,6},{4,8},{5,1},{6,10},{7,3},{8,12},{9,5},{10,14},{11,7},{... | collective-permute-start | bytes 663560 | tf_op jit(solution)/shard_map/ppermute | solution.py:457

commit v3 on v2

--- a/solution.py
+++ b/solution.py
@@ -139,12 +139,13 @@
     return jnp.concatenate([one_hot(768, column) for column in columns], axis=1)
 
 
-def write_lists(t_ref, spread, swap_ref, own_ref):
+def write_lists(t_ref, spread, swap_ref, *own_refs):
     out = picked(t_ref[...], spread)
     first = lax.broadcasted_iota(jnp.int32, (48, LANES), 1) < 64
-    places = {4 - d: (swap_ref, d - 1) for d in range(1, 5)}
-    places[4] = (swap_ref, 4)
-    places.update({3 + d: (own_ref, d - 2) for d in range(2, 5)})
+    places = {4 - d: (swap_ref, d - 1) for d in range(1, 4)}
+    places[4] = (swap_ref, 3)
+    places.update({3 + d: (own_refs[d - 2], 0) for d in range(2, 5)})
+    places[0] = (own_refs[3], 0)
     for k in range(8):
         ref, place = places[k]
         ref[UNIT * place : UNIT * place + 96, :] = out[:, 128 * k : 128 * k + 128]
@@ -157,9 +158,10 @@
         ref[UNIT * place + 96 : UNIT * place + UNIT, :] = packed
 
 
-def lists_kernel(core_ref, u_ref, send_ref, swap_ref, own_ref, t_ref):
+def lists_kernel(core_ref, u_ref, send_ref, *refs):
+    t_ref = refs[-1]
     write_table(u_ref, t_ref)
-    write_lists(t_ref, list_spread(core_ref[0], send_ref), swap_ref, own_ref)
+    write_lists(t_ref, list_spread(core_ref[0], send_ref), *refs[:-1])
 
 
 def mortar_row(ref):
@@ -223,12 +225,12 @@
     scale_ref[...] = STEP_SIZE * metric * material_ref[...]
 
 
-def write_received(core, swapped_ref, near_ref, far_ref, shared_ref, r_ref):
+def write_received(core, swapped_ref, near_ref, far_ref, across_ref, shared_ref, r_ref):
     other = 1 - core
-    swapped = pl.multiple_of(other * (5 * UNIT) + 4 * UNIT, 8)
-    shared = [pl.multiple_of(other * (3 * UNIT) + UNIT * place, 8) for place in range(3)]
+    swapped = pl.multiple_of(other * (4 * UNIT) + 3 * UNIT, 8)
+    shared = [pl.multiple_of(other * (2 * UNIT) + UNIT * place, 8) for place in range(2)]
     sources = [
-        (shared_ref, shared[2]),
+        (across_ref, 0),
         (shared_ref, shared[0]),
         (shared_ref, shared[1]),
         (swapped_ref, swapped),
@@ -392,18 +394,18 @@
     core_ref, u_ref = refs[0:2]
     del refs[0:2]
     register_ref = refs.pop(0) if section else None
-    rate_in_ref, part_ref, swapped_ref, near_ref, far_ref, shared_ref = refs[0:6]
-    spread_ref, place_ref, codes_ref, scale_ref = refs[6:10]
-    del refs[0:10]
+    rate_in_ref, part_ref = refs[0:2]
+    received = refs[2:7]
+    spread_ref, place_ref, codes_ref, scale_ref = refs[7:11]
+    del refs[0:11]
     list_spread_ref = None if section else refs.pop(0)
     new_u_ref, new_register_ref = refs[0:2]
     del refs[0:2]
-    if section == 0:
-        swap_ref, own_ref = refs[0:2]
-        del refs[0:2]
+    list_refs = [] if section else refs[0:5]
+    del refs[0 : len(list_refs)]
     r_ref, g_ref, m_ref, rate_ref, t_ref = refs
     core = core_ref[0]
-    write_received(core, swapped_ref, near_ref, far_ref, shared_ref, r_ref)
+    write_received(core, *received, r_ref)
     gathered = part_ref[...] + picked(r_ref[...], spread_ref[...])
     exterior(gathered, codes_ref, place_ref, g_ref, m_ref)
     rate_ref[...] = rate_in_ref[...]
@@ -417,7 +419,7 @@
         new_u_ref[rows, :] = u_ref[rows, :] + SECTION_B[section] * register
     if section == 0:
         write_table(new_u_ref, t_ref)
-        write_lists(t_ref, list_spread_ref[...], swap_ref, own_ref)
+        write_lists(t_ref, list_spread_ref[...], *list_refs)
 
 
 def shaped(rows, columns=LANES, dtype=jnp.float32):
@@ -437,10 +439,10 @@
     )(*given)
 
 
-LIST_OUTPUTS = [shaped(5 * UNIT), shaped(3 * UNIT)]
-
-
-def exchanged(core, swap, own):
+LIST_OUTPUTS = [shaped(4 * UNIT)] + [shaped(UNIT)] * 4
+
+
+def exchanged(core, swap, own_2, own_3, own_4, far_4):
     count = lax.axis_size("sfc")
     pairs = [[2 * chip, 2 * chip + 1] for chip in range(count // 2)]
 
@@ -448,16 +450,16 @@
         ends = [(i, i + 2 * chips if i % 2 == 0 else i - 2 * chips) for i in range(count)]
         return [(source, end) for source, end in ends if 0 <= end < count]
 
+    across = lax.ppermute(far_4, "sfc", ahead(-2))
     swapped = lax.all_gather(swap, "sfc", axis_index_groups=pairs, tiled=True)
-    theirs = lax.dynamic_slice_in_dim(swapped, (1 - core) * (5 * UNIT), 4 * UNIT)
+    theirs = lax.dynamic_slice_in_dim(swapped, (1 - core) * (4 * UNIT), 3 * UNIT)
     u = UNIT
-    near = jnp.concatenate([own[0:u], theirs[0:u], own[u : 2 * u], theirs[u : 2 * u]])
-    far = jnp.concatenate([own[2 * u : 3 * u], theirs[2 * u : 4 * u]])
+    near = jnp.concatenate([own_2, theirs[0:u], own_3, theirs[u : 2 * u]])
+    far = jnp.concatenate([own_4, theirs[2 * u : 3 * u]])
     near = lax.ppermute(near, "sfc", ahead(1))
     far = lax.ppermute(far, "sfc", ahead(2))
-    shared = jnp.concatenate([near[2 * u : 4 * u], far[2 * u : 3 * u]])
-    shared = lax.all_gather(shared, "sfc", axis_index_groups=pairs, tiled=True)
-    return swapped, near, far, shared
+    shared = lax.all_gather(near[2 * u : 4 * u], "sfc", axis_index_groups=pairs, tiled=True)
+    return swapped, near, far, across, shared
 
 
 def local(
@@ -478,7 +480,7 @@
     refinement = refinement.reshape(1, LANES)
     target = mortar_target.reshape(1, 64)
     table = (96, 768)
-    swap, own = called(
+    lists = called(
         lists_kernel,
         core_at,
         [solution, send_face],
@@ -487,7 +489,7 @@
     )
     register = None
     for section in range(2):
-        received = exchanged(core, swap, own)
+        received = exchanged(core, *lists)
         if section == 0:
             rate, part, list_spread_made, *made = called(
                 first_kernel,
@@ -542,7 +544,7 @@
         )
         solution, register = results[0:2]
         if section == 0:
-            swap, own = results[2:4]
+            lists = results[2:7]
     return (solution.reshape(6, 64, LANES), register.reshape(6, 64, LANES))
 
 

time: 58 us -> 63.9 us (1.10)
  starting transfers between devices: 25.5 us -> 33.1 us
  local copies, waits for them, and re-layouts: 1.86 us -> 8.27 us
  blocking collectives: 13.6 us -> 8.79 us
  waiting for transfers between devices: 7.42 us -> 3.67 us
    ppermute x2, waiting for transfers between devices: 7.41 us -> 0.01 us  [exchanged(): far = lax.ppermute(far, 'sfc', ahead(2))]
    ppermute x0 -> x2, starting transfers between devices: none -> 6.94 us  [exchanged(): across = lax.ppermute(far_4, 'sfc', ahead(-2))]
    unnamed x24 -> x28, local copies, waits for them, and re-layouts: 1.74 us -> 8.21 us
    all_gather x2, blocking collectives: 8.62 us -> 4.03 us  [exchanged(): lax.all_gather(near[2 * u:4 * u], 'sfc', axis_index_groups=pairs, tiled=T...]
    ppermute x0 -> x2, waiting for transfers between devices: none -> 3.66 us  [exchanged(): across = lax.ppermute(far_4, 'sfc', ahead(-2))]
  transfers between devices with their start and end apart: 4 -> 6, of which waited for: 2 -> 1; matrix products, arithmetic and copies ran while one was open for 0% -> 0% of each run, Pallas kernels for 6% -> 6%
where the time goes in v3:
time: 63.9 us; the launch traced here: 63 us
  starting transfers between devices  33.1 us (52%)
  blocking collectives  8.79 us (14%)
  Pallas kernels  8.29 us (13%)
  local copies, waits for them, and re-layouts  8.27 us (13%)
  waiting for transfers between devices  3.67 us (6%)
  between operations  0.86 us (1%)
    ppermute x2, starting transfers between devices, exchanged(): near = lax.ppermute(near, 'sfc', ahead(1))  20.7 us
    pallas_call x5, Pallas kernels, called(): pl.pallas_call(kernel, in_specs=first + [pl.BlockSpec(memory_space=pltpu....  8.29 us
    unnamed x28, local copies, waits for them, and re-layouts  8.21 us
    ppermute x2, starting transfers between devices, exchanged(): across = lax.ppermute(far_4, 'sfc', ahead(-2))  6.94 us
    ppermute x2, starting transfers between devices, exchanged(): far = lax.ppermute(far, 'sfc', ahead(2))  5.43 us
    all_gather x2, blocking collectives, exchanged(): swapped = lax.all_gather(swap, 'sfc', axis_index_groups=pairs, tiled=True)  4.76 us
    all_gather x2, blocking collectives, exchanged(): lax.all_gather(near[2 * u:4 * u], 'sfc', axis_index_groups=pairs, tiled=T...  4.03 us
    ppermute x2, waiting for transfers between devices, exchanged(): across = lax.ppermute(far_4, 'sfc', ahead(-2))  3.66 us
  transfers between devices with their start and end apart: 6, of which 1 were waited for; matrix products, arithmetic and copies ran while one was open for 0% of the time, Pallas kernels for 6%

profile of v3, /device:TPU:7, one launch (start us, length us, event | category | flops | bytes accessed | tf_op | source)
XLA Modules:
  0.0 63.0 jit_solution(2050861241967135781)
XLA Ops:
  0.6 0.0 copy-start.2
  0.6 0.9 %copy-done.2 = f32[6,64,128]{2,1,0:T(8,128)S(1)} copy-done((f32[6,64,128]{2,1,0:T(8,128)S(1)}, f32[6,64,128]{2,1,0:T(8,128)}, u32[]{:S(2)}) %copy-start.2) | copy-done | bytes 196632
  1.6 0.0 copy-start.3
  1.6 0.7 %copy-done.3 = s32[8,192]{1,0:T(8,128)S(1)} copy-done((s32[8,192]{1,0:T(8,128)S(1)}, s32[8,192]{1,0:T(8,128)}, u32[]{:S(2)}) %copy-start.3) | copy-done | bytes 6168
  2.3 0.8 %shard_map.114 = (f32[576,128]{1,0:T(8,128)S(1)}, f32[144,128]{1,0:T(8,128)S(1)}, f32[144,128]{1,0:T(8,128)S(1)}, f32[144,128]{1,0:T(8,128)S(1)}, f32[144,128]{1,0:T(8,128)S(1)}) custom-call(s32[1]{0:T(128)} %bitcast.core_ref.refs_0_, f32[384,128]{1,0:T(8,128)S(1)} %bitcast.6, s32[8,192]{1,0:T(8,128)S(1)} %copy-done.3), custom_call_target="tpu_custom_call" | custom-call | tf_op jit(solution)/shard_map/pallas_call | solution.py:432
  3.0 2.5 %all_gather.12.refs_4_ = f32[1152,128]{1,0:T(8,128)S(1)} all-gather(f32[576,128]{1,0:T(8,128)S(1)} %get-tuple-element.27), channel_id=1, replica_groups={{0,1},{2,3},{4,5},{6,7},{8,9},{10,11},{12,13},{14,15},{16,17},{18,19},{..., dimensions={0}, use_global_device_ids=true | all-gather | bytes 884736 | tf_op jit(solution)/shard_map/all_gather | solution.py:454
  5.6 13.8 %collective-permute-start = (f32[576,128]{1,0:T(8,128)S(1)}, f32[576,128]{1,0:T(8,128)S(1)}, u32[]{:S(2)}, u32[]{:S(2)}) collective-permute-start(f32[576,128]{1,0:T(8,128)S(1)} %pad_maximum_fusion), channel_id=1, source_target_pairs={{0,2},{2,4},{3,1},{4,6},{5,3},{6,8},{7,5},{8,10},{9,7},{10,12},{11... | collective-permute-start | bytes 884744 | tf_op jit(solution)/shard_map/ppermute | solution.py:459
  19.5 3.1 %collective-permute-start.1 = (f32[288,128]{1,0:T(8,128)S(1)}, f32[288,128]{1,0:T(8,128)S(1)}, u32[]{:S(2)}, u32[]{:S(2)}) collective-permute-start(f32[288,128]{1,0:T(8,128)S(1)} %pad_maximum_fusion.2), channel_id=1, source_target_pairs={{0,4},{2,6},{4,8},{5,1},{6,10},{7,3},{8,12},{9,5},{10,14},{11,7},{... | collective-permute-start | bytes 442376 | tf_op jit(solution)/shard_map/ppermute | solution.py:460
  22.6 3.1 %collective-permute-start.2 = (f32[144,128]{1,0:T(8,128)S(1)}, f32[144,128]{1,0:T(8,128)S(1)}, u32[]{:S(2)}, u32[]{:S(2)}) collective-permute-start(f32[144,128]{1,0:T(8,128)S(1)} %get-tuple-element.31), channel_id=1, source_target_pairs={{1,5},{3,7},{4,0},{5,9},{6,2},{7,11},{8,4},{9,13},{10,6},{11,15},{... | collective-permute-start | bytes 221192 | tf_op jit(solution)/shard_map/ppermute | solution.py:453
  25.7 0.0 copy-start
  25.7 1.2 %copy-done = bf16[384,1152]{1,0:T(8,128)(2,1)S(1)} copy-done((bf16[384,1152]{1,0:T(8,128)(2,1)S(1)}, bf16[384,1152]{1,0:T(8,128)(2,1)}, u32[]{:S(2)}) %copy-start) | copy-done | bytes 884760
  26.9 0.0 copy-start.4
  26.9 0.7 %copy-done.4 = s32[8,192]{1,0:T(8,128)S(1)} copy-done((s32[8,192]{1,0:T(8,128)S(1)}, s32[8,192]{1,0:T(8,128)}, u32[]{:S(2)}) %copy-start.4) | copy-done | bytes 6168
  27.6 0.0 copy-start.5
  27.6 0.7 %copy-done.5 = s32[6,128]{1,0:T(8,128)S(1)} copy-done((s32[6,128]{1,0:T(8,128)S(1)}, s32[6,128]{1,0:T(8,128)}, u32[]{:S(2)}) %copy-start.5) | copy-done | bytes 3096
  28.2 0.0 copy-start.7
  28.3 0.7 %copy-done.7 = s32[4,64]{1,0:T(4,128)S(1)} copy-done((s32[4,64]{1,0:T(4,128)S(1)}, s32[4,64]{1,0:T(4,128)}, u32[]{:S(2)}) %copy-start.7) | copy-done | bytes 1048
  28.9 0.0 copy-start.9
  28.9 0.7 %copy-done.9 = s32[6,128]{1,0:T(8,128)S(1)} copy-done((s32[6,128]{1,0:T(8,128)S(1)}, s32[6,128]{1,0:T(8,128)}, u32[]{:S(2)}) %copy-start.9) | copy-done | bytes 3096
  29.6 0.0 copy-start.10
  29.6 0.7 %copy-done.10 = s32[4,64]{1,0:T(4,128)S(1)} copy-done((s32[4,64]{1,0:T(4,128)S(1)}, s32[4,64]{1,0:T(4,128)}, u32[]{:S(2)}) %copy-start.10) | copy-done | bytes 1048
  30.3 0.0 copy-start.11
  30.3 0.7 %copy-done.11 = f32[2,128]{1,0:T(2,128)S(1)} copy-done((f32[2,128]{1,0:T(2,128)S(1)}, f32[2,128]{1,0:T(2,128)}, u32[]{:S(2)}) %copy-start.11) | copy-done | bytes 1048
  31.0 0.0 copy-start.12
  31.0 0.7 %copy-done.12 = s32[64]{0:T(128)S(1)} copy-done((s32[64]{0:T(128)S(1)}, s32[64]{0:T(128)}, u32[]{:S(2)}) %copy-start.12) | copy-done | bytes 280
  31.6 0.0 copy-start.13
  31.6 0.7 %copy-done.13 = s32[128]{0:T(128)S(1)} copy-done((s32[128]{0:T(128)S(1)}, s32[128]{0:T(128)}, u32[]{:S(2)}) %copy-start.13) | copy-done | bytes 536
  32.3 3.0 %shard_map.113 = (f32[384,128]{1,0:T(8,128)S(1)}, f32[96,1024]{1,0:T(8,128)S(1)}, bf16[768,1536]{1,0:T(8,128)(2,1)S(1)}, bf16[1536,1024]{1,0:T(8,128)(2,1)S(1)},...) custom-call(s32[1]{0:T(128)} %bitcast.core_ref.refs_0_, f32[384,128]{1,0:T(8,128)S(1)} %bitcast.7, ...), custom_call_target="tpu_custom_call" | custom-call | tf_op jit(solution)/shard_map/pallas_call | solution.py:432
  35.3 0.0 collective-permute-done.refs_5_
  35.3 2.0 %all_gather.13.refs_8_ = f32[576,128]{1,0:T(8,128)S(1)} all-gather(f32[288,128]{1,0:T(8,128)S(1)} %slice.32), channel_id=1, replica_groups={{0,1},{2,3},{4,5},{6,7},{8,9},{10,11},{12,13},{14,15},{16,17},{18,19},{..., dimensions={0}, use_global_device_ids=true | all-gather | bytes 442368 | tf_op jit(solution)/shard_map/all_gather | solution.py:461
  37.4 0.0 collective-permute-done.2.refs_7_
  37.4 0.0 collective-permute-done.1.refs_6_
  37.4 0.0 copy-start.1
  37.4 0.0 copy-start.6
  37.4 0.0 copy-start.8
  37.4 1.9 %shard_map.115 = (f32[384,128]{1,0:T(8,128)S(1)}, f32[384,128]{1,0:T(8,128)S(1)}, f32[576,128]{1,0:T(8,128)S(1)}, f32[144,128]{1,0:T(8,128)S(1)}, f32[144,128]{1...) custom-call(s32[1]{0:T(128)} %bitcast.core_ref.refs_0_, f32[384,128]{1,0:T(8,128)S(1)} %bitcast.8, ...), custom_call_target="tpu_custom_call" | custom-call | tf_op jit(solution)/shard_map/pallas_call | solution.py:432
  39.3 2.2 %all_gather.14.refs_5_ = f32[1152,128]{1,0:T(8,128)S(1)} all-gather(f32[576,128]{1,0:T(8,128)S(1)} %get-tuple-element.41), channel_id=1, replica_groups={{0,1},{2,3},{4,5},{6,7},{8,9},{10,11},{12,13},{14,15},{16,17},{18,19},{..., dimensions={0}, use_global_device_ids=true | all-gather | bytes 884736 | tf_op jit(solution)/shard_map/all_gather | solution.py:454
  41.6 6.9 %collective-permute-start.3 = (f32[576,128]{1,0:T(8,128)S(1)}, f32[576,128]{1,0:T(8,128)S(1)}, u32[]{:S(2)}, u32[]{:S(2)}) collective-permute-start(f32[576,128]{1,0:T(8,128)S(1)} %pad_maximum_fusion.1), channel_id=1, source_target_pairs={{0,2},{2,4},{3,1},{4,6},{5,3},{6,8},{7,5},{8,10},{9,7},{10,12},{11... | collective-permute-start | bytes 884744 | tf_op jit(solution)/shard_map/ppermute | solution.py:459
  48.4 2.4 %collective-permute-start.4 = (f32[288,128]{1,0:T(8,128)S(1)}, f32[288,128]{1,0:T(8,128)S(1)}, u32[]{:S(2)}, u32[]{:S(2)}) collective-permute-start(f32[288,128]{1,0:T(8,128)S(1)} %pad_maximum_fusion.3), channel_id=1, source_target_pairs={{0,4},{2,6},{4,8},{5,1},{6,10},{7,3},{8,12},{9,5},{10,14},{11,7},{... | collective-permute-start | bytes 442376 | tf_op jit(solution)/shard_map/ppermute | solution.py:460
  50.8 3.8 %collective-permute-start.5 = (f32[144,128]{1,0:T(8,128)S(1)}, f32[144,128]{1,0:T(8,128)S(1)}, u32[]{:S(2)}, u32[]{:S(2)}) collective-permute-start(f32[144,128]{1,0:T(8,128)S(1)} %get-tuple-element.45), channel_id=1, source_target_pairs={{1,5},{3,7},{4,0},{5,9},{6,2},{7,11},{8,4},{9,13},{10,6},{11,15},{... | collective-permute-start | bytes 221192 | tf_op jit(solution)/shard_map/ppermute | solution.py:453
  54.6 0.0 copy-done.1
  54.7 0.0 copy-done.6
  54.7 0.0 copy-done.8
  54.7 0.7 %shard_map.116 = (f32[384,128]{1,0:T(8,128)S(1)}, f32[96,1024]{1,0:T(8,128)S(1)}) custom-call(f32[384,128]{1,0:T(8,128)S(1)} %get-tuple-element.37.u_ref.refs_1_, bf16[384,1152]{1,0:T(8,128)(2,1)S(1)} %copy-done.1, s32[6,128]{1,0:T(8,128)S(1)} %copy-done.6, s32[4,64]{1,0:T(4,128)S(1)} %copy-done.8), custom_call_target="tpu_custom_call" | custom-call | tf_op jit(solution)/shard_map/pallas_call | solution.py:432
  55.4 0.0 collective-permute-done.3.refs_6_
  55.4 2.0 %all_gather.15.refs_9_ = f32[576,128]{1,0:T(8,128)S(1)} all-gather(f32[288,128]{1,0:T(8,128)S(1)} %slice.33), channel_id=1, replica_groups={{0,1},{2,3},{4,5},{6,7},{8,9},{10,11},{12,13},{14,15},{16,17},{18,19},{..., dimensions={0}, use_global_device_ids=true | all-gather | bytes 442368 | tf_op jit(solution)/shard_map/all_gather | solution.py:461
  57.4 3.7 %collective-permute-done.5.refs_8_ = f32[144,128]{1,0:T(8,128)S(1)} collective-permute-done((f32[144,128]{1,0:T(8,128)S(1)}, f32[144,128]{1,0:T(8,128)S(1)}, u32[]{:S(2)}, u32[]{:S(2)}) %collective-permute-start.5) | collective-permute-done | bytes 73760 | tf_op jit(solution)/shard_map/ppermute | solution.py:453
  61.1 0.0 collective-permute-done.4.refs_7_
  61.1 1.9 %shard_map.117 = (f32[384,128]{1,0:T(8,128)}, f32[384,128]{1,0:T(8,128)}) custom-call(s32[1]{0:T(128)} %bitcast.core_ref.refs_0_, f32[384,128]{1,0:T(8,128)S(1)} %get-tuple-element.37.u_ref.refs_1_, f32[384,128]{1,0:T(8,128)S(1)} %get-tuple-element.38.refs_2_, f32[384,128]{1,0:T(8,128)S(1)} %get-tuple-element.39.refs_3_, ...), custom_call_target="tpu_custom_call" | custom-call | tf_op jit(solution)/shard_map/pallas_call | solution.py:432
  (8 shorter events, 0.1 us)
Async XLA Ops:
  0.6 0.9 %copy-start.2 = (f32[6,64,128]{2,1,0:T(8,128)S(1)}, f32[6,64,128]{2,1,0:T(8,128)}, u32[]{:S(2)}) copy-start(f32[6,64,128]{2,1,0:T(8,128)} %param.10) | copy-start | bytes 589828
  1.6 0.7 %copy-start.3 = (s32[8,192]{1,0:T(8,128)S(1)}, s32[8,192]{1,0:T(8,128)}, u32[]{:S(2)}) copy-start(s32[8,192]{1,0:T(8,128)} %send_ref.3) | copy-start | bytes 18436
  5.6 29.7 %collective-permute-start = (f32[576,128]{1,0:T(8,128)S(1)}, f32[576,128]{1,0:T(8,128)S(1)}, u32[]{:S(2)}, u32[]{:S(2)}) collective-permute-start(f32[576,128]{1,0:T(8,128)S(1)} %pad_maximum_fusion), channel_id=1, source_target_pairs={{0,2},{2,4},{3,1},{4,6},{5,3},{6,8},{7,5},{8,10},{9,7},{10,12},{11... | collective-permute-start | bytes 884744 | tf_op jit(solution)/shard_map/ppermute | solution.py:459
  19.5 17.9 %collective-permute-start.1 = (f32[288,128]{1,0:T(8,128)S(1)}, f32[288,128]{1,0:T(8,128)S(1)}, u32[]{:S(2)}, u32[]{:S(2)}) collective-permute-start(f32[288,128]{1,0:T(8,128)S(1)} %pad_maximum_fusion.2), channel_id=1, source_target_pairs={{0,4},{2,6},{4,8},{5,1},{6,10},{7,3},{8,12},{9,5},{10,14},{11,7},{... | collective-permute-start | bytes 442376 | tf_op jit(solution)/shard_map/ppermute | solution.py:460
  22.6 14.8 %collective-permute-start.2 = (f32[144,128]{1,0:T(8,128)S(1)}, f32[144,128]{1,0:T(8,128)S(1)}, u32[]{:S(2)}, u32[]{:S(2)}) collective-permute-start(f32[144,128]{1,0:T(8,128)S(1)} %get-tuple-element.31), channel_id=1, source_target_pairs={{1,5},{3,7},{4,0},{5,9},{6,2},{7,11},{8,4},{9,13},{10,6},{11,15},{... | collective-permute-start | bytes 221192 | tf_op jit(solution)/shard_map/ppermute | solution.py:453
  25.7 1.2 %copy-start = (bf16[384,1152]{1,0:T(8,128)(2,1)S(1)}, bf16[384,1152]{1,0:T(8,128)(2,1)}, u32[]{:S(2)}) copy-start(bf16[384,1152]{1,0:T(8,128)(2,1)} %constant.17.clone.volume_ref) | copy-start | bytes 2654212
  26.9 0.7 %copy-start.4 = (s32[8,192]{1,0:T(8,128)S(1)}, s32[8,192]{1,0:T(8,128)}, u32[]{:S(2)}) copy-start(s32[8,192]{1,0:T(8,128)} %send_ref.3) | copy-start | bytes 18436
  27.6 0.7 %copy-start.5 = (s32[6,128]{1,0:T(8,128)S(1)}, s32[6,128]{1,0:T(8,128)}, u32[]{:S(2)}) copy-start(s32[6,128]{1,0:T(8,128)} %face_ref.3) | copy-start | bytes 9220
  28.2 0.7 %copy-start.7 = (s32[4,64]{1,0:T(4,128)S(1)}, s32[4,64]{1,0:T(4,128)}, u32[]{:S(2)}) copy-start(s32[4,64]{1,0:T(4,128)} %mortar_ref.3) | copy-start | bytes 3076
  28.9 0.7 %copy-start.9 = (s32[6,128]{1,0:T(8,128)S(1)}, s32[6,128]{1,0:T(8,128)}, u32[]{:S(2)}) copy-start(s32[6,128]{1,0:T(8,128)} %code_ref.1) | copy-start | bytes 9220
  29.6 0.7 %copy-start.10 = (s32[4,64]{1,0:T(4,128)S(1)}, s32[4,64]{1,0:T(4,128)}, u32[]{:S(2)}) copy-start(s32[4,64]{1,0:T(4,128)} %mortar_code_ref.1) | copy-start | bytes 3076
  30.3 0.7 %copy-start.11 = (f32[2,128]{1,0:T(2,128)S(1)}, f32[2,128]{1,0:T(2,128)}, u32[]{:S(2)}) copy-start(f32[2,128]{1,0:T(2,128)} %material_ref.1) | copy-start | bytes 3076
  31.0 0.7 %copy-start.12 = (s32[64]{0:T(128)S(1)}, s32[64]{0:T(128)}, u32[]{:S(2)}) copy-start(s32[64]{0:T(128)} %param.18) | copy-start | bytes 772
  31.6 0.7 %copy-start.13 = (s32[128]{0:T(128)S(1)}, s32[128]{0:T(128)}, u32[]{:S(2)}) copy-start(s32[128]{0:T(128)} %param.12) | copy-start | bytes 1540
  37.4 17.3 %copy-start.1 = (bf16[384,1152]{1,0:T(8,128)(2,1)S(1)}, bf16[384,1152]{1,0:T(8,128)(2,1)}, u32[]{:S(2)}) copy-start(bf16[384,1152]{1,0:T(8,128)(2,1)} %constant.17.clone.volume_ref) | copy-start | bytes 2654212
  37.4 17.3 %copy-start.6 = (s32[6,128]{1,0:T(8,128)S(1)}, s32[6,128]{1,0:T(8,128)}, u32[]{:S(2)}) copy-start(s32[6,128]{1,0:T(8,128)} %face_ref.3) | copy-start | bytes 9220
  37.4 17.3 %copy-start.8 = (s32[4,64]{1,0:T(4,128)S(1)}, s32[4,64]{1,0:T(4,128)}, u32[]{:S(2)}) copy-start(s32[4,64]{1,0:T(4,128)} %mortar_ref.3) | copy-start | bytes 3076
  41.6 13.8 %collective-permute-start.3 = (f32[576,128]{1,0:T(8,128)S(1)}, f32[576,128]{1,0:T(8,128)S(1)}, u32[]{:S(2)}, u32[]{:S(2)}) collective-permute-start(f32[576,128]{1,0:T(8,128)S(1)} %pad_maximum_fusion.1), channel_id=1, source_target_pairs={{0,2},{2,4},{3,1},{4,6},{5,3},{6,8},{7,5},{8,10},{9,7},{10,12},{11... | collective-permute-start | bytes 884744 | tf_op jit(solution)/shard_map/ppermute | solution.py:459
  48.4 12.6 %collective-permute-start.4 = (f32[288,128]{1,0:T(8,128)S(1)}, f32[288,128]{1,0:T(8,128)S(1)}, u32[]{:S(2)}, u32[]{:S(2)}) collective-permute-start(f32[288,128]{1,0:T(8,128)S(1)} %pad_maximum_fusion.3), channel_id=1, source_target_pairs={{0,4},{2,6},{4,8},{5,1},{6,10},{7,3},{8,12},{9,5},{10,14},{11,7},{... | collective-permute-start | bytes 442376 | tf_op jit(solution)/shard_map/ppermute | solution.py:460
  50.8 10.3 %collective-permute-start.5 = (f32[144,128]{1,0:T(8,128)S(1)}, f32[144,128]{1,0:T(8,128)S(1)}, u32[]{:S(2)}, u32[]{:S(2)}) collective-permute-start(f32[144,128]{1,0:T(8,128)S(1)} %get-tuple-element.45), channel_id=1, source_target_pairs={{1,5},{3,7},{4,0},{5,9},{6,2},{7,11},{8,4},{9,13},{10,6},{11,15},{... | collective-permute-start | bytes 221192 | tf_op jit(solution)/shard_map/ppermute | solution.py:453

commit v4 on v3

--- a/solution.py
+++ b/solution.py
@@ -159,16 +159,22 @@
 
 
 def lists_kernel(core_ref, u_ref, send_ref, *refs):
-    t_ref = refs[-1]
+    u_out_ref, send_out_ref, t_ref = refs[5:8]
     write_table(u_ref, t_ref)
-    write_lists(t_ref, list_spread(core_ref[0], send_ref), *refs[:-1])
-
-
-def mortar_row(ref):
-    return jnp.concatenate([ref[q : q + 1, :] for q in range(4)], axis=1)
-
-
-def local_part(u_ref, volume_ref, face_ref, mortar_ref, rate_ref, part_ref, t_ref):
+    write_lists(t_ref, list_spread(core_ref[0], send_ref), *refs[0:5])
+    u_out_ref[...] = u_ref[...]
+    send_out_ref[...] = send_ref[...]
+
+
+def mortar_row(index_ref, base):
+    return jnp.concatenate([index_ref[base + q : base + q + 1, 0:64] for q in range(4)], axis=1)
+
+
+def source_columns(index_ref):
+    return [index_ref[face : face + 1, :] for face in range(6)] + [mortar_row(index_ref, 12)]
+
+
+def local_kernel(u_ref, volume_ref, index_ref, rate_ref, part_ref, t_ref):
     high, low = halves_of(u_ref[...])
     rate_ref[...] = jnp.dot(
         volume_ref[...],
@@ -176,53 +182,9 @@
         preferred_element_type=jnp.float32,
     )
     write_table(u_ref, t_ref)
-    columns = [face_ref[face : face + 1, :] for face in range(6)] + [mortar_row(mortar_ref)]
-    spread = jnp.concatenate([one_hot(768, column) for column in columns], axis=1)
+    spread = [one_hot(768, column) for column in source_columns(index_ref)]
+    spread = jnp.concatenate(spread, axis=1)
     part_ref[...] = picked(t_ref[...], spread)
-
-
-def first_kernel(
-    core_ref,
-    u_ref,
-    volume_ref,
-    face_ref,
-    mortar_ref,
-    code_ref,
-    mortar_code_ref,
-    target_ref,
-    material_ref,
-    refinement_ref,
-    send_ref,
-    rate_ref,
-    part_ref,
-    list_spread_ref,
-    spread_ref,
-    place_ref,
-    codes_ref,
-    scale_ref,
-    t_ref,
-):
-    local_part(u_ref, volume_ref, face_ref, mortar_ref, rate_ref, part_ref, t_ref)
-    core = core_ref[0]
-    list_spread_ref[...] = list_spread(core, send_ref)
-    at = received_column(core, face_ref[...])
-    columns = [at[face : face + 1, :] for face in range(6)]
-    columns.append(received_column(core, mortar_row(mortar_ref)))
-    spread_ref[...] = jnp.concatenate([one_hot(1536, column) for column in columns], axis=1)
-    target = jnp.concatenate([target_ref[...]] * 4, axis=1)
-    place_ref[...] = one_hot(768, target)
-    face = jnp.zeros_like(target)
-    for k in range(1, 6):
-        face = face + jnp.where(target >= 128 * k, 1, 0)
-    row = lax.broadcasted_iota(jnp.int32, (4, LANES), 0)
-    codes = mortar_row(mortar_code_ref)
-    codes_ref[0:6, :] = code_ref[...]
-    codes_ref[6:8, :] = jnp.zeros((2, LANES), jnp.int32)
-    codes_ref[8:12, :] = jnp.where(row >= 2, codes[:, 128:256], codes[:, 0:128])
-    codes_ref[12:16, :] = jnp.where(row >= 2, face[:, 128:256], face[:, 0:128])
-    level = refinement_ref[...]
-    metric = jnp.where(level == 0, 1.0, jnp.where(level == 1, 2.0, 4.0))
-    scale_ref[...] = STEP_SIZE * metric * material_ref[...]
 
 
 def write_received(core, swapped_ref, near_ref, far_ref, across_ref, shared_ref, r_ref):
@@ -288,13 +250,13 @@
     ]
 
 
-def exterior(gathered, codes_ref, place_ref, g_ref, m_ref):
+def exterior(gathered, index_ref, g_ref, m_ref):
     _, halves, adjoint = gll_tables()
     for face in range(6):
         a = face // 2
         b, c = (a + 1) % 3, (a + 2) % 3
         s = 1.0 if face % 2 else -1.0
-        boundary = (codes_ref[face : face + 1, :] >> 3) == 1
+        boundary = (index_ref[6 + face : 7 + face, :] >> 3) == 1
         sign = jnp.where(boundary, -1.0, 1.0)
 
         def field(index):
@@ -302,7 +264,7 @@
 
         g_ref[16 * face : 16 * face + 16, :] = sign * field(b) + s * field(3 + c)
         g_ref[96 + 16 * face : 96 + 16 * face + 16, :] = sign * field(c) - s * field(3 + b)
-    code = codes_ref[0:6, :]
+    code = index_ref[6:12, :]
     kind = code >> 3
     quarter = kind - 2
     plain = kind < 2
@@ -326,8 +288,11 @@
             for b in range(4):
                 g_ref[pl.ds(96 * w + 4 * a + b, 6, stride=16), :] = out[a][b]
 
+    target = jnp.concatenate([index_ref[20:21, 0:64]] * 4, axis=1)
+    face = jnp.zeros_like(target[:, 0:128])
+    for k in range(1, 6):
+        face = face + jnp.where(target[:, 0:128] >= 128 * k, 1, 0)
     for half in range(2):
-        face = codes_ref[13 + half : 14 + half, :]
         axis = face >> 1
         s = jnp.where((face & 1) == 1, 1.0, -1.0)
         lanes = slice(768 + 128 * half, 896 + 128 * half)
@@ -350,14 +315,16 @@
     project_a = [[weight(lane >= 64, i, j) for j in range(4)] for i in range(4)]
     project_b = [[weight(row >= 2, i, j) for j in range(4)] for i in range(4)]
     nodes = [[m_ref[pl.ds(4 * a + b, 4, stride=16), :] for b in range(4)] for a in range(4)]
-    out = applied(turned(nodes, codes_ref[8:12, :]), project_a, project_b)
+    codes = mortar_row(index_ref, 16)
+    codes = jnp.where(row >= 2, codes[:, 128:256], codes[:, 0:128])
+    out = applied(turned(nodes, codes), project_a, project_b)
     for a in range(4):
         for b in range(4):
             m_ref[pl.ds(4 * a + b, 4, stride=16), :] = out[a][b]
     pieces = jnp.concatenate([m_ref[0:32, :], m_ref[32:64, :]], axis=1)
     both = jnp.concatenate(halves_of(pieces), axis=0)
     placed = lax.dot_general(
-        both, place_ref[...], (((1,), (1,)), ((), ())), preferred_element_type=jnp.float32
+        both, one_hot(768, target), (((1,), (1,)), ((), ())), preferred_element_type=jnp.float32
     )
     placed = placed[0:32] + placed[32:64]
     for w in range(2):
@@ -396,9 +363,9 @@
     register_ref = refs.pop(0) if section else None
     rate_in_ref, part_ref = refs[0:2]
     received = refs[2:7]
-    spread_ref, place_ref, codes_ref, scale_ref = refs[7:11]
-    del refs[0:11]
-    list_spread_ref = None if section else refs.pop(0)
+    index_ref, scale_ref = refs[7:9]
+    del refs[0:9]
+    send_ref = None if section else refs.pop(0)
     new_u_ref, new_register_ref = refs[0:2]
     del refs[0:2]
     list_refs = [] if section else refs[0:5]
@@ -406,8 +373,10 @@
     r_ref, g_ref, m_ref, rate_ref, t_ref = refs
     core = core_ref[0]
     write_received(core, *received, r_ref)
-    gathered = part_ref[...] + picked(r_ref[...], spread_ref[...])
-    exterior(gathered, codes_ref, place_ref, g_ref, m_ref)
+    columns = [received_column(core, column) for column in source_columns(index_ref)]
+    spread = jnp.concatenate([one_hot(1536, column) for column in columns], axis=1)
+    gathered = part_ref[...] + picked(r_ref[...], spread)
+    exterior(gathered, index_ref, g_ref, m_ref)
     rate_ref[...] = rate_in_ref[...]
     add_lift(rate_ref, g_ref)
     for half in range(2):
@@ -419,7 +388,7 @@
         new_u_ref[rows, :] = u_ref[rows, :] + SECTION_B[section] * register
     if section == 0:
         write_table(new_u_ref, t_ref)
-        write_lists(t_ref, list_spread_ref[...], *list_refs)
+        write_lists(t_ref, list_spread(core, send_ref), *list_refs)
 
 
 def shaped(rows, columns=LANES, dtype=jnp.float32):
@@ -460,6 +429,25 @@
     far = lax.ppermute(far, "sfc", ahead(2))
     shared = lax.all_gather(near[2 * u : 4 * u], "sfc", axis_index_groups=pairs, tiled=True)
     return swapped, near, far, across, shared
+
+
+def packed(
+    face_source, face_code, mortar_source, mortar_code, mortar_target, refinement, material
+):
+    def wide(rows):
+        return jnp.pad(rows, ((0, 0), (0, LANES - rows.shape[1])))
+
+    index = jnp.concatenate(
+        [
+            face_source,
+            face_code,
+            wide(mortar_source),
+            wide(mortar_code),
+            wide(mortar_target[None]),
+        ]
+    )
+    metric = jnp.left_shift(jnp.ones_like(refinement), refinement).astype(jnp.float32)
+    return index, STEP_SIZE * metric * material
 
 
 def local(
@@ -477,59 +465,36 @@
     core_at = core.reshape(1)
     volume = jnp.asarray(volume_operand())
     solution = fields.reshape(384, LANES)
-    refinement = refinement.reshape(1, LANES)
-    target = mortar_target.reshape(1, 64)
     table = (96, 768)
-    lists = called(
+    *lists, solution, send_face = called(
         lists_kernel,
         core_at,
         [solution, send_face],
-        LIST_OUTPUTS,
+        LIST_OUTPUTS + [shaped(384), shaped(8, 192, jnp.int32)],
         [table],
     )
     register = None
+    index = scale = None
     for section in range(2):
         received = exchanged(core, *lists)
         if section == 0:
-            rate, part, list_spread_made, *made = called(
-                first_kernel,
-                core_at,
-                [
-                    solution,
-                    volume,
-                    face_source,
-                    mortar_source,
-                    face_code,
-                    mortar_code,
-                    target,
-                    material,
-                    refinement,
-                    send_face,
-                ],
-                [
-                    shaped(384),
-                    shaped(96, 1024),
-                    shaped(768, 1536, jnp.bfloat16),
-                    shaped(1536, 1024, jnp.bfloat16),
-                    shaped(768, 256, jnp.bfloat16),
-                    shaped(16, LANES, jnp.int32),
-                    shaped(2, LANES),
-                ],
-                [table],
-            )
-        else:
-            rate, part = called(
-                local_part,
-                None,
-                [solution, volume, face_source, mortar_source],
-                [shaped(384), shaped(96, 1024)],
-                [table],
-            )
+            arrays = (face_source, face_code, mortar_source, mortar_code)
+            arrays = (*arrays, mortar_target, refinement, material)
+            arrays, swapped = lax.optimization_barrier((arrays, received[0]))
+            received = (swapped, *received[1:])
+            index, scale = packed(*arrays)
+        rate, part = called(
+            local_kernel,
+            None,
+            [solution, volume, index],
+            [shaped(384), shaped(96, 1024)],
+            [table],
+        )
         operands = [solution] + ([register] if section else [])
-        operands += [rate, part, *received, *made]
+        operands += [rate, part, *received, index, scale]
         outputs = [shaped(384), shaped(384)]
         if section == 0:
-            operands.append(list_spread_made)
+            operands.append(send_face)
             outputs = outputs + LIST_OUTPUTS
 
         def kernel(*refs, section=section):

time: 63.9 us -> 62.7 us (0.981)
  blocking collectives: 8.79 us -> 27.3 us
  starting transfers between devices: 33.1 us -> 20.6 us
  local copies, waits for them, and re-layouts: 8.27 us -> 3.13 us
  Pallas kernels: 8.29 us -> 6.26 us
    ppermute x2, starting transfers between devices: 20.7 us -> 6.33 us  [exchanged(): near = lax.ppermute(near, 'sfc', ahead(1))]
    all_gather x2, blocking collectives: 4.76 us -> 14.4 us  [exchanged(): swapped = lax.all_gather(swap, 'sfc', axis_index_groups=pairs, tiled=True)]
    all_gather x2, blocking collectives: 4.03 us -> 12.9 us  [exchanged(): lax.all_gather(near[2 * u:4 * u], 'sfc', axis_index_groups=pairs, tiled=T...]
    unnamed x28 -> x20, local copies, waits for them, and re-layouts: 8.21 us -> 2.97 us
    ppermute x2, waiting for transfers between devices: 0.01 us -> 2.58 us  [exchanged(): near = lax.ppermute(near, 'sfc', ahead(1))]
    ppermute x2, waiting for transfers between devices: 3.66 us -> 1.36 us  [exchanged(): across = lax.ppermute(far_4, 'sfc', ahead(-2))]
    pallas_call x5, Pallas kernels: 8.29 us -> 6.26 us  [called(): pl.pallas_call(kernel, in_specs=first + [pl.BlockSpec(memory_space=pltpu....]
    ppermute x2, starting transfers between devices: 6.94 us -> 8.7 us  [exchanged(): across = lax.ppermute(far_4, 'sfc', ahead(-2))]
  transfers between devices with their start and end apart: 6 -> 6, of which waited for: 1 -> 2; matrix products, arithmetic and copies ran while one was open for 0% -> 0% of each run, Pallas kernels for 6% -> 2%
where the time goes in v4:
time: 62.7 us; the launch traced here: 62.2 us
  blocking collectives  27.3 us (44%)
  starting transfers between devices  20.6 us (33%)
  Pallas kernels  6.26 us (10%)
  waiting for transfers between devices  3.94 us (6%)
  local copies, waits for them, and re-layouts  3.13 us (5%)
  between operations  0.89 us (1%)
    all_gather x2, blocking collectives, exchanged(): swapped = lax.all_gather(swap, 'sfc', axis_index_groups=pairs, tiled=True)  14.4 us
    all_gather x2, blocking collectives, exchanged(): lax.all_gather(near[2 * u:4 * u], 'sfc', axis_index_groups=pairs, tiled=T...  12.9 us
    ppermute x2, starting transfers between devices, exchanged(): across = lax.ppermute(far_4, 'sfc', ahead(-2))  8.7 us
    ppermute x2, starting transfers between devices, exchanged(): near = lax.ppermute(near, 'sfc', ahead(1))  6.33 us
    pallas_call x5, Pallas kernels, called(): pl.pallas_call(kernel, in_specs=first + [pl.BlockSpec(memory_space=pltpu....  6.26 us
    ppermute x2, starting transfers between devices, exchanged(): far = lax.ppermute(far, 'sfc', ahead(2))  5.58 us
    unnamed x20, local copies, waits for them, and re-layouts  2.97 us
    ppermute x2, waiting for transfers between devices, exchanged(): near = lax.ppermute(near, 'sfc', ahead(1))  2.58 us
  transfers between devices with their start and end apart: 6, of which 2 were waited for; matrix products, arithmetic and copies ran while one was open for 0% of the time, Pallas kernels for 2%

profile of v4, /device:TPU:7, one launch (start us, length us, event | category | flops | bytes accessed | tf_op | source)
XLA Modules:
  0.0 62.2 jit_solution(4155375511710364663)
XLA Ops:
  0.6 0.0 copy-start.2
  0.6 0.7 %copy-done.2 = s32[8,192]{1,0:T(8,128)S(1)} copy-done((s32[8,192]{1,0:T(8,128)S(1)}, s32[8,192]{1,0:T(8,128)}, u32[]{:S(2)}) %copy-start.2) | copy-done | bytes 6168
  1.3 0.0 copy-start.1
  1.3 0.9 %copy-done.1 = f32[6,64,128]{2,1,0:T(8,128)S(1)} copy-done((f32[6,64,128]{2,1,0:T(8,128)S(1)}, f32[6,64,128]{2,1,0:T(8,128)}, u32[]{:S(2)}) %copy-start.1) | copy-done | bytes 196632
  2.3 0.8 %shard_map.113 = (f32[576,128]{1,0:T(8,128)S(1)}, f32[144,128]{1,0:T(8,128)S(1)}, f32[144,128]{1,0:T(8,128)S(1)}, f32[144,128]{1,0:T(8,128)S(1)}, f32[144,128]{1...) custom-call(s32[1]{0:T(128)} %bitcast.core_ref.refs_0_, f32[384,128]{1,0:T(8,128)S(1)} %bitcast.5, ...), custom_call_target="tpu_custom_call" | custom-call | tf_op jit(solution)/shard_map/pallas_call | solution.py:401
  3.0 4.9 %collective-permute-start.2 = (f32[144,128]{1,0:T(8,128)S(1)}, f32[144,128]{1,0:T(8,128)S(1)}, u32[]{:S(2)}, u32[]{:S(2)}) collective-permute-start(f32[144,128]{1,0:T(8,128)S(1)} %get-tuple-element.43), channel_id=1, source_target_pairs={{1,5},{3,7},{4,0},{5,9},{6,2},{7,11},{8,4},{9,13},{10,6},{11,15},{... | collective-permute-start | bytes 221192 | tf_op jit(solution)/shard_map/ppermute | solution.py:422
  8.0 12.2 %all_gather.12.refs_4_ = f32[1152,128]{1,0:T(8,128)S(1)} all-gather(f32[576,128]{1,0:T(8,128)S(1)} %get-tuple-element.31), channel_id=1, replica_groups={{0,1},{2,3},{4,5},{6,7},{8,9},{10,11},{12,13},{14,15},{16,17},{18,19},{..., dimensions={0}, use_global_device_ids=true | all-gather | bytes 884736 | tf_op jit(solution)/shard_map/all_gather | solution.py:423
  20.2 0.0 copy-start
  20.2 3.2 %collective-permute-start.1 = (f32[288,128]{1,0:T(8,128)S(1)}, f32[288,128]{1,0:T(8,128)S(1)}, u32[]{:S(2)}, u32[]{:S(2)}) collective-permute-start(f32[288,128]{1,0:T(8,128)S(1)} %pad_maximum_fusion.2), channel_id=1, source_target_pairs={{0,4},{2,6},{4,8},{5,1},{6,10},{7,3},{8,12},{9,5},{10,14},{11,7},{... | collective-permute-start | bytes 442376 | tf_op jit(solution)/shard_map/ppermute | solution.py:429
  23.4 0.0 copy-start.8
  23.4 0.0 copy-start.9
  23.4 0.0 copy-start.6
  23.5 0.0 copy-start.7
  23.5 3.9 %collective-permute-start = (f32[576,128]{1,0:T(8,128)S(1)}, f32[576,128]{1,0:T(8,128)S(1)}, u32[]{:S(2)}, u32[]{:S(2)}) collective-permute-start(f32[576,128]{1,0:T(8,128)S(1)} %pad_maximum_fusion), channel_id=1, source_target_pairs={{0,2},{2,4},{3,1},{4,6},{5,3},{6,8},{7,5},{8,10},{9,7},{10,12},{11... | collective-permute-start | bytes 884744 | tf_op jit(solution)/shard_map/ppermute | solution.py:428
  27.3 0.0 copy-done.8
  27.4 0.0 copy-done.7
  27.4 0.0 copy-start.5
  27.4 0.0 copy-done.9
  27.4 0.6 %copy-done.5 = s32[4,64]{1,0:T(4,128)S(1)} copy-done((s32[4,64]{1,0:T(4,128)S(1)}, s32[4,64]{1,0:T(4,128)}, u32[]{:S(2)}) %copy-start.5) | copy-done | bytes 1048
  28.1 0.0 copy-start.3
  28.1 0.0 copy-start.4
  28.1 0.0 copy-done.6
  28.1 0.7 %copy-done.3 = s32[6,128]{1,0:T(8,128)S(1)} copy-done((s32[6,128]{1,0:T(8,128)S(1)}, s32[6,128]{1,0:T(8,128)}, u32[]{:S(2)}) %copy-start.3) | copy-done | bytes 3096
  28.8 0.0 copy-done.4
  28.8 0.1 concatenate.15.index_ref.refs_9_.refs_10_
  28.9 0.0 copy-done
  28.9 0.7 %shard_map.114 = (f32[384,128]{1,0:T(8,128)S(1)}, f32[96,1024]{1,0:T(8,128)S(1)}) custom-call(f32[384,128]{1,0:T(8,128)S(1)} %get-tuple-element.30.u_ref.refs_1_, bf16[384,1152]{1,0:T(8,128)(2,1)S(1)} %copy-done, s32[21,128]{1,0:T(8,128)S(1)} %concatenate.15.index_ref.refs_9_.refs_10_), custom_call_target="tpu_custom_call" | custom-call | tf_op jit(solution)/shard_map/pallas_call | solution.py:401
  29.6 2.6 %collective-permute-done.refs_5_ = f32[576,128]{1,0:T(8,128)S(1)} collective-permute-done((f32[576,128]{1,0:T(8,128)S(1)}, f32[576,128]{1,0:T(8,128)S(1)}, u32[]{:S(2)}, u32[]{:S(2)}) %collective-permute-start) | collective-permute-done | bytes 294944 | tf_op jit(solution)/shard_map/ppermute | solution.py:428
  32.2 6.7 %all_gather.13.refs_8_ = f32[576,128]{1,0:T(8,128)S(1)} all-gather(f32[288,128]{1,0:T(8,128)S(1)} %slice.32), channel_id=1, replica_groups={{0,1},{2,3},{4,5},{6,7},{8,9},{10,11},{12,13},{14,15},{16,17},{18,19},{..., dimensions={0}, use_global_device_ids=true | all-gather | bytes 442368 | tf_op jit(solution)/shard_map/all_gather | solution.py:430
  38.8 0.0 collective-permute-done.2.refs_7_
  38.8 0.0 collective-permute-done.1.refs_6_
  38.8 2.0 %shard_map.115 = (f32[384,128]{1,0:T(8,128)S(1)}, f32[384,128]{1,0:T(8,128)S(1)}, f32[576,128]{1,0:T(8,128)S(1)}, f32[144,128]{1,0:T(8,128)S(1)}, f32[144,128]{1...) custom-call(s32[1]{0:T(128)} %bitcast.core_ref.refs_0_, f32[384,128]{1,0:T(8,128)S(1)} %get-tuple-element.30.u_ref.refs_1_, ...), custom_call_target="tpu_custom_call" | custom-call | tf_op jit(solution)/shard_map/pallas_call | solution.py:401
  40.9 2.2 %all_gather.14.refs_5_ = f32[1152,128]{1,0:T(8,128)S(1)} all-gather(f32[576,128]{1,0:T(8,128)S(1)} %get-tuple-element.51), channel_id=1, replica_groups={{0,1},{2,3},{4,5},{6,7},{8,9},{10,11},{12,13},{14,15},{16,17},{18,19},{..., dimensions={0}, use_global_device_ids=true | all-gather | bytes 884736 | tf_op jit(solution)/shard_map/all_gather | solution.py:423
  43.1 2.5 %collective-permute-start.3 = (f32[576,128]{1,0:T(8,128)S(1)}, f32[576,128]{1,0:T(8,128)S(1)}, u32[]{:S(2)}, u32[]{:S(2)}) collective-permute-start(f32[576,128]{1,0:T(8,128)S(1)} %pad_maximum_fusion.1), channel_id=1, source_target_pairs={{0,2},{2,4},{3,1},{4,6},{5,3},{6,8},{7,5},{8,10},{9,7},{10,12},{11... | collective-permute-start | bytes 884744 | tf_op jit(solution)/shard_map/ppermute | solution.py:428
  45.6 2.4 %collective-permute-start.4 = (f32[288,128]{1,0:T(8,128)S(1)}, f32[288,128]{1,0:T(8,128)S(1)}, u32[]{:S(2)}, u32[]{:S(2)}) collective-permute-start(f32[288,128]{1,0:T(8,128)S(1)} %pad_maximum_fusion.3), channel_id=1, source_target_pairs={{0,4},{2,6},{4,8},{5,1},{6,10},{7,3},{8,12},{9,5},{10,14},{11,7},{... | collective-permute-start | bytes 442376 | tf_op jit(solution)/shard_map/ppermute | solution.py:429
  48.0 3.8 %collective-permute-start.5 = (f32[144,128]{1,0:T(8,128)S(1)}, f32[144,128]{1,0:T(8,128)S(1)}, u32[]{:S(2)}, u32[]{:S(2)}) collective-permute-start(f32[144,128]{1,0:T(8,128)S(1)} %get-tuple-element.55), channel_id=1, source_target_pairs={{1,5},{3,7},{4,0},{5,9},{6,2},{7,11},{8,4},{9,13},{10,6},{11,15},{... | collective-permute-start | bytes 221192 | tf_op jit(solution)/shard_map/ppermute | solution.py:422
  51.8 0.7 %shard_map.116 = (f32[384,128]{1,0:T(8,128)S(1)}, f32[96,1024]{1,0:T(8,128)S(1)}) custom-call(f32[384,128]{1,0:T(8,128)S(1)} %get-tuple-element.47.u_ref.refs_1_, bf16[384,1152]{1,0:T(8,128)(2,1)S(1)} %copy-done, s32[21,128]{1,0:T(8,128)S(1)} %concatenate.15.index_ref.refs_9_.refs_10_), custom_call_target="tpu_custom_call" | custom-call | tf_op jit(solution)/shard_map/pallas_call | solution.py:401
  52.5 0.0 collective-permute-done.3.refs_6_
  52.6 6.2 %all_gather.15.refs_9_ = f32[576,128]{1,0:T(8,128)S(1)} all-gather(f32[288,128]{1,0:T(8,128)S(1)} %slice.33), channel_id=1, replica_groups={{0,1},{2,3},{4,5},{6,7},{8,9},{10,11},{12,13},{14,15},{16,17},{18,19},{..., dimensions={0}, use_global_device_ids=true | all-gather | bytes 442368 | tf_op jit(solution)/shard_map/all_gather | solution.py:430
  58.8 1.4 %collective-permute-done.5.refs_8_ = f32[144,128]{1,0:T(8,128)S(1)} collective-permute-done((f32[144,128]{1,0:T(8,128)S(1)}, f32[144,128]{1,0:T(8,128)S(1)}, u32[]{:S(2)}, u32[]{:S(2)}) %collective-permute-start.5) | collective-permute-done | bytes 73760 | tf_op jit(solution)/shard_map/ppermute | solution.py:422
  60.2 0.0 collective-permute-done.4.refs_7_
  60.2 2.1 %shard_map.117 = (f32[384,128]{1,0:T(8,128)}, f32[384,128]{1,0:T(8,128)}) custom-call(s32[1]{0:T(128)} %bitcast.core_ref.refs_0_, f32[384,128]{1,0:T(8,128)S(1)} %get-tuple-element.47.u_ref.refs_1_, f32[384,128]{1,0:T(8,128)S(1)} %get-tuple-element.48.refs_2_, f32[384,128]{1,0:T(8,128)S(1)} %get-tuple-element.49.refs_3_, ...), custom_call_target="tpu_custom_call" | custom-call | tf_op jit(solution)/shard_map/pallas_call | solution.py:401
  (13 shorter events, 0.2 us)
Async XLA Ops:
  0.6 0.7 %copy-start.2 = (s32[8,192]{1,0:T(8,128)S(1)}, s32[8,192]{1,0:T(8,128)}, u32[]{:S(2)}) copy-start(s32[8,192]{1,0:T(8,128)} %send_ref.1) | copy-start | bytes 18436
  1.3 0.9 %copy-start.1 = (f32[6,64,128]{2,1,0:T(8,128)S(1)}, f32[6,64,128]{2,1,0:T(8,128)}, u32[]{:S(2)}) copy-start(f32[6,64,128]{2,1,0:T(8,128)} %param.10) | copy-start | bytes 589828
  3.0 35.8 %collective-permute-start.2 = (f32[144,128]{1,0:T(8,128)S(1)}, f32[144,128]{1,0:T(8,128)S(1)}, u32[]{:S(2)}, u32[]{:S(2)}) collective-permute-start(f32[144,128]{1,0:T(8,128)S(1)} %get-tuple-element.43), channel_id=1, source_target_pairs={{1,5},{3,7},{4,0},{5,9},{6,2},{7,11},{8,4},{9,13},{10,6},{11,15},{... | collective-permute-start | bytes 221192 | tf_op jit(solution)/shard_map/ppermute | solution.py:422
  20.2 8.7 %copy-start = (bf16[384,1152]{1,0:T(8,128)(2,1)S(1)}, bf16[384,1152]{1,0:T(8,128)(2,1)}, u32[]{:S(2)}) copy-start(bf16[384,1152]{1,0:T(8,128)(2,1)} %constant.20.clone.volume_ref) | copy-start | bytes 2654212
  20.2 18.6 %collective-permute-start.1 = (f32[288,128]{1,0:T(8,128)S(1)}, f32[288,128]{1,0:T(8,128)S(1)}, u32[]{:S(2)}, u32[]{:S(2)}) collective-permute-start(f32[288,128]{1,0:T(8,128)S(1)} %pad_maximum_fusion.2), channel_id=1, source_target_pairs={{0,4},{2,6},{4,8},{5,1},{6,10},{7,3},{8,12},{9,5},{10,14},{11,7},{... | collective-permute-start | bytes 442376 | tf_op jit(solution)/shard_map/ppermute | solution.py:429
  23.4 3.9 %copy-start.8 = (s32[128]{0:T(128)S(1)}, s32[128]{0:T(128)}, u32[]{:S(2)}) copy-start(s32[128]{0:T(128)} %param.12) | copy-start | bytes 1540
  23.4 4.0 %copy-start.9 = (s32[64]{0:T(128)S(1)}, s32[64]{0:T(128)}, u32[]{:S(2)}) copy-start(s32[64]{0:T(128)} %param.18) | copy-start | bytes 772
  23.4 4.7 %copy-start.6 = (s32[4,64]{1,0:T(4,128)S(1)}, s32[4,64]{1,0:T(4,128)}, u32[]{:S(2)}) copy-start(s32[4,64]{1,0:T(4,128)} %param.17) | copy-start | bytes 3076
  23.5 3.9 %copy-start.7 = (f32[2,128]{1,0:T(2,128)S(1)}, f32[2,128]{1,0:T(2,128)}, u32[]{:S(2)}) copy-start(f32[2,128]{1,0:T(2,128)} %param.11) | copy-start | bytes 3076
  23.5 8.7 %collective-permute-start = (f32[576,128]{1,0:T(8,128)S(1)}, f32[576,128]{1,0:T(8,128)S(1)}, u32[]{:S(2)}, u32[]{:S(2)}) collective-permute-start(f32[576,128]{1,0:T(8,128)S(1)} %pad_maximum_fusion), channel_id=1, source_target_pairs={{0,2},{2,4},{3,1},{4,6},{5,3},{6,8},{7,5},{8,10},{9,7},{10,12},{11... | collective-permute-start | bytes 884744 | tf_op jit(solution)/shard_map/ppermute | solution.py:428
  27.4 0.7 %copy-start.5 = (s32[4,64]{1,0:T(4,128)S(1)}, s32[4,64]{1,0:T(4,128)}, u32[]{:S(2)}) copy-start(s32[4,64]{1,0:T(4,128)} %param.16) | copy-start | bytes 3076
  28.1 0.7 %copy-start.3 = (s32[6,128]{1,0:T(8,128)S(1)}, s32[6,128]{1,0:T(8,128)}, u32[]{:S(2)}) copy-start(s32[6,128]{1,0:T(8,128)} %param.13) | copy-start | bytes 9220
  28.1 0.7 %copy-start.4 = (s32[6,128]{1,0:T(8,128)S(1)}, s32[6,128]{1,0:T(8,128)}, u32[]{:S(2)}) copy-start(s32[6,128]{1,0:T(8,128)} %param.14) | copy-start | bytes 9220
  43.1 9.4 %collective-permute-start.3 = (f32[576,128]{1,0:T(8,128)S(1)}, f32[576,128]{1,0:T(8,128)S(1)}, u32[]{:S(2)}, u32[]{:S(2)}) collective-permute-start(f32[576,128]{1,0:T(8,128)S(1)} %pad_maximum_fusion.1), channel_id=1, source_target_pairs={{0,2},{2,4},{3,1},{4,6},{5,3},{6,8},{7,5},{8,10},{9,7},{10,12},{11... | collective-permute-start | bytes 884744 | tf_op jit(solution)/shard_map/ppermute | solution.py:428
  45.6 14.5 %collective-permute-start.4 = (f32[288,128]{1,0:T(8,128)S(1)}, f32[288,128]{1,0:T(8,128)S(1)}, u32[]{:S(2)}, u32[]{:S(2)}) collective-permute-start(f32[288,128]{1,0:T(8,128)S(1)} %pad_maximum_fusion.3), channel_id=1, source_target_pairs={{0,4},{2,6},{4,8},{5,1},{6,10},{7,3},{8,12},{9,5},{10,14},{11,7},{... | collective-permute-start | bytes 442376 | tf_op jit(solution)/shard_map/ppermute | solution.py:429
  48.0 12.1 %collective-permute-start.5 = (f32[144,128]{1,0:T(8,128)S(1)}, f32[144,128]{1,0:T(8,128)S(1)}, u32[]{:S(2)}, u32[]{:S(2)}) collective-permute-start(f32[144,128]{1,0:T(8,128)S(1)} %get-tuple-element.55), channel_id=1, source_target_pairs={{1,5},{3,7},{4,0},{5,9},{6,2},{7,11},{8,4},{9,13},{10,6},{11,15},{... | collective-permute-start | bytes 221192 | tf_op jit(solution)/shard_map/ppermute | solution.py:422

commit v5 on v2

--- a/solution.py
+++ b/solution.py
@@ -157,9 +157,18 @@
         ref[UNIT * place + 96 : UNIT * place + UNIT, :] = packed
 
 
-def lists_kernel(core_ref, u_ref, send_ref, swap_ref, own_ref, t_ref):
+def lists_kernel(
+    core_ref, u_hbm, send_hbm, swap_ref, own_ref, t_ref, u_ref, send_ref, send_sem, u_sem
+):
+    send_copy = pltpu.make_async_copy(send_hbm, send_ref, send_sem)
+    u_copy = pltpu.make_async_copy(u_hbm, u_ref, u_sem)
+    send_copy.start()
+    u_copy.start()
+    send_copy.wait()
+    spread = list_spread(core_ref[0], send_ref)
+    u_copy.wait()
     write_table(u_ref, t_ref)
-    write_lists(t_ref, list_spread(core_ref[0], send_ref), swap_ref, own_ref)
+    write_lists(t_ref, spread, swap_ref, own_ref)
 
 
 def mortar_row(ref):
@@ -424,15 +433,18 @@
     return jax.ShapeDtypeStruct((rows, columns), dtype)
 
 
-def called(kernel, core, operands, outputs, scratch):
+def called(kernel, core, operands, outputs, scratch, space=pltpu.VMEM):
     first = [] if core is None else [pl.BlockSpec(memory_space=pltpu.SMEM)]
     given = list(operands) if core is None else [core, *operands]
     return pl.pallas_call(
         kernel,
-        in_specs=first + [pl.BlockSpec(memory_space=pltpu.VMEM)] * len(operands),
+        in_specs=first + [pl.BlockSpec(memory_space=space)] * len(operands),
         out_specs=[pl.BlockSpec(memory_space=pltpu.VMEM)] * len(outputs),
         out_shape=outputs,
-        scratch_shapes=[pltpu.VMEM(shape, jnp.float32) for shape in scratch],
+        scratch_shapes=[
+            pltpu.VMEM(shape, jnp.float32) if isinstance(shape, tuple) else shape
+            for shape in scratch
+        ],
         compiler_params=pltpu.CompilerParams(vmem_limit_bytes=VMEM_LIMIT),
     )(*given)
 
@@ -481,9 +493,19 @@
     swap, own = called(
         lists_kernel,
         core_at,
-        [solution, send_face],
+        [
+            pltpu.with_memory_space_constraint(operand, pltpu.HBM)
+            for operand in (solution, send_face)
+        ],
         LIST_OUTPUTS,
-        [table],
+        [
+            table,
+            (384, LANES),
+            pltpu.VMEM((8, 192), jnp.int32),
+            pltpu.SemaphoreType.DMA,
+            pltpu.SemaphoreType.DMA,
+        ],
+        space=pltpu.HBM,
     )
     register = None
     for section in range(2):

time: 58 us -> 57.6 us (level)
  local copies, waits for them, and re-layouts: 1.86 us -> 0.17 us
  Pallas kernels: 8.28 us -> 9.64 us
    unnamed x24 -> x20, local copies, waits for them, and re-layouts: 1.74 us -> 0.04 us
    pallas_call x5, Pallas kernels: 8.28 us -> 9.64 us  [called(): pl.pallas_call(kernel, in_specs=first + [pl.BlockSpec(memory_space=space)...]
where the time goes in v5:
time: 57.6 us; the launch traced here: 57.4 us
  starting transfers between devices  25.5 us (44%)
  blocking collectives  13.6 us (24%)
  Pallas kernels  9.64 us (17%)
  waiting for transfers between devices  7.42 us (13%)
  between operations  0.97 us (2%)
    ppermute x2, starting transfers between devices, exchanged(): near = lax.ppermute(near, 'sfc', ahead(1))  20.5 us
    pallas_call x5, Pallas kernels, called(): pl.pallas_call(kernel, in_specs=first + [pl.BlockSpec(memory_space=space)...  9.64 us
    all_gather x2, blocking collectives, exchanged(): shared = lax.all_gather(shared, 'sfc', axis_index_groups=pairs, tiled=True)  8.61 us
    ppermute x2, waiting for transfers between devices, exchanged(): far = lax.ppermute(far, 'sfc', ahead(2))  7.42 us
    ppermute x2, starting transfers between devices, exchanged(): far = lax.ppermute(far, 'sfc', ahead(2))  5 us
    all_gather x2, blocking collectives, exchanged(): swapped = lax.all_gather(swap, 'sfc', axis_index_groups=pairs, tiled=True)  4.97 us
  transfers between devices with their start and end apart: 4, of which 2 were waited for; matrix products, arithmetic and copies ran while one was open for 0% of the time, Pallas kernels for 6%

profile of v5, /device:TPU:7, one launch (start us, length us, event | category | flops | bytes accessed | tf_op | source)
XLA Modules:
  0.0 57.4 jit_solution(7742280187756704196)
XLA Ops:
  0.6 0.0 copy-start
  0.6 0.0 copy-start.2
  0.7 0.0 copy-start.1
  0.7 0.0 copy-start.4
  0.7 0.0 copy-start.3
  0.7 0.0 copy-start.8
  0.7 0.0 copy-start.6
  0.7 0.0 copy-start.5
  0.7 0.0 copy-start.9
  0.7 0.0 copy-start.7
  0.7 2.1 %shard_map.114 = (f32[720,128]{1,0:T(8,128)S(1)}, f32[432,128]{1,0:T(8,128)S(1)}) custom-call(s32[1]{0:T(128)} %bitcast.core_ref.refs_0_, f32[384,128]{1,0:T(8,128)} %bitcast.6, s32[8,192]{1,0:T(8,128)} %send_hbm.1), custom_call_target="tpu_custom_call" | custom-call | tf_op jit(solution)/shard_map/pallas_call | solution.py:439
  2.9 2.6 %all_gather.12.refs_4_ = f32[1440,128]{1,0:T(8,128)S(1)} all-gather(f32[720,128]{1,0:T(8,128)S(1)} %get-tuple-element.21), channel_id=1, replica_groups={{0,1},{2,3},{4,5},{6,7},{8,9},{10,11},{12,13},{14,15},{16,17},{18,19},{..., dimensions={0}, use_global_device_ids=true | all-gather | bytes 1105920 | tf_op jit(solution)/shard_map/all_gather | solution.py:463
  5.6 13.8 %collective-permute-start = (f32[576,128]{1,0:T(8,128)S(1)}, f32[576,128]{1,0:T(8,128)S(1)}, u32[]{:S(2)}, u32[]{:S(2)}) collective-permute-start(f32[576,128]{1,0:T(8,128)S(1)} %pad_maximum_fusion), channel_id=1, source_target_pairs={{0,2},{2,4},{3,1},{4,6},{5,3},{6,8},{7,5},{8,10},{9,7},{10,12},{11... | collective-permute-start | bytes 884744 | tf_op jit(solution)/shard_map/ppermute | solution.py:468
  19.5 3.1 %collective-permute-start.1 = (f32[432,128]{1,0:T(8,128)S(1)}, f32[432,128]{1,0:T(8,128)S(1)}, u32[]{:S(2)}, u32[]{:S(2)}) collective-permute-start(f32[432,128]{1,0:T(8,128)S(1)} %pad_maximum_fusion.2), channel_id=1, source_target_pairs={{0,4},{2,6},{4,8},{5,1},{6,10},{7,3},{8,12},{9,5},{10,14},{11,7},{... | collective-permute-start | bytes 663560 | tf_op jit(solution)/shard_map/ppermute | solution.py:469
  22.6 0.0 copy-done
  22.6 0.0 copy-done.2
  22.6 0.0 copy-done.1
  22.6 0.0 copy-done.4
  22.6 0.0 copy-done.3
  22.6 0.0 copy-done.8
  22.6 0.0 copy-done.6
  22.6 0.0 copy-done.5
  22.7 0.0 copy-done.9
  22.7 0.0 copy-done.7
  22.7 3.0 %shard_map.113 = (f32[384,128]{1,0:T(8,128)S(1)}, f32[96,1024]{1,0:T(8,128)S(1)}, bf16[768,1536]{1,0:T(8,128)(2,1)S(1)}, bf16[1536,1024]{1,0:T(8,128)(2,1)S(1)},...) custom-call(s32[1]{0:T(128)} %bitcast.core_ref.refs_0_, f32[384,128]{1,0:T(8,128)S(1)} %bitcast.7, ...), custom_call_target="tpu_custom_call" | custom-call | tf_op jit(solution)/shard_map/pallas_call | solution.py:439
  25.7 1.7 %collective-permute-done.1.refs_6_ = f32[432,128]{1,0:T(8,128)S(1)} collective-permute-done((f32[432,128]{1,0:T(8,128)S(1)}, f32[432,128]{1,0:T(8,128)S(1)}, u32[]{:S(2)}, u32[]{:S(2)}) %collective-permute-start.1) | collective-permute-done | bytes 221216 | tf_op jit(solution)/shard_map/ppermute | solution.py:469
  27.4 0.0 collective-permute-done.refs_5_
  27.5 4.4 %all_gather.13.refs_7_ = f32[864,128]{1,0:T(8,128)S(1)} all-gather(f32[432,128]{1,0:T(8,128)S(1)} %pad_maximum_fusion.3), channel_id=1, replica_groups={{0,1},{2,3},{4,5},{6,7},{8,9},{10,11},{12,13},{14,15},{16,17},{18,19},{..., dimensions={0}, use_global_device_ids=true | all-gather | bytes 663552 | tf_op jit(solution)/shard_map/all_gather | solution.py:471
  31.8 1.9 %shard_map.115 = (f32[384,128]{1,0:T(8,128)S(1)}, f32[384,128]{1,0:T(8,128)S(1)}, f32[720,128]{1,0:T(8,128)S(1)}, f32[432,128]{1,0:T(8,128)S(1)}) custom-call(s32[1]{0:T(128)} %bitcast.core_ref.refs_0_, f32[384,128]{1,0:T(8,128)S(1)} %bitcast.8, f32[384,128]{1,0:T(8,128)S(1)} %get-tuple-element.19.refs_2_, f32[96,1024]{1,0:T(8,128)S(1)} %get-tuple-element.20.refs_3_, ...), custom_call_target="tpu_custom_call" | custom-call | tf_op jit(solution)/shard_map/pallas_call | solution.py:439
  33.7 2.3 %all_gather.14.refs_5_ = f32[1440,128]{1,0:T(8,128)S(1)} all-gather(f32[720,128]{1,0:T(8,128)S(1)} %get-tuple-element.32), channel_id=1, replica_groups={{0,1},{2,3},{4,5},{6,7},{8,9},{10,11},{12,13},{14,15},{16,17},{18,19},{..., dimensions={0}, use_global_device_ids=true | all-gather | bytes 1105920 | tf_op jit(solution)/shard_map/all_gather | solution.py:463
  36.1 6.6 %collective-permute-start.2 = (f32[576,128]{1,0:T(8,128)S(1)}, f32[576,128]{1,0:T(8,128)S(1)}, u32[]{:S(2)}, u32[]{:S(2)}) collective-permute-start(f32[576,128]{1,0:T(8,128)S(1)} %pad_maximum_fusion.1), channel_id=1, source_target_pairs={{0,2},{2,4},{3,1},{4,6},{5,3},{6,8},{7,5},{8,10},{9,7},{10,12},{11... | collective-permute-start | bytes 884744 | tf_op jit(solution)/shard_map/ppermute | solution.py:468
  42.8 1.9 %collective-permute-start.3 = (f32[432,128]{1,0:T(8,128)S(1)}, f32[432,128]{1,0:T(8,128)S(1)}, u32[]{:S(2)}, u32[]{:S(2)}) collective-permute-start(f32[432,128]{1,0:T(8,128)S(1)} %pad_maximum_fusion.4), channel_id=1, source_target_pairs={{0,4},{2,6},{4,8},{5,1},{6,10},{7,3},{8,12},{9,5},{10,14},{11,7},{... | collective-permute-start | bytes 663560 | tf_op jit(solution)/shard_map/ppermute | solution.py:469
  44.7 0.7 %shard_map.116 = (f32[384,128]{1,0:T(8,128)S(1)}, f32[96,1024]{1,0:T(8,128)S(1)}) custom-call(f32[384,128]{1,0:T(8,128)S(1)} %get-tuple-element.28.u_ref.refs_1_, bf16[384,1152]{1,0:T(8,128)(2,1)S(1)} %copy-done, s32[6,128]{1,0:T(8,128)S(1)} %copy-done.3, s32[4,64]{1,0:T(4,128)S(1)} %copy-done.4), custom_call_target="tpu_custom_call" | custom-call | tf_op jit(solution)/shard_map/pallas_call | solution.py:439
  45.4 5.7 %collective-permute-done.3.refs_7_ = f32[432,128]{1,0:T(8,128)S(1)} collective-permute-done((f32[432,128]{1,0:T(8,128)S(1)}, f32[432,128]{1,0:T(8,128)S(1)}, u32[]{:S(2)}, u32[]{:S(2)}) %collective-permute-start.3) | collective-permute-done | bytes 221216 | tf_op jit(solution)/shard_map/ppermute | solution.py:469
  51.2 0.0 collective-permute-done.2.refs_6_
  51.2 4.3 %all_gather.15.refs_8_ = f32[864,128]{1,0:T(8,128)S(1)} all-gather(f32[432,128]{1,0:T(8,128)S(1)} %pad_maximum_fusion.5), channel_id=1, replica_groups={{0,1},{2,3},{4,5},{6,7},{8,9},{10,11},{12,13},{14,15},{16,17},{18,19},{..., dimensions={0}, use_global_device_ids=true | all-gather | bytes 663552 | tf_op jit(solution)/shard_map/all_gather | solution.py:471
  55.5 1.9 %shard_map.117 = (f32[384,128]{1,0:T(8,128)}, f32[384,128]{1,0:T(8,128)}) custom-call(s32[1]{0:T(128)} %bitcast.core_ref.refs_0_, f32[384,128]{1,0:T(8,128)S(1)} %get-tuple-element.28.u_ref.refs_1_, f32[384,128]{1,0:T(8,128)S(1)} %get-tuple-element.29.refs_2_, f32[384,128]{1,0:T(8,128)S(1)} %get-tuple-element.30.refs_3_, ...), custom_call_target="tpu_custom_call" | custom-call | tf_op jit(solution)/shard_map/pallas_call | solution.py:439
  (16 shorter events, 0.2 us)
Async XLA Ops:
  0.6 21.9 %copy-start = (bf16[384,1152]{1,0:T(8,128)(2,1)S(1)}, bf16[384,1152]{1,0:T(8,128)(2,1)}, u32[]{:S(2)}) copy-start(bf16[384,1152]{1,0:T(8,128)(2,1)} %constant.17.clone.volume_ref) | copy-start | bytes 2654212
  0.6 21.9 %copy-start.2 = (s32[8,192]{1,0:T(8,128)S(1)}, s32[8,192]{1,0:T(8,128)}, u32[]{:S(2)}) copy-start(s32[8,192]{1,0:T(8,128)} %send_hbm.1) | copy-start | bytes 18436
  0.7 21.9 %copy-start.1 = (f32[6,64,128]{2,1,0:T(8,128)S(1)}, f32[6,64,128]{2,1,0:T(8,128)}, u32[]{:S(2)}) copy-start(f32[6,64,128]{2,1,0:T(8,128)} %param.10) | copy-start | bytes 589828
  0.7 21.9 %copy-start.4 = (s32[4,64]{1,0:T(4,128)S(1)}, s32[4,64]{1,0:T(4,128)}, u32[]{:S(2)}) copy-start(s32[4,64]{1,0:T(4,128)} %mortar_ref.3) | copy-start | bytes 3076
  0.7 21.9 %copy-start.3 = (s32[6,128]{1,0:T(8,128)S(1)}, s32[6,128]{1,0:T(8,128)}, u32[]{:S(2)}) copy-start(s32[6,128]{1,0:T(8,128)} %face_ref.3) | copy-start | bytes 9220
  0.7 21.9 %copy-start.8 = (s32[64]{0:T(128)S(1)}, s32[64]{0:T(128)}, u32[]{:S(2)}) copy-start(s32[64]{0:T(128)} %param.18) | copy-start | bytes 772
  0.7 21.9 %copy-start.6 = (s32[4,64]{1,0:T(4,128)S(1)}, s32[4,64]{1,0:T(4,128)}, u32[]{:S(2)}) copy-start(s32[4,64]{1,0:T(4,128)} %mortar_code_ref.1) | copy-start | bytes 3076
  0.7 21.9 %copy-start.5 = (s32[6,128]{1,0:T(8,128)S(1)}, s32[6,128]{1,0:T(8,128)}, u32[]{:S(2)}) copy-start(s32[6,128]{1,0:T(8,128)} %code_ref.1) | copy-start | bytes 9220
  0.7 21.9 %copy-start.9 = (s32[128]{0:T(128)S(1)}, s32[128]{0:T(128)}, u32[]{:S(2)}) copy-start(s32[128]{0:T(128)} %param.12) | copy-start | bytes 1540
  0.7 21.9 %copy-start.7 = (f32[2,128]{1,0:T(2,128)S(1)}, f32[2,128]{1,0:T(2,128)}, u32[]{:S(2)}) copy-start(f32[2,128]{1,0:T(2,128)} %material_ref.1) | copy-start | bytes 3076
  5.6 21.8 %collective-permute-start = (f32[576,128]{1,0:T(8,128)S(1)}, f32[576,128]{1,0:T(8,128)S(1)}, u32[]{:S(2)}, u32[]{:S(2)}) collective-permute-start(f32[576,128]{1,0:T(8,128)S(1)} %pad_maximum_fusion), channel_id=1, source_target_pairs={{0,2},{2,4},{3,1},{4,6},{5,3},{6,8},{7,5},{8,10},{9,7},{10,12},{11... | collective-permute-start | bytes 884744 | tf_op jit(solution)/shard_map/ppermute | solution.py:468
  19.5 7.9 %collective-permute-start.1 = (f32[432,128]{1,0:T(8,128)S(1)}, f32[432,128]{1,0:T(8,128)S(1)}, u32[]{:S(2)}, u32[]{:S(2)}) collective-permute-start(f32[432,128]{1,0:T(8,128)S(1)} %pad_maximum_fusion.2), channel_id=1, source_target_pairs={{0,4},{2,6},{4,8},{5,1},{6,10},{7,3},{8,12},{9,5},{10,14},{11,7},{... | collective-permute-start | bytes 663560 | tf_op jit(solution)/shard_map/ppermute | solution.py:469
  36.1 15.0 %collective-permute-start.2 = (f32[576,128]{1,0:T(8,128)S(1)}, f32[576,128]{1,0:T(8,128)S(1)}, u32[]{:S(2)}, u32[]{:S(2)}) collective-permute-start(f32[576,128]{1,0:T(8,128)S(1)} %pad_maximum_fusion.1), channel_id=1, source_target_pairs={{0,2},{2,4},{3,1},{4,6},{5,3},{6,8},{7,5},{8,10},{9,7},{10,12},{11... | collective-permute-start | bytes 884744 | tf_op jit(solution)/shard_map/ppermute | solution.py:468
  42.8 8.3 %collective-permute-start.3 = (f32[432,128]{1,0:T(8,128)S(1)}, f32[432,128]{1,0:T(8,128)S(1)}, u32[]{:S(2)}, u32[]{:S(2)}) collective-permute-start(f32[432,128]{1,0:T(8,128)S(1)} %pad_maximum_fusion.4), channel_id=1, source_target_pairs={{0,4},{2,6},{4,8},{5,1},{6,10},{7,3},{8,12},{9,5},{10,14},{11,7},{... | collective-permute-start | bytes 663560 | tf_op jit(solution)/shard_map/ppermute | solution.py:469

commit v6 on v5

--- a/solution.py
+++ b/solution.py
@@ -13,6 +13,8 @@
 SECTION_B = (1432997174477.0 / 9575080441755.0, 5161836677717.0 / 13612068292357.0)
 UNIT = 144
 LANES = 128
+NEAR_ROWS = 640
+ALL_ROWS = 1664
 VMEM_LIMIT = 24 * 1024 * 1024
 
 
@@ -112,8 +114,8 @@
     return out[:rows] + out[rows:]
 
 
-def write_table(u_ref, t_ref):
-    for f in range(6):
+def write_table(u_ref, t_ref, fields=range(6)):
+    for f in fields:
         base = 64 * f
         rows = slice(16 * f, 16 * f + 16)
         t_ref[rows, 0:128] = u_ref[base : base + 16, :]
@@ -158,16 +160,23 @@
 
 
 def lists_kernel(
-    core_ref, u_hbm, send_hbm, swap_ref, own_ref, t_ref, u_ref, send_ref, send_sem, u_sem
+    core_ref, u_hbm, send_hbm, swap_ref, own_ref, t_ref, u_ref, send_ref, send_sem, u_sems
 ):
     send_copy = pltpu.make_async_copy(send_hbm, send_ref, send_sem)
-    u_copy = pltpu.make_async_copy(u_hbm, u_ref, u_sem)
     send_copy.start()
-    u_copy.start()
+    u_copies = [
+        pltpu.make_async_copy(
+            u_hbm.at[pl.ds(64 * f, 64)], u_ref.at[pl.ds(64 * f, 64)], u_sems.at[f]
+        )
+        for f in range(6)
+    ]
+    for copy in u_copies:
+        copy.start()
     send_copy.wait()
     spread = list_spread(core_ref[0], send_ref)
-    u_copy.wait()
-    write_table(u_ref, t_ref)
+    for f, copy in enumerate(u_copies):
+        copy.wait()
+        write_table(u_ref, t_ref, [f])
     write_lists(t_ref, spread, swap_ref, own_ref)
 
 
@@ -215,7 +224,7 @@
     at = received_column(core, face_ref[...])
     columns = [at[face : face + 1, :] for face in range(6)]
     columns.append(received_column(core, mortar_row(mortar_ref)))
-    spread_ref[...] = jnp.concatenate([one_hot(1536, column) for column in columns], axis=1)
+    spread_ref[...] = jnp.concatenate([one_hot(ALL_ROWS, column) for column in columns], axis=1)
     target = jnp.concatenate([target_ref[...]] * 4, axis=1)
     place_ref[...] = one_hot(768, target)
     face = jnp.zeros_like(target)
@@ -232,30 +241,37 @@
     scale_ref[...] = STEP_SIZE * metric * material_ref[...]
 
 
-def write_received(core, swapped_ref, near_ref, far_ref, shared_ref, r_ref):
-    other = 1 - core
-    swapped = pl.multiple_of(other * (5 * UNIT) + 4 * UNIT, 8)
-    shared = [pl.multiple_of(other * (3 * UNIT) + UNIT * place, 8) for place in range(3)]
-    sources = [
-        (shared_ref, shared[2]),
-        (shared_ref, shared[0]),
-        (shared_ref, shared[1]),
-        (swapped_ref, swapped),
-        (near_ref, UNIT),
-        (near_ref, 0),
-        (far_ref, UNIT),
-        (far_ref, 0),
-    ]
+def write_units(sources, r_ref):
+    count = len(sources)
     first = lax.broadcasted_iota(jnp.int32, (48, LANES), 1) < 64
+    none = jnp.zeros((48, LANES), jnp.float32)
     rests = []
     for k, (ref, start) in enumerate(sources):
         r_ref[:, 128 * k : 128 * k + 128] = ref[pl.ds(start, 96), :]
         rests.append(ref[pl.ds(start + 96, 48), :])
-    for pair in range(4):
-        even, odd = rests[2 * pair], rests[2 * pair + 1]
-        at = 1024 + 128 * pair
+    for k in range(0, count, 2):
+        even, odd = rests[k], rests[k + 1] if k + 1 < count else none
+        at = 128 * count + 64 * k
         r_ref[0:48, at : at + 128] = jnp.where(first, even, pltpu.roll(odd, 64, 1))
         r_ref[48:96, at : at + 128] = jnp.where(first, pltpu.roll(even, 64, 1), odd)
+
+
+def near_kernel(core_ref, part_ref, spread_ref, swapped_ref, near_ref, out_ref, give_ref, r_ref):
+    swapped = pl.multiple_of((1 - core_ref[0]) * (5 * UNIT) + 4 * UNIT, 8)
+    write_units([(swapped_ref, swapped), (near_ref, UNIT), (near_ref, 0)], r_ref)
+    out_ref[...] = part_ref[...] + picked(r_ref[...], spread_ref[0:NEAR_ROWS, :])
+    give_ref[...] = near_ref[2 * UNIT : 4 * UNIT, :]
+
+
+def join_kernel(give_ref, far_ref, out_ref):
+    out_ref[0 : 2 * UNIT, :] = give_ref[...]
+    out_ref[2 * UNIT : 3 * UNIT, :] = far_ref[2 * UNIT : 3 * UNIT, :]
+
+
+def write_far(core, far_ref, shared_ref, r_ref):
+    shared = [pl.multiple_of((1 - core) * (3 * UNIT) + UNIT * place, 8) for place in range(3)]
+    sources = [(shared_ref, shared[place]) for place in (2, 0, 1)]
+    write_units(sources + [(far_ref, UNIT), (far_ref, 0)], r_ref)
 
 
 def received_column(core, source):
@@ -265,8 +281,11 @@
         list_at = list_at + jnp.where(remote >= 192 * k, 1, 0)
     slot = remote - 192 * list_at
     seen = list_at + core * (7 - 2 * list_at)
-    rest = 1024 + 64 * seen + slot - 128
-    return jnp.where(remote < 0, -1, jnp.where(slot < 128, 128 * seen + slot, rest))
+    near = (seen >= 3) & (seen < 6)
+    place = jnp.where(seen < 3, seen, seen - 3)
+    main = jnp.where(near, 0, NEAR_ROWS) + 128 * place + slot
+    rest = jnp.where(near, 384, NEAR_ROWS + 640) + 64 * place + slot - 128
+    return jnp.where(remote < 0, -1, jnp.where(slot < 128, main, rest))
 
 
 def turned(nodes, code):
@@ -401,22 +420,27 @@
     core_ref, u_ref = refs[0:2]
     del refs[0:2]
     register_ref = refs.pop(0) if section else None
-    rate_in_ref, part_ref, swapped_ref, near_ref, far_ref, shared_ref = refs[0:6]
-    spread_ref, place_ref, codes_ref, scale_ref = refs[6:10]
-    del refs[0:10]
+    rate_in_ref, part_ref, far_ref, shared_ref = refs[0:4]
+    spread_ref, place_ref, codes_ref, scale_ref = refs[4:8]
+    del refs[0:8]
     list_spread_ref = None if section else refs.pop(0)
-    new_u_ref, new_register_ref = refs[0:2]
+    outs = refs[0:2]
     del refs[0:2]
     if section == 0:
         swap_ref, own_ref = refs[0:2]
         del refs[0:2]
+        new_u_ref, new_register_ref = outs
+    else:
+        new_u_ref, new_register_ref, sems = refs[0:3]
+        del refs[0:3]
     r_ref, g_ref, m_ref, rate_ref, t_ref = refs
     core = core_ref[0]
-    write_received(core, swapped_ref, near_ref, far_ref, shared_ref, r_ref)
-    gathered = part_ref[...] + picked(r_ref[...], spread_ref[...])
+    write_far(core, far_ref, shared_ref, r_ref)
+    gathered = part_ref[...] + picked(r_ref[...], spread_ref[NEAR_ROWS:ALL_ROWS, :])
     exterior(gathered, codes_ref, place_ref, g_ref, m_ref)
     rate_ref[...] = rate_in_ref[...]
     add_lift(rate_ref, g_ref)
+    copies = []
     for half in range(2):
         rows = slice(192 * half, 192 * half + 192)
         register = scale_ref[half : half + 1, :] * rate_ref[rows, :]
@@ -424,6 +448,17 @@
             register = register + SECTION_A[section] * register_ref[rows, :]
         new_register_ref[rows, :] = register
         new_u_ref[rows, :] = u_ref[rows, :] + SECTION_B[section] * register
+        if section:
+            for f in range(3 * half, 3 * half + 3):
+                for which, ref in enumerate((new_u_ref, new_register_ref)):
+                    rows = pl.ds(64 * f, 64)
+                    copy = pltpu.make_async_copy(
+                        ref.at[rows], outs[which].at[rows], sems.at[2 * f + which]
+                    )
+                    copy.start()
+                    copies.append(copy)
+    for copy in copies:
+        copy.wait()
     if section == 0:
         write_table(new_u_ref, t_ref)
         write_lists(t_ref, list_spread_ref[...], swap_ref, own_ref)
@@ -433,13 +468,13 @@
     return jax.ShapeDtypeStruct((rows, columns), dtype)
 
 
-def called(kernel, core, operands, outputs, scratch, space=pltpu.VMEM):
+def called(kernel, core, operands, outputs, scratch, space=pltpu.VMEM, out=pltpu.VMEM):
     first = [] if core is None else [pl.BlockSpec(memory_space=pltpu.SMEM)]
     given = list(operands) if core is None else [core, *operands]
     return pl.pallas_call(
         kernel,
         in_specs=first + [pl.BlockSpec(memory_space=space)] * len(operands),
-        out_specs=[pl.BlockSpec(memory_space=pltpu.VMEM)] * len(outputs),
+        out_specs=[pl.BlockSpec(memory_space=out)] * len(outputs),
         out_shape=outputs,
         scratch_shapes=[
             pltpu.VMEM(shape, jnp.float32) if isinstance(shape, tuple) else shape
@@ -452,7 +487,7 @@
 LIST_OUTPUTS = [shaped(5 * UNIT), shaped(3 * UNIT)]
 
 
-def exchanged(core, swap, own):
+def exchanged(core, swap, own, gather_near):
     count = lax.axis_size("sfc")
     pairs = [[2 * chip, 2 * chip + 1] for chip in range(count // 2)]
 
@@ -467,9 +502,10 @@
     far = jnp.concatenate([own[2 * u : 3 * u], theirs[2 * u : 4 * u]])
     near = lax.ppermute(near, "sfc", ahead(1))
     far = lax.ppermute(far, "sfc", ahead(2))
-    shared = jnp.concatenate([near[2 * u : 4 * u], far[2 * u : 3 * u]])
+    part, give = gather_near(swapped, near)
+    (shared,) = called(join_kernel, None, [give, far], [shaped(3 * u)], [])
     shared = lax.all_gather(shared, "sfc", axis_index_groups=pairs, tiled=True)
-    return swapped, near, far, shared
+    return part, far, shared
 
 
 def local(
@@ -503,13 +539,12 @@
             (384, LANES),
             pltpu.VMEM((8, 192), jnp.int32),
             pltpu.SemaphoreType.DMA,
-            pltpu.SemaphoreType.DMA,
+            pltpu.SemaphoreType.DMA((6,)),
         ],
         space=pltpu.HBM,
     )
     register = None
     for section in range(2):
-        received = exchanged(core, swap, own)
         if section == 0:
             rate, part, list_spread_made, *made = called(
                 first_kernel,
@@ -530,7 +565,7 @@
                     shaped(384),
                     shaped(96, 1024),
                     shaped(768, 1536, jnp.bfloat16),
-                    shaped(1536, 1024, jnp.bfloat16),
+                    shaped(ALL_ROWS, 1024, jnp.bfloat16),
                     shaped(768, 256, jnp.bfloat16),
                     shaped(16, LANES, jnp.int32),
                     shaped(2, LANES),
@@ -545,9 +580,19 @@
                 [shaped(384), shaped(96, 1024)],
                 [table],
             )
+
+        def gather_near(swapped, near, part=part):
+            operands = [part, made[0], swapped, near]
+            outputs = [shaped(96, 1024), shaped(2 * UNIT)]
+            return called(near_kernel, core_at, operands, outputs, [(96, NEAR_ROWS)])
+
+        part, far, shared = exchanged(core, swap, own, gather_near)
         operands = [solution] + ([register] if section else [])
-        operands += [rate, part, *received, *made]
+        operands += [rate, part, far, shared, *made]
         outputs = [shaped(384), shaped(384)]
+        scratch = [(96, ALL_ROWS - NEAR_ROWS), (192, LANES), (64, LANES), (384, LANES), table]
+        if section:
+            scratch = [(384, LANES), (384, LANES), pltpu.SemaphoreType.DMA((12,)), *scratch]
         if section == 0:
             operands.append(list_spread_made)
             outputs = outputs + LIST_OUTPUTS
@@ -560,7 +605,8 @@
             core_at,
             operands,
             outputs,
-            [(96, 1536), (192, LANES), (64, LANES), (384, LANES), table],
+            scratch,
+            out=pltpu.HBM if section else pltpu.VMEM,
         )
         solution, register = results[0:2]
         if section == 0:

time: 57.6 us -> 57.4 us (level)
  waiting for transfers between devices: 7.42 us -> 5.86 us
  Pallas kernels: 9.64 us -> 10.6 us
    ppermute x2, waiting for transfers between devices: 7.42 us -> 4.86 us  [exchanged(): far = lax.ppermute(far, 'sfc', ahead(2))]
    ppermute x2, waiting for transfers between devices: 0.01 us -> 1 us  [exchanged(): near = lax.ppermute(near, 'sfc', ahead(1))]
    pallas_call x5 -> x9, Pallas kernels: 9.64 us -> 10.6 us  [called(): pl.pallas_call(kernel, in_specs=first + [pl.BlockSpec(memory_space=space)...]
  transfers between devices with their start and end apart: 4 -> 4, of which waited for: 2 -> 3; matrix products, arithmetic and copies ran while one was open for 0% -> 0% of each run, Pallas kernels for 6% -> 8%
where the time goes in v6:
time: 57.4 us; the launch traced here: 57.1 us
  starting transfers between devices  25.5 us (44%)
  blocking collectives  14 us (24%)
  Pallas kernels  10.6 us (18%)
  waiting for transfers between devices  5.86 us (10%)
  between operations  0.97 us (2%)
    ppermute x2, starting transfers between devices, exchanged(): near = lax.ppermute(near, 'sfc', ahead(1))  20.5 us
    pallas_call x9, Pallas kernels, called(): pl.pallas_call(kernel, in_specs=first + [pl.BlockSpec(memory_space=space)...  10.6 us
    all_gather x2, blocking collectives, exchanged(): shared = lax.all_gather(shared, 'sfc', axis_index_groups=pairs, tiled=True)  9 us
    ppermute x2, starting transfers between devices, exchanged(): far = lax.ppermute(far, 'sfc', ahead(2))  5 us
    all_gather x2, blocking collectives, exchanged(): swapped = lax.all_gather(swap, 'sfc', axis_index_groups=pairs, tiled=True)  4.96 us
    ppermute x2, waiting for transfers between devices, exchanged(): far = lax.ppermute(far, 'sfc', ahead(2))  4.86 us
  transfers between devices with their start and end apart: 4, of which 3 were waited for; matrix products, arithmetic and copies ran while one was open for 0% of the time, Pallas kernels for 8%

profile of v6, /device:TPU:7, one launch (start us, length us, event | category | flops | bytes accessed | tf_op | source)
XLA Modules:
  0.0 57.1 jit_solution(6149058267966881217)
XLA Ops:
  0.6 0.0 copy-start
  0.6 0.0 copy-start.1
  0.7 0.0 copy-start.2
  0.7 0.0 copy-start.8
  0.7 0.0 copy-start.9
  0.7 0.0 copy-start.7
  0.7 0.0 copy-start.3
  0.7 0.0 copy-start.5
  0.7 0.0 copy-start.4
  0.7 0.0 copy-start.6
  0.7 2.3 %shard_map.114 = (f32[720,128]{1,0:T(8,128)S(1)}, f32[432,128]{1,0:T(8,128)S(1)}) custom-call(s32[1]{0:T(128)} %bitcast.core_ref.refs_0_, f32[384,128]{1,0:T(8,128)} %bitcast.6, s32[8,192]{1,0:T(8,128)} %send_hbm.1), custom_call_target="tpu_custom_call" | custom-call | tf_op jit(solution)/shard_map/pallas_call | solution.py:474
  3.0 2.6 %all_gather.12.swapped_ref = f32[1440,128]{1,0:T(8,128)S(1)} all-gather(f32[720,128]{1,0:T(8,128)S(1)} %get-tuple-element.26), channel_id=1, replica_groups={{0,1},{2,3},{4,5},{6,7},{8,9},{10,11},{12,13},{14,15},{16,17},{18,19},{..., dimensions={0}, use_global_device_ids=true | all-gather | bytes 1105920 | tf_op jit(solution)/shard_map/all_gather | solution.py:498
  5.7 13.8 %collective-permute-start = (f32[576,128]{1,0:T(8,128)S(1)}, f32[576,128]{1,0:T(8,128)S(1)}, u32[]{:S(2)}, u32[]{:S(2)}) collective-permute-start(f32[576,128]{1,0:T(8,128)S(1)} %pad_maximum_fusion), channel_id=1, source_target_pairs={{0,2},{2,4},{3,1},{4,6},{5,3},{6,8},{7,5},{8,10},{9,7},{10,12},{11... | collective-permute-start | bytes 884744 | tf_op jit(solution)/shard_map/ppermute | solution.py:503
  19.6 3.1 %collective-permute-start.1 = (f32[432,128]{1,0:T(8,128)S(1)}, f32[432,128]{1,0:T(8,128)S(1)}, u32[]{:S(2)}, u32[]{:S(2)}) collective-permute-start(f32[432,128]{1,0:T(8,128)S(1)} %pad_maximum_fusion.2), channel_id=1, source_target_pairs={{0,4},{2,6},{4,8},{5,1},{6,10},{7,3},{8,12},{9,5},{10,14},{11,7},{... | collective-permute-start | bytes 663560 | tf_op jit(solution)/shard_map/ppermute | solution.py:504
  22.7 0.0 copy-done
  22.7 0.0 copy-done.1
  22.8 0.0 copy-done.2
  22.8 0.0 copy-done.8
  22.8 0.0 copy-done.9
  22.8 0.0 copy-done.7
  22.8 0.0 copy-done.3
  22.8 0.0 copy-done.5
  22.8 0.0 copy-done.4
  22.8 0.0 copy-done.6
  22.8 3.1 %shard_map.113 = (f32[384,128]{1,0:T(8,128)S(1)}, f32[96,1024]{1,0:T(8,128)S(1)}, bf16[768,1536]{1,0:T(8,128)(2,1)S(1)}, bf16[1664,1024]{1,0:T(8,128)(2,1)S(1)},...) custom-call(s32[1]{0:T(128)} %bitcast.core_ref.refs_0_, f32[384,128]{1,0:T(8,128)S(1)} %bitcast.7, ...), custom_call_target="tpu_custom_call" | custom-call | tf_op jit(solution)/shard_map/pallas_call | solution.py:474
  26.0 0.0 collective-permute-done.near_ref
  26.0 0.5 shard_map.115
  26.5 1.1 %collective-permute-done.1.far_ref.refs_4_ = f32[432,128]{1,0:T(8,128)S(1)} collective-permute-done((f32[432,128]{1,0:T(8,128)S(1)}, f32[432,128]{1,0:T(8,128)S(1)}, u32[]{:S(2)}, u32[]{:S(2)}) %collective-permute-start.1) | collective-permute-done | bytes 221216 | tf_op jit(solution)/shard_map/ppermute | solution.py:504
  27.6 4.4 %all_gather.13.refs_5_ = f32[864,128]{1,0:T(8,128)S(1)} all-gather(f32[432,128]{1,0:T(8,128)S(1)} %shard_map.116), channel_id=1, replica_groups={{0,1},{2,3},{4,5},{6,7},{8,9},{10,11},{12,13},{14,15},{16,17},{18,19},{..., dimensions={0}, use_global_device_ids=true | all-gather | bytes 663552 | tf_op jit(solution)/shard_map/all_gather | solution.py:507
  32.0 1.7 %shard_map.117 = (f32[384,128]{1,0:T(8,128)S(1)}, f32[384,128]{1,0:T(8,128)S(1)}, f32[720,128]{1,0:T(8,128)S(1)}, f32[432,128]{1,0:T(8,128)S(1)}) custom-call(s32[1]{0:T(128)} %bitcast.core_ref.refs_0_, f32[384,128]{1,0:T(8,128)S(1)} %bitcast.8, f32[384,128]{1,0:T(8,128)S(1)} %get-tuple-element.23.refs_2_, f32[96,1024]{1,0:T(8,128)S(1)} %get-tuple-element.28.refs_3_, ...), custom_call_target="tpu_custom_call" | custom-call | tf_op jit(solution)/shard_map/pallas_call | solution.py:474
  33.6 2.3 %all_gather.14.swapped_ref = f32[1440,128]{1,0:T(8,128)S(1)} all-gather(f32[720,128]{1,0:T(8,128)S(1)} %get-tuple-element.38), channel_id=1, replica_groups={{0,1},{2,3},{4,5},{6,7},{8,9},{10,11},{12,13},{14,15},{16,17},{18,19},{..., dimensions={0}, use_global_device_ids=true | all-gather | bytes 1105920 | tf_op jit(solution)/shard_map/all_gather | solution.py:498
  36.1 6.6 %collective-permute-start.2 = (f32[576,128]{1,0:T(8,128)S(1)}, f32[576,128]{1,0:T(8,128)S(1)}, u32[]{:S(2)}, u32[]{:S(2)}) collective-permute-start(f32[576,128]{1,0:T(8,128)S(1)} %pad_maximum_fusion.1), channel_id=1, source_target_pairs={{0,2},{2,4},{3,1},{4,6},{5,3},{6,8},{7,5},{8,10},{9,7},{10,12},{11... | collective-permute-start | bytes 884744 | tf_op jit(solution)/shard_map/ppermute | solution.py:503
  42.7 1.9 %collective-permute-start.3 = (f32[432,128]{1,0:T(8,128)S(1)}, f32[432,128]{1,0:T(8,128)S(1)}, u32[]{:S(2)}, u32[]{:S(2)}) collective-permute-start(f32[432,128]{1,0:T(8,128)S(1)} %pad_maximum_fusion.3), channel_id=1, source_target_pairs={{0,4},{2,6},{4,8},{5,1},{6,10},{7,3},{8,12},{9,5},{10,14},{11,7},{... | collective-permute-start | bytes 663560 | tf_op jit(solution)/shard_map/ppermute | solution.py:504
  44.6 0.7 %shard_map.118 = (f32[384,128]{1,0:T(8,128)S(1)}, f32[96,1024]{1,0:T(8,128)S(1)}) custom-call(f32[384,128]{1,0:T(8,128)S(1)} %get-tuple-element.34.u_ref.refs_1_, bf16[384,1152]{1,0:T(8,128)(2,1)S(1)} %copy-done, s32[6,128]{1,0:T(8,128)S(1)} %copy-done.3, s32[4,64]{1,0:T(4,128)S(1)} %copy-done.4), custom_call_target="tpu_custom_call" | custom-call | tf_op jit(solution)/shard_map/pallas_call | solution.py:474
  45.3 1.0 %collective-permute-done.2.near_ref = f32[576,128]{1,0:T(8,128)S(1)} collective-permute-done((f32[576,128]{1,0:T(8,128)S(1)}, f32[576,128]{1,0:T(8,128)S(1)}, u32[]{:S(2)}, u32[]{:S(2)}) %collective-permute-start.2) | collective-permute-done | bytes 294944 | tf_op jit(solution)/shard_map/ppermute | solution.py:503
  46.3 0.5 shard_map.119
  46.8 3.8 %collective-permute-done.3.far_ref.refs_5_ = f32[432,128]{1,0:T(8,128)S(1)} collective-permute-done((f32[432,128]{1,0:T(8,128)S(1)}, f32[432,128]{1,0:T(8,128)S(1)}, u32[]{:S(2)}, u32[]{:S(2)}) %collective-permute-start.3) | collective-permute-done | bytes 221216 | tf_op jit(solution)/shard_map/ppermute | solution.py:504
  50.6 4.6 %all_gather.15.refs_6_ = f32[864,128]{1,0:T(8,128)S(1)} all-gather(f32[432,128]{1,0:T(8,128)S(1)} %shard_map.120), channel_id=1, replica_groups={{0,1},{2,3},{4,5},{6,7},{8,9},{10,11},{12,13},{14,15},{16,17},{18,19},{..., dimensions={0}, use_global_device_ids=true | all-gather | bytes 663552 | tf_op jit(solution)/shard_map/all_gather | solution.py:507
  55.3 1.8 %shard_map.121 = (f32[384,128]{1,0:T(8,128)}, f32[384,128]{1,0:T(8,128)}) custom-call(s32[1]{0:T(128)} %bitcast.core_ref.refs_0_, f32[384,128]{1,0:T(8,128)S(1)} %get-tuple-element.34.u_ref.refs_1_, f32[384,128]{1,0:T(8,128)S(1)} %get-tuple-element.35.refs_2_, f32[384,128]{1,0:T(8,128)S(1)} %get-tuple-element.36.refs_3_, ...), custom_call_target="tpu_custom_call" | custom-call | tf_op jit(solution)/shard_map/pallas_call | solution.py:474
  (12 shorter events, 0.2 us)
Async XLA Ops:
  0.6 22.1 %copy-start = (bf16[384,1152]{1,0:T(8,128)(2,1)S(1)}, bf16[384,1152]{1,0:T(8,128)(2,1)}, u32[]{:S(2)}) copy-start(bf16[384,1152]{1,0:T(8,128)(2,1)} %constant.17.clone.volume_ref) | copy-start | bytes 2654212
  0.6 22.1 %copy-start.1 = (f32[6,64,128]{2,1,0:T(8,128)S(1)}, f32[6,64,128]{2,1,0:T(8,128)}, u32[]{:S(2)}) copy-start(f32[6,64,128]{2,1,0:T(8,128)} %param.10) | copy-start | bytes 589828
  0.7 22.1 %copy-start.2 = (s32[8,192]{1,0:T(8,128)S(1)}, s32[8,192]{1,0:T(8,128)}, u32[]{:S(2)}) copy-start(s32[8,192]{1,0:T(8,128)} %send_hbm.1) | copy-start | bytes 18436
  0.7 22.1 %copy-start.8 = (s32[64]{0:T(128)S(1)}, s32[64]{0:T(128)}, u32[]{:S(2)}) copy-start(s32[64]{0:T(128)} %param.18) | copy-start | bytes 772
  0.7 22.1 %copy-start.9 = (s32[128]{0:T(128)S(1)}, s32[128]{0:T(128)}, u32[]{:S(2)}) copy-start(s32[128]{0:T(128)} %param.12) | copy-start | bytes 1540
  0.7 22.1 %copy-start.7 = (f32[2,128]{1,0:T(2,128)S(1)}, f32[2,128]{1,0:T(2,128)}, u32[]{:S(2)}) copy-start(f32[2,128]{1,0:T(2,128)} %material_ref.1) | copy-start | bytes 3076
  0.7 22.1 %copy-start.3 = (s32[6,128]{1,0:T(8,128)S(1)}, s32[6,128]{1,0:T(8,128)}, u32[]{:S(2)}) copy-start(s32[6,128]{1,0:T(8,128)} %face_ref.3) | copy-start | bytes 9220
  0.7 22.1 %copy-start.5 = (s32[6,128]{1,0:T(8,128)S(1)}, s32[6,128]{1,0:T(8,128)}, u32[]{:S(2)}) copy-start(s32[6,128]{1,0:T(8,128)} %code_ref.1) | copy-start | bytes 9220
  0.7 22.1 %copy-start.4 = (s32[4,64]{1,0:T(4,128)S(1)}, s32[4,64]{1,0:T(4,128)}, u32[]{:S(2)}) copy-start(s32[4,64]{1,0:T(4,128)} %mortar_ref.3) | copy-start | bytes 3076
  0.7 22.1 %copy-start.6 = (s32[4,64]{1,0:T(4,128)S(1)}, s32[4,64]{1,0:T(4,128)}, u32[]{:S(2)}) copy-start(s32[4,64]{1,0:T(4,128)} %mortar_code_ref.1) | copy-start | bytes 3076
  5.7 20.2 %collective-permute-start = (f32[576,128]{1,0:T(8,128)S(1)}, f32[576,128]{1,0:T(8,128)S(1)}, u32[]{:S(2)}, u32[]{:S(2)}) collective-permute-start(f32[576,128]{1,0:T(8,128)S(1)} %pad_maximum_fusion), channel_id=1, source_target_pairs={{0,2},{2,4},{3,1},{4,6},{5,3},{6,8},{7,5},{8,10},{9,7},{10,12},{11... | collective-permute-start | bytes 884744 | tf_op jit(solution)/shard_map/ppermute | solution.py:503
  19.6 7.9 %collective-permute-start.1 = (f32[432,128]{1,0:T(8,128)S(1)}, f32[432,128]{1,0:T(8,128)S(1)}, u32[]{:S(2)}, u32[]{:S(2)}) collective-permute-start(f32[432,128]{1,0:T(8,128)S(1)} %pad_maximum_fusion.2), channel_id=1, source_target_pairs={{0,4},{2,6},{4,8},{5,1},{6,10},{7,3},{8,12},{9,5},{10,14},{11,7},{... | collective-permute-start | bytes 663560 | tf_op jit(solution)/shard_map/ppermute | solution.py:504
  36.1 10.3 %collective-permute-start.2 = (f32[576,128]{1,0:T(8,128)S(1)}, f32[576,128]{1,0:T(8,128)S(1)}, u32[]{:S(2)}, u32[]{:S(2)}) collective-permute-start(f32[576,128]{1,0:T(8,128)S(1)} %pad_maximum_fusion.1), channel_id=1, source_target_pairs={{0,2},{2,4},{3,1},{4,6},{5,3},{6,8},{7,5},{8,10},{9,7},{10,12},{11... | collective-permute-start | bytes 884744 | tf_op jit(solution)/shard_map/ppermute | solution.py:503
  42.7 7.9 %collective-permute-start.3 = (f32[432,128]{1,0:T(8,128)S(1)}, f32[432,128]{1,0:T(8,128)S(1)}, u32[]{:S(2)}, u32[]{:S(2)}) collective-permute-start(f32[432,128]{1,0:T(8,128)S(1)} %pad_maximum_fusion.3), channel_id=1, source_target_pairs={{0,4},{2,6},{4,8},{5,1},{6,10},{7,3},{8,12},{9,5},{10,14},{11,7},{... | collective-permute-start | bytes 663560 | tf_op jit(solution)/shard_map/ppermute | solution.py:504

commit v7 on v6

--- a/solution.py
+++ b/solution.py
@@ -160,23 +160,16 @@
 
 
 def lists_kernel(
-    core_ref, u_hbm, send_hbm, swap_ref, own_ref, t_ref, u_ref, send_ref, send_sem, u_sems
+    core_ref, u_hbm, send_hbm, swap_ref, own_ref, t_ref, u_ref, send_ref, send_sem, u_sem
 ):
     send_copy = pltpu.make_async_copy(send_hbm, send_ref, send_sem)
     send_copy.start()
-    u_copies = [
-        pltpu.make_async_copy(
-            u_hbm.at[pl.ds(64 * f, 64)], u_ref.at[pl.ds(64 * f, 64)], u_sems.at[f]
-        )
-        for f in range(6)
-    ]
-    for copy in u_copies:
-        copy.start()
+    u_copy = pltpu.make_async_copy(u_hbm, u_ref, u_sem)
+    u_copy.start()
     send_copy.wait()
     spread = list_spread(core_ref[0], send_ref)
-    for f, copy in enumerate(u_copies):
-        copy.wait()
-        write_table(u_ref, t_ref, [f])
+    u_copy.wait()
+    write_table(u_ref, t_ref)
     write_lists(t_ref, spread, swap_ref, own_ref)
 
 
@@ -449,14 +442,13 @@
         new_register_ref[rows, :] = register
         new_u_ref[rows, :] = u_ref[rows, :] + SECTION_B[section] * register
         if section:
-            for f in range(3 * half, 3 * half + 3):
-                for which, ref in enumerate((new_u_ref, new_register_ref)):
-                    rows = pl.ds(64 * f, 64)
-                    copy = pltpu.make_async_copy(
-                        ref.at[rows], outs[which].at[rows], sems.at[2 * f + which]
-                    )
-                    copy.start()
-                    copies.append(copy)
+            for which, ref in enumerate((new_u_ref, new_register_ref)):
+                rows = pl.ds(192 * half, 192)
+                copy = pltpu.make_async_copy(
+                    ref.at[rows], outs[which].at[rows], sems.at[2 * half + which]
+                )
+                copy.start()
+                copies.append(copy)
     for copy in copies:
         copy.wait()
     if section == 0:
@@ -539,7 +531,7 @@
             (384, LANES),
             pltpu.VMEM((8, 192), jnp.int32),
             pltpu.SemaphoreType.DMA,
-            pltpu.SemaphoreType.DMA((6,)),
+            pltpu.SemaphoreType.DMA,
         ],
         space=pltpu.HBM,
     )
@@ -592,7 +584,7 @@
         outputs = [shaped(384), shaped(384)]
         scratch = [(96, ALL_ROWS - NEAR_ROWS), (192, LANES), (64, LANES), (384, LANES), table]
         if section:
-            scratch = [(384, LANES), (384, LANES), pltpu.SemaphoreType.DMA((12,)), *scratch]
+            scratch = [(384, LANES), (384, LANES), pltpu.SemaphoreType.DMA((4,)), *scratch]
         if section == 0:
             operands.append(list_spread_made)
             outputs = outputs + LIST_OUTPUTS

time: 57.4 us -> 57.2 us (level)
  no operation moved by 1% of the time
where the time goes in v7:
time: 57.2 us; the launch traced here: 56.9 us
  starting transfers between devices  25.5 us (45%)
  blocking collectives  14 us (24%)
  Pallas kernels  10.4 us (18%)
  waiting for transfers between devices  5.86 us (10%)
  between operations  0.97 us (2%)
    ppermute x2, starting transfers between devices, exchanged(): near = lax.ppermute(near, 'sfc', ahead(1))  20.5 us
    pallas_call x9, Pallas kernels, called(): pl.pallas_call(kernel, in_specs=first + [pl.BlockSpec(memory_space=space)...  10.4 us
    all_gather x2, blocking collectives, exchanged(): shared = lax.all_gather(shared, 'sfc', axis_index_groups=pairs, tiled=True)  9.03 us
    ppermute x2, starting transfers between devices, exchanged(): far = lax.ppermute(far, 'sfc', ahead(2))  5 us
    all_gather x2, blocking collectives, exchanged(): swapped = lax.all_gather(swap, 'sfc', axis_index_groups=pairs, tiled=True)  4.97 us
    ppermute x2, waiting for transfers between devices, exchanged(): far = lax.ppermute(far, 'sfc', ahead(2))  4.86 us
  transfers between devices with their start and end apart: 4, of which 3 were waited for; matrix products, arithmetic and copies ran while one was open for 0% of the time, Pallas kernels for 8%

profile of v7, /device:TPU:7, one launch (start us, length us, event | category | flops | bytes accessed | tf_op | source)
XLA Modules:
  0.0 56.9 jit_solution(1093951838154046624)
XLA Ops:
  0.6 0.0 copy-start
  0.6 0.0 copy-start.1
  0.7 0.0 copy-start.2
  0.7 0.0 copy-start.8
  0.7 0.0 copy-start.9
  0.7 0.0 copy-start.7
  0.7 0.0 copy-start.3
  0.7 0.0 copy-start.5
  0.7 0.0 copy-start.4
  0.7 0.0 copy-start.6
  0.7 2.1 %shard_map.114 = (f32[720,128]{1,0:T(8,128)S(1)}, f32[432,128]{1,0:T(8,128)S(1)}) custom-call(s32[1]{0:T(128)} %bitcast.core_ref.refs_0_, f32[384,128]{1,0:T(8,128)} %bitcast.6, s32[8,192]{1,0:T(8,128)} %send_hbm.1), custom_call_target="tpu_custom_call" | custom-call | tf_op jit(solution)/shard_map/pallas_call | solution.py:466
  2.9 2.6 %all_gather.12.swapped_ref = f32[1440,128]{1,0:T(8,128)S(1)} all-gather(f32[720,128]{1,0:T(8,128)S(1)} %get-tuple-element.26), channel_id=1, replica_groups={{0,1},{2,3},{4,5},{6,7},{8,9},{10,11},{12,13},{14,15},{16,17},{18,19},{..., dimensions={0}, use_global_device_ids=true | all-gather | bytes 1105920 | tf_op jit(solution)/shard_map/all_gather | solution.py:490
  5.6 13.8 %collective-permute-start = (f32[576,128]{1,0:T(8,128)S(1)}, f32[576,128]{1,0:T(8,128)S(1)}, u32[]{:S(2)}, u32[]{:S(2)}) collective-permute-start(f32[576,128]{1,0:T(8,128)S(1)} %pad_maximum_fusion), channel_id=1, source_target_pairs={{0,2},{2,4},{3,1},{4,6},{5,3},{6,8},{7,5},{8,10},{9,7},{10,12},{11... | collective-permute-start | bytes 884744 | tf_op jit(solution)/shard_map/ppermute | solution.py:495
  19.5 3.1 %collective-permute-start.1 = (f32[432,128]{1,0:T(8,128)S(1)}, f32[432,128]{1,0:T(8,128)S(1)}, u32[]{:S(2)}, u32[]{:S(2)}) collective-permute-start(f32[432,128]{1,0:T(8,128)S(1)} %pad_maximum_fusion.2), channel_id=1, source_target_pairs={{0,4},{2,6},{4,8},{5,1},{6,10},{7,3},{8,12},{9,5},{10,14},{11,7},{... | collective-permute-start | bytes 663560 | tf_op jit(solution)/shard_map/ppermute | solution.py:496
  22.6 0.0 copy-done
  22.6 0.0 copy-done.1
  22.6 0.0 copy-done.2
  22.6 0.0 copy-done.8
  22.6 0.0 copy-done.9
  22.6 0.0 copy-done.7
  22.6 0.0 copy-done.3
  22.7 0.0 copy-done.5
  22.7 0.0 copy-done.4
  22.7 0.0 copy-done.6
  22.7 3.1 %shard_map.113 = (f32[384,128]{1,0:T(8,128)S(1)}, f32[96,1024]{1,0:T(8,128)S(1)}, bf16[768,1536]{1,0:T(8,128)(2,1)S(1)}, bf16[1664,1024]{1,0:T(8,128)(2,1)S(1)},...) custom-call(s32[1]{0:T(128)} %bitcast.core_ref.refs_0_, f32[384,128]{1,0:T(8,128)S(1)} %bitcast.7, ...), custom_call_target="tpu_custom_call" | custom-call | tf_op jit(solution)/shard_map/pallas_call | solution.py:466
  25.8 0.0 collective-permute-done.near_ref
  25.8 0.5 shard_map.115
  26.3 1.1 %collective-permute-done.1.far_ref.refs_4_ = f32[432,128]{1,0:T(8,128)S(1)} collective-permute-done((f32[432,128]{1,0:T(8,128)S(1)}, f32[432,128]{1,0:T(8,128)S(1)}, u32[]{:S(2)}, u32[]{:S(2)}) %collective-permute-start.1) | collective-permute-done | bytes 221216 | tf_op jit(solution)/shard_map/ppermute | solution.py:496
  27.4 4.4 %all_gather.13.refs_5_ = f32[864,128]{1,0:T(8,128)S(1)} all-gather(f32[432,128]{1,0:T(8,128)S(1)} %shard_map.116), channel_id=1, replica_groups={{0,1},{2,3},{4,5},{6,7},{8,9},{10,11},{12,13},{14,15},{16,17},{18,19},{..., dimensions={0}, use_global_device_ids=true | all-gather | bytes 663552 | tf_op jit(solution)/shard_map/all_gather | solution.py:499
  31.8 1.7 %shard_map.117 = (f32[384,128]{1,0:T(8,128)S(1)}, f32[384,128]{1,0:T(8,128)S(1)}, f32[720,128]{1,0:T(8,128)S(1)}, f32[432,128]{1,0:T(8,128)S(1)}) custom-call(s32[1]{0:T(128)} %bitcast.core_ref.refs_0_, f32[384,128]{1,0:T(8,128)S(1)} %bitcast.8, f32[384,128]{1,0:T(8,128)S(1)} %get-tuple-element.23.refs_2_, f32[96,1024]{1,0:T(8,128)S(1)} %get-tuple-element.28.refs_3_, ...), custom_call_target="tpu_custom_call" | custom-call | tf_op jit(solution)/shard_map/pallas_call | solution.py:466
  33.4 2.3 %all_gather.14.swapped_ref = f32[1440,128]{1,0:T(8,128)S(1)} all-gather(f32[720,128]{1,0:T(8,128)S(1)} %get-tuple-element.38), channel_id=1, replica_groups={{0,1},{2,3},{4,5},{6,7},{8,9},{10,11},{12,13},{14,15},{16,17},{18,19},{..., dimensions={0}, use_global_device_ids=true | all-gather | bytes 1105920 | tf_op jit(solution)/shard_map/all_gather | solution.py:490
  35.9 6.7 %collective-permute-start.2 = (f32[576,128]{1,0:T(8,128)S(1)}, f32[576,128]{1,0:T(8,128)S(1)}, u32[]{:S(2)}, u32[]{:S(2)}) collective-permute-start(f32[576,128]{1,0:T(8,128)S(1)} %pad_maximum_fusion.1), channel_id=1, source_target_pairs={{0,2},{2,4},{3,1},{4,6},{5,3},{6,8},{7,5},{8,10},{9,7},{10,12},{11... | collective-permute-start | bytes 884744 | tf_op jit(solution)/shard_map/ppermute | solution.py:495
  42.6 1.9 %collective-permute-start.3 = (f32[432,128]{1,0:T(8,128)S(1)}, f32[432,128]{1,0:T(8,128)S(1)}, u32[]{:S(2)}, u32[]{:S(2)}) collective-permute-start(f32[432,128]{1,0:T(8,128)S(1)} %pad_maximum_fusion.3), channel_id=1, source_target_pairs={{0,4},{2,6},{4,8},{5,1},{6,10},{7,3},{8,12},{9,5},{10,14},{11,7},{... | collective-permute-start | bytes 663560 | tf_op jit(solution)/shard_map/ppermute | solution.py:496
  44.5 0.7 %shard_map.118 = (f32[384,128]{1,0:T(8,128)S(1)}, f32[96,1024]{1,0:T(8,128)S(1)}) custom-call(f32[384,128]{1,0:T(8,128)S(1)} %get-tuple-element.34.u_ref.refs_1_, bf16[384,1152]{1,0:T(8,128)(2,1)S(1)} %copy-done, s32[6,128]{1,0:T(8,128)S(1)} %copy-done.3, s32[4,64]{1,0:T(4,128)S(1)} %copy-done.4), custom_call_target="tpu_custom_call" | custom-call | tf_op jit(solution)/shard_map/pallas_call | solution.py:466
  45.2 1.0 %collective-permute-done.2.near_ref = f32[576,128]{1,0:T(8,128)S(1)} collective-permute-done((f32[576,128]{1,0:T(8,128)S(1)}, f32[576,128]{1,0:T(8,128)S(1)}, u32[]{:S(2)}, u32[]{:S(2)}) %collective-permute-start.2) | collective-permute-done | bytes 294944 | tf_op jit(solution)/shard_map/ppermute | solution.py:495
  46.2 0.5 shard_map.119
  46.7 3.8 %collective-permute-done.3.far_ref.refs_5_ = f32[432,128]{1,0:T(8,128)S(1)} collective-permute-done((f32[432,128]{1,0:T(8,128)S(1)}, f32[432,128]{1,0:T(8,128)S(1)}, u32[]{:S(2)}, u32[]{:S(2)}) %collective-permute-start.3) | collective-permute-done | bytes 221216 | tf_op jit(solution)/shard_map/ppermute | solution.py:496
  50.5 4.7 %all_gather.15.refs_6_ = f32[864,128]{1,0:T(8,128)S(1)} all-gather(f32[432,128]{1,0:T(8,128)S(1)} %shard_map.120), channel_id=1, replica_groups={{0,1},{2,3},{4,5},{6,7},{8,9},{10,11},{12,13},{14,15},{16,17},{18,19},{..., dimensions={0}, use_global_device_ids=true | all-gather | bytes 663552 | tf_op jit(solution)/shard_map/all_gather | solution.py:499
  55.2 1.8 %shard_map.121 = (f32[384,128]{1,0:T(8,128)}, f32[384,128]{1,0:T(8,128)}) custom-call(s32[1]{0:T(128)} %bitcast.core_ref.refs_0_, f32[384,128]{1,0:T(8,128)S(1)} %get-tuple-element.34.u_ref.refs_1_, f32[384,128]{1,0:T(8,128)S(1)} %get-tuple-element.35.refs_2_, f32[384,128]{1,0:T(8,128)S(1)} %get-tuple-element.36.refs_3_, ...), custom_call_target="tpu_custom_call" | custom-call | tf_op jit(solution)/shard_map/pallas_call | solution.py:466
  (12 shorter events, 0.2 us)
Async XLA Ops:
  0.6 21.9 %copy-start = (bf16[384,1152]{1,0:T(8,128)(2,1)S(1)}, bf16[384,1152]{1,0:T(8,128)(2,1)}, u32[]{:S(2)}) copy-start(bf16[384,1152]{1,0:T(8,128)(2,1)} %constant.17.clone.volume_ref) | copy-start | bytes 2654212
  0.6 21.9 %copy-start.1 = (f32[6,64,128]{2,1,0:T(8,128)S(1)}, f32[6,64,128]{2,1,0:T(8,128)}, u32[]{:S(2)}) copy-start(f32[6,64,128]{2,1,0:T(8,128)} %param.10) | copy-start | bytes 589828
  0.7 21.9 %copy-start.2 = (s32[8,192]{1,0:T(8,128)S(1)}, s32[8,192]{1,0:T(8,128)}, u32[]{:S(2)}) copy-start(s32[8,192]{1,0:T(8,128)} %send_hbm.1) | copy-start | bytes 18436
  0.7 21.9 %copy-start.8 = (s32[64]{0:T(128)S(1)}, s32[64]{0:T(128)}, u32[]{:S(2)}) copy-start(s32[64]{0:T(128)} %param.18) | copy-start | bytes 772
  0.7 21.9 %copy-start.9 = (s32[128]{0:T(128)S(1)}, s32[128]{0:T(128)}, u32[]{:S(2)}) copy-start(s32[128]{0:T(128)} %param.12) | copy-start | bytes 1540
  0.7 21.9 %copy-start.7 = (f32[2,128]{1,0:T(2,128)S(1)}, f32[2,128]{1,0:T(2,128)}, u32[]{:S(2)}) copy-start(f32[2,128]{1,0:T(2,128)} %material_ref.1) | copy-start | bytes 3076
  0.7 21.9 %copy-start.3 = (s32[6,128]{1,0:T(8,128)S(1)}, s32[6,128]{1,0:T(8,128)}, u32[]{:S(2)}) copy-start(s32[6,128]{1,0:T(8,128)} %face_ref.3) | copy-start | bytes 9220
  0.7 21.9 %copy-start.5 = (s32[6,128]{1,0:T(8,128)S(1)}, s32[6,128]{1,0:T(8,128)}, u32[]{:S(2)}) copy-start(s32[6,128]{1,0:T(8,128)} %code_ref.1) | copy-start | bytes 9220
  0.7 21.9 %copy-start.4 = (s32[4,64]{1,0:T(4,128)S(1)}, s32[4,64]{1,0:T(4,128)}, u32[]{:S(2)}) copy-start(s32[4,64]{1,0:T(4,128)} %mortar_ref.3) | copy-start | bytes 3076
  0.7 21.9 %copy-start.6 = (s32[4,64]{1,0:T(4,128)S(1)}, s32[4,64]{1,0:T(4,128)}, u32[]{:S(2)}) copy-start(s32[4,64]{1,0:T(4,128)} %mortar_code_ref.1) | copy-start | bytes 3076
  5.6 20.2 %collective-permute-start = (f32[576,128]{1,0:T(8,128)S(1)}, f32[576,128]{1,0:T(8,128)S(1)}, u32[]{:S(2)}, u32[]{:S(2)}) collective-permute-start(f32[576,128]{1,0:T(8,128)S(1)} %pad_maximum_fusion), channel_id=1, source_target_pairs={{0,2},{2,4},{3,1},{4,6},{5,3},{6,8},{7,5},{8,10},{9,7},{10,12},{11... | collective-permute-start | bytes 884744 | tf_op jit(solution)/shard_map/ppermute | solution.py:495
  19.5 7.9 %collective-permute-start.1 = (f32[432,128]{1,0:T(8,128)S(1)}, f32[432,128]{1,0:T(8,128)S(1)}, u32[]{:S(2)}, u32[]{:S(2)}) collective-permute-start(f32[432,128]{1,0:T(8,128)S(1)} %pad_maximum_fusion.2), channel_id=1, source_target_pairs={{0,4},{2,6},{4,8},{5,1},{6,10},{7,3},{8,12},{9,5},{10,14},{11,7},{... | collective-permute-start | bytes 663560 | tf_op jit(solution)/shard_map/ppermute | solution.py:496
  35.9 10.3 %collective-permute-start.2 = (f32[576,128]{1,0:T(8,128)S(1)}, f32[576,128]{1,0:T(8,128)S(1)}, u32[]{:S(2)}, u32[]{:S(2)}) collective-permute-start(f32[576,128]{1,0:T(8,128)S(1)} %pad_maximum_fusion.1), channel_id=1, source_target_pairs={{0,2},{2,4},{3,1},{4,6},{5,3},{6,8},{7,5},{8,10},{9,7},{10,12},{11... | collective-permute-start | bytes 884744 | tf_op jit(solution)/shard_map/ppermute | solution.py:495
  42.6 7.9 %collective-permute-start.3 = (f32[432,128]{1,0:T(8,128)S(1)}, f32[432,128]{1,0:T(8,128)S(1)}, u32[]{:S(2)}, u32[]{:S(2)}) collective-permute-start(f32[432,128]{1,0:T(8,128)S(1)} %pad_maximum_fusion.3), channel_id=1, source_target_pairs={{0,4},{2,6},{4,8},{5,1},{6,10},{7,3},{8,12},{9,5},{10,14},{11,7},{... | collective-permute-start | bytes 663560 | tf_op jit(solution)/shard_map/ppermute | solution.py:496

commit v8 on v7

--- a/solution.py
+++ b/solution.py
@@ -13,7 +13,7 @@
 SECTION_B = (1432997174477.0 / 9575080441755.0, 5161836677717.0 / 13612068292357.0)
 UNIT = 144
 LANES = 128
-NEAR_ROWS = 640
+EARLY_ROWS = 1024
 ALL_ROWS = 1664
 VMEM_LIMIT = 24 * 1024 * 1024
 
@@ -249,22 +249,24 @@
         r_ref[48:96, at : at + 128] = jnp.where(first, pltpu.roll(even, 64, 1), odd)
 
 
-def near_kernel(core_ref, part_ref, spread_ref, swapped_ref, near_ref, out_ref, give_ref, r_ref):
-    swapped = pl.multiple_of((1 - core_ref[0]) * (5 * UNIT) + 4 * UNIT, 8)
-    write_units([(swapped_ref, swapped), (near_ref, UNIT), (near_ref, 0)], r_ref)
-    out_ref[...] = part_ref[...] + picked(r_ref[...], spread_ref[0:NEAR_ROWS, :])
-    give_ref[...] = near_ref[2 * UNIT : 4 * UNIT, :]
-
-
-def join_kernel(give_ref, far_ref, out_ref):
-    out_ref[0 : 2 * UNIT, :] = give_ref[...]
-    out_ref[2 * UNIT : 3 * UNIT, :] = far_ref[2 * UNIT : 3 * UNIT, :]
-
-
-def write_far(core, far_ref, shared_ref, r_ref):
-    shared = [pl.multiple_of((1 - core) * (3 * UNIT) + UNIT * place, 8) for place in range(3)]
-    sources = [(shared_ref, shared[place]) for place in (2, 0, 1)]
-    write_units(sources + [(far_ref, UNIT), (far_ref, 0)], r_ref)
+def early_kernel(
+    core_ref, part_ref, spread_ref, swapped_ref, near_ref, shared_ref, out_ref, r_ref
+):
+    other = 1 - core_ref[0]
+    swapped = pl.multiple_of(other * (5 * UNIT) + 4 * UNIT, 8)
+    shared = [pl.multiple_of(other * (2 * UNIT) + UNIT * place, 8) for place in range(2)]
+    sources = [(shared_ref, shared[0]), (shared_ref, shared[1]), (swapped_ref, swapped)]
+    write_units(sources + [(near_ref, UNIT), (near_ref, 0)], r_ref)
+    out_ref[...] = part_ref[...] + picked(r_ref[...], spread_ref[0:EARLY_ROWS, :])
+
+
+def give_kernel(part_ref, far_ref, out_ref):
+    out_ref[...] = far_ref[2 * UNIT : 3 * UNIT, :]
+
+
+def write_late(core, far_ref, shared_ref, r_ref):
+    shared = pl.multiple_of((1 - core) * UNIT, 8)
+    write_units([(shared_ref, shared), (far_ref, UNIT), (far_ref, 0)], r_ref)
 
 
 def received_column(core, source):
@@ -274,10 +276,10 @@
         list_at = list_at + jnp.where(remote >= 192 * k, 1, 0)
     slot = remote - 192 * list_at
     seen = list_at + core * (7 - 2 * list_at)
-    near = (seen >= 3) & (seen < 6)
-    place = jnp.where(seen < 3, seen, seen - 3)
-    main = jnp.where(near, 0, NEAR_ROWS) + 128 * place + slot
-    rest = jnp.where(near, 384, NEAR_ROWS + 640) + 64 * place + slot - 128
+    early = (seen >= 1) & (seen < 6)
+    place = jnp.where(early, seen - 1, jnp.maximum(seen - 5, 0))
+    main = jnp.where(early, 0, EARLY_ROWS) + 128 * place + slot
+    rest = jnp.where(early, 640, EARLY_ROWS + 384) + 64 * place + slot - 128
     return jnp.where(remote < 0, -1, jnp.where(slot < 128, main, rest))
 
 
@@ -428,8 +430,8 @@
         del refs[0:3]
     r_ref, g_ref, m_ref, rate_ref, t_ref = refs
     core = core_ref[0]
-    write_far(core, far_ref, shared_ref, r_ref)
-    gathered = part_ref[...] + picked(r_ref[...], spread_ref[NEAR_ROWS:ALL_ROWS, :])
+    write_late(core, far_ref, shared_ref, r_ref)
+    gathered = part_ref[...] + picked(r_ref[...], spread_ref[EARLY_ROWS:ALL_ROWS, :])
     exterior(gathered, codes_ref, place_ref, g_ref, m_ref)
     rate_ref[...] = rate_in_ref[...]
     add_lift(rate_ref, g_ref)
@@ -479,7 +481,7 @@
 LIST_OUTPUTS = [shaped(5 * UNIT), shaped(3 * UNIT)]
 
 
-def exchanged(core, swap, own, gather_near):
+def exchanged(core, swap, own, gather_early):
     count = lax.axis_size("sfc")
     pairs = [[2 * chip, 2 * chip + 1] for chip in range(count // 2)]
 
@@ -494,10 +496,13 @@
     far = jnp.concatenate([own[2 * u : 3 * u], theirs[2 * u : 4 * u]])
     near = lax.ppermute(near, "sfc", ahead(1))
     far = lax.ppermute(far, "sfc", ahead(2))
-    part, give = gather_near(swapped, near)
-    (shared,) = called(join_kernel, None, [give, far], [shaped(3 * u)], [])
-    shared = lax.all_gather(shared, "sfc", axis_index_groups=pairs, tiled=True)
-    return part, far, shared
+
+    def shared(given):
+        return lax.all_gather(given, "sfc", axis_index_groups=pairs, tiled=True)
+
+    part = gather_early(swapped, near, shared(near[2 * u : 4 * u]))
+    (given,) = called(give_kernel, None, [part, far], [shaped(u)], [])
+    return part, far, shared(given)
 
 
 def local(
@@ -573,16 +578,16 @@
                 [table],
             )
 
-        def gather_near(swapped, near, part=part):
-            operands = [part, made[0], swapped, near]
-            outputs = [shaped(96, 1024), shaped(2 * UNIT)]
-            return called(near_kernel, core_at, operands, outputs, [(96, NEAR_ROWS)])
-
-        part, far, shared = exchanged(core, swap, own, gather_near)
+        def gather_early(swapped, near, shared, part=part):
+            operands = [part, made[0], swapped, near, shared]
+            outputs = [shaped(96, 1024)]
+            return called(early_kernel, core_at, operands, outputs, [(96, EARLY_ROWS)])[0]
+
+        part, far, shared = exchanged(core, swap, own, gather_early)
         operands = [solution] + ([register] if section else [])
         operands += [rate, part, far, shared, *made]
         outputs = [shaped(384), shaped(384)]
-        scratch = [(96, ALL_ROWS - NEAR_ROWS), (192, LANES), (64, LANES), (384, LANES), table]
+        scratch = [(96, ALL_ROWS - EARLY_ROWS), (192, LANES), (64, LANES), (384, LANES), table]
         if section:
             scratch = [(384, LANES), (384, LANES), pltpu.SemaphoreType.DMA((4,)), *scratch]
         if section == 0:

time: 57.2 us -> 56.5 us (0.988)
  waiting for transfers between devices: 5.86 us -> 0.98 us
  blocking collectives: 14 us -> 18.1 us
    ppermute x2, waiting for transfers between devices: 4.86 us -> 0.01 us  [exchanged(): far = lax.ppermute(far, 'sfc', ahead(2))]
    all_gather x2 -> x4, blocking collectives: 9.03 us -> 13.2 us  [shared(): return lax.all_gather(given, 'sfc', axis_index_groups=pairs, tiled=True)]
  transfers between devices with their start and end apart: 4 -> 4, of which waited for: 3 -> 1; matrix products, arithmetic and copies ran while one was open for 0% -> 0% of each run, Pallas kernels for 8% -> 9%
where the time goes in v8:
time: 56.5 us; the launch traced here: 56.2 us
  starting transfers between devices  25.5 us (45%)
  blocking collectives  18.1 us (32%)
  Pallas kernels  10.4 us (18%)
  between operations  1 us (2%)
  waiting for transfers between devices  0.98 us (2%)
    ppermute x2, starting transfers between devices, exchanged(): near = lax.ppermute(near, 'sfc', ahead(1))  20.5 us
    all_gather x4, blocking collectives, shared(): return lax.all_gather(given, 'sfc', axis_index_groups=pairs, tiled=True)  13.2 us
    pallas_call x9, Pallas kernels, called(): pl.pallas_call(kernel, in_specs=first + [pl.BlockSpec(memory_space=space)...  10.4 us
    ppermute x2, starting transfers between devices, exchanged(): far = lax.ppermute(far, 'sfc', ahead(2))  5 us
    all_gather x2, blocking collectives, exchanged(): swapped = lax.all_gather(swap, 'sfc', axis_index_groups=pairs, tiled=True)  4.97 us
  transfers between devices with their start and end apart: 4, of which 1 were waited for; matrix products, arithmetic and copies ran while one was open for 0% of the time, Pallas kernels for 9%

profile of v8, /device:TPU:7, one launch (start us, length us, event | category | flops | bytes accessed | tf_op | source)
XLA Modules:
  0.0 56.2 jit_solution(9151761747738595520)
XLA Ops:
  0.6 0.0 copy-start
  0.6 0.0 copy-start.1
  0.7 0.0 copy-start.2
  0.7 0.0 copy-start.8
  0.7 0.0 copy-start.9
  0.7 0.0 copy-start.7
  0.7 0.0 copy-start.3
  0.7 0.0 copy-start.5
  0.7 0.0 copy-start.4
  0.7 0.0 copy-start.6
  0.7 2.1 %shard_map.114 = (f32[720,128]{1,0:T(8,128)S(1)}, f32[432,128]{1,0:T(8,128)S(1)}) custom-call(s32[1]{0:T(128)} %bitcast.core_ref.refs_0_, f32[384,128]{1,0:T(8,128)} %bitcast.6, s32[8,192]{1,0:T(8,128)} %send_hbm.1), custom_call_target="tpu_custom_call" | custom-call | tf_op jit(solution)/shard_map/pallas_call | solution.py:468
  2.9 2.6 %all_gather.18.swapped_ref = f32[1440,128]{1,0:T(8,128)S(1)} all-gather(f32[720,128]{1,0:T(8,128)S(1)} %get-tuple-element.22), channel_id=1, replica_groups={{0,1},{2,3},{4,5},{6,7},{8,9},{10,11},{12,13},{14,15},{16,17},{18,19},{..., dimensions={0}, use_global_device_ids=true | all-gather | bytes 1105920 | tf_op jit(solution)/shard_map/all_gather | solution.py:492
  5.6 13.8 %collective-permute-start = (f32[576,128]{1,0:T(8,128)S(1)}, f32[576,128]{1,0:T(8,128)S(1)}, u32[]{:S(2)}, u32[]{:S(2)}) collective-permute-start(f32[576,128]{1,0:T(8,128)S(1)} %pad_maximum_fusion), channel_id=1, source_target_pairs={{0,2},{2,4},{3,1},{4,6},{5,3},{6,8},{7,5},{8,10},{9,7},{10,12},{11... | collective-permute-start | bytes 884744 | tf_op jit(solution)/shard_map/ppermute | solution.py:497
  19.5 3.1 %collective-permute-start.1 = (f32[432,128]{1,0:T(8,128)S(1)}, f32[432,128]{1,0:T(8,128)S(1)}, u32[]{:S(2)}, u32[]{:S(2)}) collective-permute-start(f32[432,128]{1,0:T(8,128)S(1)} %pad_maximum_fusion.2), channel_id=1, source_target_pairs={{0,4},{2,6},{4,8},{5,1},{6,10},{7,3},{8,12},{9,5},{10,14},{11,7},{... | collective-permute-start | bytes 663560 | tf_op jit(solution)/shard_map/ppermute | solution.py:498
  22.6 0.0 copy-done
  22.6 0.0 copy-done.1
  22.6 0.0 copy-done.2
  22.6 0.0 copy-done.8
  22.6 0.0 copy-done.9
  22.6 0.0 copy-done.7
  22.6 0.0 copy-done.3
  22.7 0.0 copy-done.5
  22.7 0.0 copy-done.4
  22.7 0.0 copy-done.6
  22.7 3.1 %shard_map.113 = (f32[384,128]{1,0:T(8,128)S(1)}, f32[96,1024]{1,0:T(8,128)S(1)}, bf16[768,1536]{1,0:T(8,128)(2,1)S(1)}, bf16[1664,1024]{1,0:T(8,128)(2,1)S(1)},...) custom-call(s32[1]{0:T(128)} %bitcast.core_ref.refs_0_, f32[384,128]{1,0:T(8,128)S(1)} %bitcast.7, ...), custom_call_target="tpu_custom_call" | custom-call | tf_op jit(solution)/shard_map/pallas_call | solution.py:468
  25.8 0.0 collective-permute-done.near_ref
  25.9 2.0 %all_gather.19.shared_ref = f32[576,128]{1,0:T(8,128)S(1)} all-gather(f32[288,128]{1,0:T(8,128)S(1)} %slice.56), channel_id=1, replica_groups={{0,1},{2,3},{4,5},{6,7},{8,9},{10,11},{12,13},{14,15},{16,17},{18,19},{..., dimensions={0}, use_global_device_ids=true | all-gather | bytes 442368 | tf_op jit(solution)/shard_map/all_gather | solution.py:501
  27.9 0.6 %shard_map.115.part_ref.refs_3_ = f32[96,1024]{1,0:T(8,128)S(1)} custom-call(s32[1]{0:T(128)} %bitcast.core_ref.refs_0_, f32[96,1024]{1,0:T(8,128)S(1)} %get-tuple-element.20.part_ref, bf16[1664,1024]{1,0:T(8,128)(2,1)S(1)} %get-tuple-element.21.spread_ref.refs_6_.refs_7_, f32[1440,128]{1,0:T(8,128)S(1)} %all_gather.18.swapped_ref, ...), custom_call_target="tpu_custom_call" | custom-call | tf_op jit(solution)/shard_map/pallas_call | solution.py:468
  28.5 0.0 collective-permute-done.1.far_ref.refs_4_
  28.5 3.0 %all_gather.20.refs_5_ = f32[288,128]{1,0:T(8,128)S(1)} all-gather(f32[144,128]{1,0:T(8,128)S(1)} %shard_map.116), channel_id=1, replica_groups={{0,1},{2,3},{4,5},{6,7},{8,9},{10,11},{12,13},{14,15},{16,17},{18,19},{..., dimensions={0}, use_global_device_ids=true | all-gather | bytes 221184 | tf_op jit(solution)/shard_map/all_gather | solution.py:501
  31.6 1.5 %shard_map.117 = (f32[384,128]{1,0:T(8,128)S(1)}, f32[384,128]{1,0:T(8,128)S(1)}, f32[720,128]{1,0:T(8,128)S(1)}, f32[432,128]{1,0:T(8,128)S(1)}) custom-call(s32[1]{0:T(128)} %bitcast.core_ref.refs_0_, f32[384,128]{1,0:T(8,128)S(1)} %bitcast.8, f32[384,128]{1,0:T(8,128)S(1)} %get-tuple-element.19.refs_2_, f32[96,1024]{1,0:T(8,128)S(1)} %shard_map.115.part_ref.refs_3_, ...), custom_call_target="tpu_custom_call" | custom-call | tf_op jit(solution)/shard_map/pallas_call | solution.py:468
  33.1 2.3 %all_gather.21.swapped_ref = f32[1440,128]{1,0:T(8,128)S(1)} all-gather(f32[720,128]{1,0:T(8,128)S(1)} %get-tuple-element.32), channel_id=1, replica_groups={{0,1},{2,3},{4,5},{6,7},{8,9},{10,11},{12,13},{14,15},{16,17},{18,19},{..., dimensions={0}, use_global_device_ids=true | all-gather | bytes 1105920 | tf_op jit(solution)/shard_map/all_gather | solution.py:492
  35.5 6.6 %collective-permute-start.2 = (f32[576,128]{1,0:T(8,128)S(1)}, f32[576,128]{1,0:T(8,128)S(1)}, u32[]{:S(2)}, u32[]{:S(2)}) collective-permute-start(f32[576,128]{1,0:T(8,128)S(1)} %pad_maximum_fusion.1), channel_id=1, source_target_pairs={{0,2},{2,4},{3,1},{4,6},{5,3},{6,8},{7,5},{8,10},{9,7},{10,12},{11... | collective-permute-start | bytes 884744 | tf_op jit(solution)/shard_map/ppermute | solution.py:497
  42.2 1.9 %collective-permute-start.3 = (f32[432,128]{1,0:T(8,128)S(1)}, f32[432,128]{1,0:T(8,128)S(1)}, u32[]{:S(2)}, u32[]{:S(2)}) collective-permute-start(f32[432,128]{1,0:T(8,128)S(1)} %pad_maximum_fusion.3), channel_id=1, source_target_pairs={{0,4},{2,6},{4,8},{5,1},{6,10},{7,3},{8,12},{9,5},{10,14},{11,7},{... | collective-permute-start | bytes 663560 | tf_op jit(solution)/shard_map/ppermute | solution.py:498
  44.2 0.7 %shard_map.118 = (f32[384,128]{1,0:T(8,128)S(1)}, f32[96,1024]{1,0:T(8,128)S(1)}) custom-call(f32[384,128]{1,0:T(8,128)S(1)} %get-tuple-element.28.u_ref.refs_1_, bf16[384,1152]{1,0:T(8,128)(2,1)S(1)} %copy-done, s32[6,128]{1,0:T(8,128)S(1)} %copy-done.3, s32[4,64]{1,0:T(4,128)S(1)} %copy-done.4), custom_call_target="tpu_custom_call" | custom-call | tf_op jit(solution)/shard_map/pallas_call | solution.py:468
  44.9 1.0 %collective-permute-done.2.near_ref = f32[576,128]{1,0:T(8,128)S(1)} collective-permute-done((f32[576,128]{1,0:T(8,128)S(1)}, f32[576,128]{1,0:T(8,128)S(1)}, u32[]{:S(2)}, u32[]{:S(2)}) %collective-permute-start.2) | collective-permute-done | bytes 294944 | tf_op jit(solution)/shard_map/ppermute | solution.py:497
  45.8 4.5 %all_gather.22.shared_ref = f32[576,128]{1,0:T(8,128)S(1)} all-gather(f32[288,128]{1,0:T(8,128)S(1)} %slice.57), channel_id=1, replica_groups={{0,1},{2,3},{4,5},{6,7},{8,9},{10,11},{12,13},{14,15},{16,17},{18,19},{..., dimensions={0}, use_global_device_ids=true | all-gather | bytes 442368 | tf_op jit(solution)/shard_map/all_gather | solution.py:501
  50.4 0.6 %shard_map.119.part_ref.refs_4_ = f32[96,1024]{1,0:T(8,128)S(1)} custom-call(s32[1]{0:T(128)} %bitcast.core_ref.refs_0_, f32[96,1024]{1,0:T(8,128)S(1)} %get-tuple-element.31.part_ref, bf16[1664,1024]{1,0:T(8,128)(2,1)S(1)} %get-tuple-element.21.spread_ref.refs_6_.refs_7_, f32[1440,128]{1,0:T(8,128)S(1)} %all_gather.21.swapped_ref, ...), custom_call_target="tpu_custom_call" | custom-call | tf_op jit(solution)/shard_map/pallas_call | solution.py:468
  51.0 0.0 collective-permute-done.3.far_ref.refs_5_
  51.0 3.5 %all_gather.23.refs_6_ = f32[288,128]{1,0:T(8,128)S(1)} all-gather(f32[144,128]{1,0:T(8,128)S(1)} %shard_map.120), channel_id=1, replica_groups={{0,1},{2,3},{4,5},{6,7},{8,9},{10,11},{12,13},{14,15},{16,17},{18,19},{..., dimensions={0}, use_global_device_ids=true | all-gather | bytes 221184 | tf_op jit(solution)/shard_map/all_gather | solution.py:501
  54.6 1.6 %shard_map.121 = (f32[384,128]{1,0:T(8,128)}, f32[384,128]{1,0:T(8,128)}) custom-call(s32[1]{0:T(128)} %bitcast.core_ref.refs_0_, f32[384,128]{1,0:T(8,128)S(1)} %get-tuple-element.28.u_ref.refs_1_, f32[384,128]{1,0:T(8,128)S(1)} %get-tuple-element.29.refs_2_, f32[384,128]{1,0:T(8,128)S(1)} %get-tuple-element.30.refs_3_, ...), custom_call_target="tpu_custom_call" | custom-call | tf_op jit(solution)/shard_map/pallas_call | solution.py:468
  (14 shorter events, 0.2 us)
Async XLA Ops:
  0.6 21.9 %copy-start = (bf16[384,1152]{1,0:T(8,128)(2,1)S(1)}, bf16[384,1152]{1,0:T(8,128)(2,1)}, u32[]{:S(2)}) copy-start(bf16[384,1152]{1,0:T(8,128)(2,1)} %constant.17.clone.volume_ref) | copy-start | bytes 2654212
  0.6 21.9 %copy-start.1 = (f32[6,64,128]{2,1,0:T(8,128)S(1)}, f32[6,64,128]{2,1,0:T(8,128)}, u32[]{:S(2)}) copy-start(f32[6,64,128]{2,1,0:T(8,128)} %param.10) | copy-start | bytes 589828
  0.7 21.9 %copy-start.2 = (s32[8,192]{1,0:T(8,128)S(1)}, s32[8,192]{1,0:T(8,128)}, u32[]{:S(2)}) copy-start(s32[8,192]{1,0:T(8,128)} %send_hbm.1) | copy-start | bytes 18436
  0.7 21.9 %copy-start.8 = (s32[64]{0:T(128)S(1)}, s32[64]{0:T(128)}, u32[]{:S(2)}) copy-start(s32[64]{0:T(128)} %param.18) | copy-start | bytes 772
  0.7 21.9 %copy-start.9 = (s32[128]{0:T(128)S(1)}, s32[128]{0:T(128)}, u32[]{:S(2)}) copy-start(s32[128]{0:T(128)} %param.12) | copy-start | bytes 1540
  0.7 21.9 %copy-start.7 = (f32[2,128]{1,0:T(2,128)S(1)}, f32[2,128]{1,0:T(2,128)}, u32[]{:S(2)}) copy-start(f32[2,128]{1,0:T(2,128)} %material_ref.1) | copy-start | bytes 3076
  0.7 21.9 %copy-start.3 = (s32[6,128]{1,0:T(8,128)S(1)}, s32[6,128]{1,0:T(8,128)}, u32[]{:S(2)}) copy-start(s32[6,128]{1,0:T(8,128)} %face_ref.3) | copy-start | bytes 9220
  0.7 21.9 %copy-start.5 = (s32[6,128]{1,0:T(8,128)S(1)}, s32[6,128]{1,0:T(8,128)}, u32[]{:S(2)}) copy-start(s32[6,128]{1,0:T(8,128)} %code_ref.1) | copy-start | bytes 9220
  0.7 21.9 %copy-start.4 = (s32[4,64]{1,0:T(4,128)S(1)}, s32[4,64]{1,0:T(4,128)}, u32[]{:S(2)}) copy-start(s32[4,64]{1,0:T(4,128)} %mortar_ref.3) | copy-start | bytes 3076
  0.7 21.9 %copy-start.6 = (s32[4,64]{1,0:T(4,128)S(1)}, s32[4,64]{1,0:T(4,128)}, u32[]{:S(2)}) copy-start(s32[4,64]{1,0:T(4,128)} %mortar_code_ref.1) | copy-start | bytes 3076
  5.6 20.2 %collective-permute-start = (f32[576,128]{1,0:T(8,128)S(1)}, f32[576,128]{1,0:T(8,128)S(1)}, u32[]{:S(2)}, u32[]{:S(2)}) collective-permute-start(f32[576,128]{1,0:T(8,128)S(1)} %pad_maximum_fusion), channel_id=1, source_target_pairs={{0,2},{2,4},{3,1},{4,6},{5,3},{6,8},{7,5},{8,10},{9,7},{10,12},{11... | collective-permute-start | bytes 884744 | tf_op jit(solution)/shard_map/ppermute | solution.py:497
  19.5 9.0 %collective-permute-start.1 = (f32[432,128]{1,0:T(8,128)S(1)}, f32[432,128]{1,0:T(8,128)S(1)}, u32[]{:S(2)}, u32[]{:S(2)}) collective-permute-start(f32[432,128]{1,0:T(8,128)S(1)} %pad_maximum_fusion.2), channel_id=1, source_target_pairs={{0,4},{2,6},{4,8},{5,1},{6,10},{7,3},{8,12},{9,5},{10,14},{11,7},{... | collective-permute-start | bytes 663560 | tf_op jit(solution)/shard_map/ppermute | solution.py:498
  35.5 10.3 %collective-permute-start.2 = (f32[576,128]{1,0:T(8,128)S(1)}, f32[576,128]{1,0:T(8,128)S(1)}, u32[]{:S(2)}, u32[]{:S(2)}) collective-permute-start(f32[576,128]{1,0:T(8,128)S(1)} %pad_maximum_fusion.1), channel_id=1, source_target_pairs={{0,2},{2,4},{3,1},{4,6},{5,3},{6,8},{7,5},{8,10},{9,7},{10,12},{11... | collective-permute-start | bytes 884744 | tf_op jit(solution)/shard_map/ppermute | solution.py:497
  42.2 8.8 %collective-permute-start.3 = (f32[432,128]{1,0:T(8,128)S(1)}, f32[432,128]{1,0:T(8,128)S(1)}, u32[]{:S(2)}, u32[]{:S(2)}) collective-permute-start(f32[432,128]{1,0:T(8,128)S(1)} %pad_maximum_fusion.3), channel_id=1, source_target_pairs={{0,4},{2,6},{4,8},{5,1},{6,10},{7,3},{8,12},{9,5},{10,14},{11,7},{... | collective-permute-start | bytes 663560 | tf_op jit(solution)/shard_map/ppermute | solution.py:498

commit v9 on v8

--- a/solution.py
+++ b/solution.py
@@ -201,10 +201,8 @@
     target_ref,
     material_ref,
     refinement_ref,
-    send_ref,
     rate_ref,
     part_ref,
-    list_spread_ref,
     spread_ref,
     place_ref,
     codes_ref,
@@ -213,7 +211,6 @@
 ):
     local_part(u_ref, volume_ref, face_ref, mortar_ref, rate_ref, part_ref, t_ref)
     core = core_ref[0]
-    list_spread_ref[...] = list_spread(core, send_ref)
     at = received_column(core, face_ref[...])
     columns = [at[face : face + 1, :] for face in range(6)]
     columns.append(received_column(core, mortar_row(mortar_ref)))
@@ -418,7 +415,7 @@
     rate_in_ref, part_ref, far_ref, shared_ref = refs[0:4]
     spread_ref, place_ref, codes_ref, scale_ref = refs[4:8]
     del refs[0:8]
-    list_spread_ref = None if section else refs.pop(0)
+    send_ref = None if section else refs.pop(0)
     outs = refs[0:2]
     del refs[0:2]
     if section == 0:
@@ -455,7 +452,7 @@
         copy.wait()
     if section == 0:
         write_table(new_u_ref, t_ref)
-        write_lists(t_ref, list_spread_ref[...], swap_ref, own_ref)
+        write_lists(t_ref, list_spread(core, send_ref), swap_ref, own_ref)
 
 
 def shaped(rows, columns=LANES, dtype=jnp.float32):
@@ -543,7 +540,7 @@
     register = None
     for section in range(2):
         if section == 0:
-            rate, part, list_spread_made, *made = called(
+            rate, part, *made = called(
                 first_kernel,
                 core_at,
                 [
@@ -556,12 +553,10 @@
                     target,
                     material,
                     refinement,
-                    send_face,
                 ],
                 [
                     shaped(384),
                     shaped(96, 1024),
-                    shaped(768, 1536, jnp.bfloat16),
                     shaped(ALL_ROWS, 1024, jnp.bfloat16),
                     shaped(768, 256, jnp.bfloat16),
                     shaped(16, LANES, jnp.int32),
@@ -591,7 +586,7 @@
         if section:
             scratch = [(384, LANES), (384, LANES), pltpu.SemaphoreType.DMA((4,)), *scratch]
         if section == 0:
-            operands.append(list_spread_made)
+            operands.append(send_face)
             outputs = outputs + LIST_OUTPUTS
 
         def kernel(*refs, section=section):

time: 56.5 us -> 56.5 us (level)
  blocking collectives: 18.1 us -> 19 us
  Pallas kernels: 10.4 us -> 9.55 us
    all_gather x4, blocking collectives: 13.2 us -> 14.1 us  [shared(): return lax.all_gather(given, 'sfc', axis_index_groups=pairs, tiled=True)]
    pallas_call x9, Pallas kernels: 10.4 us -> 9.55 us  [called(): pl.pallas_call(kernel, in_specs=first + [pl.BlockSpec(memory_space=space)...]
  transfers between devices with their start and end apart: 4 -> 4, of which waited for: 1 -> 1; matrix products, arithmetic and copies ran while one was open for 0% -> 0% of each run, Pallas kernels for 9% -> 7%
where the time goes in v9:
time: 56.5 us; the launch traced here: 56.3 us
  starting transfers between devices  25.5 us (45%)
  blocking collectives  19 us (34%)
  Pallas kernels  9.55 us (17%)
  between operations  0.99 us (2%)
  waiting for transfers between devices  0.98 us (2%)
    ppermute x2, starting transfers between devices, exchanged(): near = lax.ppermute(near, 'sfc', ahead(1))  20.5 us
    all_gather x4, blocking collectives, shared(): return lax.all_gather(given, 'sfc', axis_index_groups=pairs, tiled=True)  14.1 us
    pallas_call x9, Pallas kernels, called(): pl.pallas_call(kernel, in_specs=first + [pl.BlockSpec(memory_space=space)...  9.55 us
    ppermute x2, starting transfers between devices, exchanged(): far = lax.ppermute(far, 'sfc', ahead(2))  5 us
    all_gather x2, blocking collectives, exchanged(): swapped = lax.all_gather(swap, 'sfc', axis_index_groups=pairs, tiled=True)  4.97 us
  transfers between devices with their start and end apart: 4, of which 1 were waited for; matrix products, arithmetic and copies ran while one was open for 0% of the time, Pallas kernels for 7%

profile of v9, /device:TPU:7, one launch (start us, length us, event | category | flops | bytes accessed | tf_op | source)
XLA Modules:
  0.0 56.3 jit_solution(3300963571968092326)
XLA Ops:
  0.6 0.0 copy-start
  0.6 0.0 copy-start.1
  0.7 0.0 copy-start.3
  0.7 0.0 copy-start.4
  0.7 0.0 copy-start.5
  0.7 0.0 copy-start.6
  0.7 0.0 copy-start.8
  0.7 0.0 copy-start.7
  0.7 0.0 copy-start.9
  0.7 2.1 %shard_map.114 = (f32[720,128]{1,0:T(8,128)S(1)}, f32[432,128]{1,0:T(8,128)S(1)}) custom-call(s32[1]{0:T(128)} %bitcast.core_ref.refs_0_, f32[384,128]{1,0:T(8,128)} %bitcast.6, s32[8,192]{1,0:T(8,128)} %refs_10_.1), custom_call_target="tpu_custom_call" | custom-call | tf_op jit(solution)/shard_map/pallas_call | solution.py:465
  2.9 2.6 %all_gather.18.swapped_ref = f32[1440,128]{1,0:T(8,128)S(1)} all-gather(f32[720,128]{1,0:T(8,128)S(1)} %get-tuple-element.21), channel_id=1, replica_groups={{0,1},{2,3},{4,5},{6,7},{8,9},{10,11},{12,13},{14,15},{16,17},{18,19},{..., dimensions={0}, use_global_device_ids=true | all-gather | bytes 1105920 | tf_op jit(solution)/shard_map/all_gather | solution.py:489
  5.6 13.8 %collective-permute-start = (f32[576,128]{1,0:T(8,128)S(1)}, f32[576,128]{1,0:T(8,128)S(1)}, u32[]{:S(2)}, u32[]{:S(2)}) collective-permute-start(f32[576,128]{1,0:T(8,128)S(1)} %pad_maximum_fusion), channel_id=1, source_target_pairs={{0,2},{2,4},{3,1},{4,6},{5,3},{6,8},{7,5},{8,10},{9,7},{10,12},{11... | collective-permute-start | bytes 884744 | tf_op jit(solution)/shard_map/ppermute | solution.py:494
  19.5 3.1 %collective-permute-start.1 = (f32[432,128]{1,0:T(8,128)S(1)}, f32[432,128]{1,0:T(8,128)S(1)}, u32[]{:S(2)}, u32[]{:S(2)}) collective-permute-start(f32[432,128]{1,0:T(8,128)S(1)} %pad_maximum_fusion.2), channel_id=1, source_target_pairs={{0,4},{2,6},{4,8},{5,1},{6,10},{7,3},{8,12},{9,5},{10,14},{11,7},{... | collective-permute-start | bytes 663560 | tf_op jit(solution)/shard_map/ppermute | solution.py:495
  22.6 0.0 copy-done
  22.6 0.0 copy-done.1
  22.6 0.0 copy-done.3
  22.6 0.0 copy-done.4
  22.6 0.0 copy-done.5
  22.6 0.0 copy-done.6
  22.6 0.0 copy-done.8
  22.6 0.0 copy-done.7
  22.7 0.0 copy-done.9
  22.7 2.3 %shard_map.113 = (f32[384,128]{1,0:T(8,128)S(1)}, f32[96,1024]{1,0:T(8,128)S(1)}, bf16[1664,1024]{1,0:T(8,128)(2,1)S(1)}, bf16[768,256]{1,0:T(8,128)(2,1)S(1)}, ...) custom-call(s32[1]{0:T(128)} %bitcast.core_ref.refs_0_, f32[384,128]{1,0:T(8,128)S(1)} %bitcast.7, ...), custom_call_target="tpu_custom_call" | custom-call | tf_op jit(solution)/shard_map/pallas_call | solution.py:465
  24.9 0.0 collective-permute-done.near_ref
  25.0 0.0 copy-start.2
  25.0 2.0 %all_gather.19.shared_ref = f32[576,128]{1,0:T(8,128)S(1)} all-gather(f32[288,128]{1,0:T(8,128)S(1)} %slice.56), channel_id=1, replica_groups={{0,1},{2,3},{4,5},{6,7},{8,9},{10,11},{12,13},{14,15},{16,17},{18,19},{..., dimensions={0}, use_global_device_ids=true | all-gather | bytes 442368 | tf_op jit(solution)/shard_map/all_gather | solution.py:498
  27.0 0.6 %shard_map.115.part_ref.refs_3_ = f32[96,1024]{1,0:T(8,128)S(1)} custom-call(s32[1]{0:T(128)} %bitcast.core_ref.refs_0_, f32[96,1024]{1,0:T(8,128)S(1)} %get-tuple-element.19.part_ref, bf16[1664,1024]{1,0:T(8,128)(2,1)S(1)} %get-tuple-element.20.spread_ref.refs_6_.refs_7_, f32[1440,128]{1,0:T(8,128)S(1)} %all_gather.18.swapped_ref, ...), custom_call_target="tpu_custom_call" | custom-call | tf_op jit(solution)/shard_map/pallas_call | solution.py:465
  27.6 0.0 collective-permute-done.1.far_ref.refs_4_
  27.6 3.9 %all_gather.20.refs_5_ = f32[288,128]{1,0:T(8,128)S(1)} all-gather(f32[144,128]{1,0:T(8,128)S(1)} %shard_map.116), channel_id=1, replica_groups={{0,1},{2,3},{4,5},{6,7},{8,9},{10,11},{12,13},{14,15},{16,17},{18,19},{..., dimensions={0}, use_global_device_ids=true | all-gather | bytes 221184 | tf_op jit(solution)/shard_map/all_gather | solution.py:498
  31.6 0.0 copy-done.2
  31.6 1.6 %shard_map.117 = (f32[384,128]{1,0:T(8,128)S(1)}, f32[384,128]{1,0:T(8,128)S(1)}, f32[720,128]{1,0:T(8,128)S(1)}, f32[432,128]{1,0:T(8,128)S(1)}) custom-call(s32[1]{0:T(128)} %bitcast.core_ref.refs_0_, f32[384,128]{1,0:T(8,128)S(1)} %bitcast.8, f32[384,128]{1,0:T(8,128)S(1)} %get-tuple-element.18.refs_2_, f32[96,1024]{1,0:T(8,128)S(1)} %shard_map.115.part_ref.refs_3_, ...), custom_call_target="tpu_custom_call" | custom-call | tf_op jit(solution)/shard_map/pallas_call | solution.py:465
  33.2 2.3 %all_gather.21.swapped_ref = f32[1440,128]{1,0:T(8,128)S(1)} all-gather(f32[720,128]{1,0:T(8,128)S(1)} %get-tuple-element.30), channel_id=1, replica_groups={{0,1},{2,3},{4,5},{6,7},{8,9},{10,11},{12,13},{14,15},{16,17},{18,19},{..., dimensions={0}, use_global_device_ids=true | all-gather | bytes 1105920 | tf_op jit(solution)/shard_map/all_gather | solution.py:489
  35.6 6.6 %collective-permute-start.2 = (f32[576,128]{1,0:T(8,128)S(1)}, f32[576,128]{1,0:T(8,128)S(1)}, u32[]{:S(2)}, u32[]{:S(2)}) collective-permute-start(f32[576,128]{1,0:T(8,128)S(1)} %pad_maximum_fusion.1), channel_id=1, source_target_pairs={{0,2},{2,4},{3,1},{4,6},{5,3},{6,8},{7,5},{8,10},{9,7},{10,12},{11... | collective-permute-start | bytes 884744 | tf_op jit(solution)/shard_map/ppermute | solution.py:494
  42.3 1.9 %collective-permute-start.3 = (f32[432,128]{1,0:T(8,128)S(1)}, f32[432,128]{1,0:T(8,128)S(1)}, u32[]{:S(2)}, u32[]{:S(2)}) collective-permute-start(f32[432,128]{1,0:T(8,128)S(1)} %pad_maximum_fusion.3), channel_id=1, source_target_pairs={{0,4},{2,6},{4,8},{5,1},{6,10},{7,3},{8,12},{9,5},{10,14},{11,7},{... | collective-permute-start | bytes 663560 | tf_op jit(solution)/shard_map/ppermute | solution.py:495
  44.2 0.7 %shard_map.118 = (f32[384,128]{1,0:T(8,128)S(1)}, f32[96,1024]{1,0:T(8,128)S(1)}) custom-call(f32[384,128]{1,0:T(8,128)S(1)} %get-tuple-element.26.u_ref.refs_1_, bf16[384,1152]{1,0:T(8,128)(2,1)S(1)} %copy-done, s32[6,128]{1,0:T(8,128)S(1)} %copy-done.3, s32[4,64]{1,0:T(4,128)S(1)} %copy-done.4), custom_call_target="tpu_custom_call" | custom-call | tf_op jit(solution)/shard_map/pallas_call | solution.py:465
  44.9 1.0 %collective-permute-done.2.near_ref = f32[576,128]{1,0:T(8,128)S(1)} collective-permute-done((f32[576,128]{1,0:T(8,128)S(1)}, f32[576,128]{1,0:T(8,128)S(1)}, u32[]{:S(2)}, u32[]{:S(2)}) %collective-permute-start.2) | collective-permute-done | bytes 294944 | tf_op jit(solution)/shard_map/ppermute | solution.py:494
  45.9 4.5 %all_gather.22.shared_ref = f32[576,128]{1,0:T(8,128)S(1)} all-gather(f32[288,128]{1,0:T(8,128)S(1)} %slice.57), channel_id=1, replica_groups={{0,1},{2,3},{4,5},{6,7},{8,9},{10,11},{12,13},{14,15},{16,17},{18,19},{..., dimensions={0}, use_global_device_ids=true | all-gather | bytes 442368 | tf_op jit(solution)/shard_map/all_gather | solution.py:498
  50.4 0.6 %shard_map.119.part_ref.refs_4_ = f32[96,1024]{1,0:T(8,128)S(1)} custom-call(s32[1]{0:T(128)} %bitcast.core_ref.refs_0_, f32[96,1024]{1,0:T(8,128)S(1)} %get-tuple-element.29.part_ref, bf16[1664,1024]{1,0:T(8,128)(2,1)S(1)} %get-tuple-element.20.spread_ref.refs_6_.refs_7_, f32[1440,128]{1,0:T(8,128)S(1)} %all_gather.21.swapped_ref, ...), custom_call_target="tpu_custom_call" | custom-call | tf_op jit(solution)/shard_map/pallas_call | solution.py:465
  51.1 0.0 collective-permute-done.3.far_ref.refs_5_
  51.1 3.6 %all_gather.23.refs_6_ = f32[288,128]{1,0:T(8,128)S(1)} all-gather(f32[144,128]{1,0:T(8,128)S(1)} %shard_map.120), channel_id=1, replica_groups={{0,1},{2,3},{4,5},{6,7},{8,9},{10,11},{12,13},{14,15},{16,17},{18,19},{..., dimensions={0}, use_global_device_ids=true | all-gather | bytes 221184 | tf_op jit(solution)/shard_map/all_gather | solution.py:498
  54.6 1.6 %shard_map.121 = (f32[384,128]{1,0:T(8,128)}, f32[384,128]{1,0:T(8,128)}) custom-call(s32[1]{0:T(128)} %bitcast.core_ref.refs_0_, f32[384,128]{1,0:T(8,128)S(1)} %get-tuple-element.26.u_ref.refs_1_, f32[384,128]{1,0:T(8,128)S(1)} %get-tuple-element.27.refs_2_, f32[384,128]{1,0:T(8,128)S(1)} %get-tuple-element.28.refs_3_, ...), custom_call_target="tpu_custom_call" | custom-call | tf_op jit(solution)/shard_map/pallas_call | solution.py:465
  (14 shorter events, 0.2 us)
Async XLA Ops:
  0.6 21.9 %copy-start = (bf16[384,1152]{1,0:T(8,128)(2,1)S(1)}, bf16[384,1152]{1,0:T(8,128)(2,1)}, u32[]{:S(2)}) copy-start(bf16[384,1152]{1,0:T(8,128)(2,1)} %constant.17.clone.volume_ref) | copy-start | bytes 2654212
  0.6 21.9 %copy-start.1 = (f32[6,64,128]{2,1,0:T(8,128)S(1)}, f32[6,64,128]{2,1,0:T(8,128)}, u32[]{:S(2)}) copy-start(f32[6,64,128]{2,1,0:T(8,128)} %param.10) | copy-start | bytes 589828
  0.7 21.9 %copy-start.3 = (s32[6,128]{1,0:T(8,128)S(1)}, s32[6,128]{1,0:T(8,128)}, u32[]{:S(2)}) copy-start(s32[6,128]{1,0:T(8,128)} %face_ref.3) | copy-start | bytes 9220
  0.7 21.9 %copy-start.4 = (s32[4,64]{1,0:T(4,128)S(1)}, s32[4,64]{1,0:T(4,128)}, u32[]{:S(2)}) copy-start(s32[4,64]{1,0:T(4,128)} %mortar_ref.3) | copy-start | bytes 3076
  0.7 21.9 %copy-start.5 = (s32[6,128]{1,0:T(8,128)S(1)}, s32[6,128]{1,0:T(8,128)}, u32[]{:S(2)}) copy-start(s32[6,128]{1,0:T(8,128)} %code_ref.1) | copy-start | bytes 9220
  0.7 21.9 %copy-start.6 = (s32[4,64]{1,0:T(4,128)S(1)}, s32[4,64]{1,0:T(4,128)}, u32[]{:S(2)}) copy-start(s32[4,64]{1,0:T(4,128)} %mortar_code_ref.1) | copy-start | bytes 3076
  0.7 21.9 %copy-start.8 = (s32[64]{0:T(128)S(1)}, s32[64]{0:T(128)}, u32[]{:S(2)}) copy-start(s32[64]{0:T(128)} %param.18) | copy-start | bytes 772
  0.7 21.9 %copy-start.7 = (f32[2,128]{1,0:T(2,128)S(1)}, f32[2,128]{1,0:T(2,128)}, u32[]{:S(2)}) copy-start(f32[2,128]{1,0:T(2,128)} %material_ref.1) | copy-start | bytes 3076
  0.7 21.9 %copy-start.9 = (s32[128]{0:T(128)S(1)}, s32[128]{0:T(128)}, u32[]{:S(2)}) copy-start(s32[128]{0:T(128)} %param.12) | copy-start | bytes 1540
  5.6 19.3 %collective-permute-start = (f32[576,128]{1,0:T(8,128)S(1)}, f32[576,128]{1,0:T(8,128)S(1)}, u32[]{:S(2)}, u32[]{:S(2)}) collective-permute-start(f32[576,128]{1,0:T(8,128)S(1)} %pad_maximum_fusion), channel_id=1, source_target_pairs={{0,2},{2,4},{3,1},{4,6},{5,3},{6,8},{7,5},{8,10},{9,7},{10,12},{11... | collective-permute-start | bytes 884744 | tf_op jit(solution)/shard_map/ppermute | solution.py:494
  19.5 8.1 %collective-permute-start.1 = (f32[432,128]{1,0:T(8,128)S(1)}, f32[432,128]{1,0:T(8,128)S(1)}, u32[]{:S(2)}, u32[]{:S(2)}) collective-permute-start(f32[432,128]{1,0:T(8,128)S(1)} %pad_maximum_fusion.2), channel_id=1, source_target_pairs={{0,4},{2,6},{4,8},{5,1},{6,10},{7,3},{8,12},{9,5},{10,14},{11,7},{... | collective-permute-start | bytes 663560 | tf_op jit(solution)/shard_map/ppermute | solution.py:495
  25.0 6.6 %copy-start.2 = (s32[8,192]{1,0:T(8,128)S(1)}, s32[8,192]{1,0:T(8,128)}, u32[]{:S(2)}) copy-start(s32[8,192]{1,0:T(8,128)} %refs_10_.1) | copy-start | bytes 18436
  35.6 10.3 %collective-permute-start.2 = (f32[576,128]{1,0:T(8,128)S(1)}, f32[576,128]{1,0:T(8,128)S(1)}, u32[]{:S(2)}, u32[]{:S(2)}) collective-permute-start(f32[576,128]{1,0:T(8,128)S(1)} %pad_maximum_fusion.1), channel_id=1, source_target_pairs={{0,2},{2,4},{3,1},{4,6},{5,3},{6,8},{7,5},{8,10},{9,7},{10,12},{11... | collective-permute-start | bytes 884744 | tf_op jit(solution)/shard_map/ppermute | solution.py:494
  42.3 8.8 %collective-permute-start.3 = (f32[432,128]{1,0:T(8,128)S(1)}, f32[432,128]{1,0:T(8,128)S(1)}, u32[]{:S(2)}, u32[]{:S(2)}) collective-permute-start(f32[432,128]{1,0:T(8,128)S(1)} %pad_maximum_fusion.3), channel_id=1, source_target_pairs={{0,4},{2,6},{4,8},{5,1},{6,10},{7,3},{8,12},{9,5},{10,14},{11,7},{... | collective-permute-start | bytes 663560 | tf_op jit(solution)/shard_map/ppermute | solution.py:495
